TPU v7x, 256 devices: a whole 4x4x8 slice. The times are simulated.
256 devices in a mesh: chan: 8 (over y_lo, x), ctx: 32 (over z, y_hi, core).
Axes of the slice: x: 4, y: 4 (y_hi: 2, y_lo: 2; y = y_hi * 2 + y_lo), z: 8, core: 2. Of those that a mesh axis runs over, the one named last changes fastest.
Arguments:
- value: bfloat16 [16384, 4096], P('ctx', 'chan'), may hold values from -6 to 6
- gate_in: bfloat16 [16384, 4096], P('ctx', 'chan'), may hold values from -6 to 6
- gate_out: bfloat16 [16384, 4096], P('ctx', 'chan'), may hold values from -6 to 6
- filt: bfloat16 [16384, 4096], P('ctx', 'chan'), may hold values from -0.046875 to 0.046875
- skip: float32 [4096], P('chan'), may hold values from -1 to 1
- w_out: bfloat16 [4096, 4096], P('chan'), may hold values from -0.125 to 0.125
Outputs:
- layer_out: bfloat16 [16384, 4096], P('ctx', 'chan')
All inputs are finite; a program needn't handle non-finite values.
Results may differ from a plain program's by a relative error of at most 0.0058.
Values may be sent and summed in bfloat16 or wider, within the bound.
No kernel may reach another device: no remote copies, remote signals or barrier semaphores. Data moves between devices by JAX's collectives and lax.ppermute only.
A program may use at most 128 MiB of HBM per device.

v0:
```python
import math

import jax
import jax.numpy as jnp
from jax import lax
from jax.sharding import PartitionSpec as P

matmul_mode = lax.Precision.HIGH


def phase_pair(first, second, modulus):
    product = first[:, None] * second[None, :] % modulus
    angle = product.astype(jnp.float32) * (2.0 * math.pi / modulus)
    return (jnp.cos(angle), jnp.sin(angle))


def per_device(value, gate_in, gate_out, filt, skip, w_out):
    rows_dev, width = value.shape
    groups = lax.axis_size("ctx")
    slab = rows_dev // groups
    double = 2 * groups
    period = 2 * rows_dev * groups
    place = lax.axis_index("ctx")
    gated = (gate_in.astype(jnp.float32) * value.astype(jnp.float32)).astype(jnp.bfloat16)
    block_ids = jnp.arange(groups, dtype=jnp.int32)
    wave_ids = jnp.arange(double, dtype=jnp.int32)
    row_ids = jnp.arange(rows_dev, dtype=jnp.int32)
    cos_block, sin_block = phase_pair(wave_ids, block_ids, double)
    cos_row, sin_row = phase_pair(row_ids, row_ids, rows_dev)
    signals = jnp.stack([gated, filt]).reshape(2, groups, slab, width)
    spread = lax.all_to_all(signals, "ctx", split_axis=1, concat_axis=1, tiled=True).astype(
        jnp.float32
    )
    real_part = jnp.einsum("kj,sjbc->skbc", cos_block, spread, precision=matmul_mode)
    imag_part = -jnp.einsum("kj,sjbc->skbc", sin_block, spread, precision=matmul_mode)
    local_rows = place * slab + jnp.arange(slab, dtype=jnp.int32)
    cos_turn, sin_turn = phase_pair(wave_ids, local_rows, period)
    cos_turn = cos_turn[None, :, :, None]
    sin_turn = sin_turn[None, :, :, None]
    turned_real = real_part * cos_turn + imag_part * sin_turn
    turned_imag = imag_part * cos_turn - real_part * sin_turn
    packed = jnp.stack([turned_real, turned_imag])
    spectra = lax.all_to_all(packed, "ctx", split_axis=2, concat_axis=3, tiled=True)
    spec_real = jnp.einsum(
        "qr,serc->seqc", cos_row, spectra[0], precision=matmul_mode
    ) + jnp.einsum("qr,serc->seqc", sin_row, spectra[1], precision=matmul_mode)
    spec_imag = jnp.einsum(
        "qr,serc->seqc", cos_row, spectra[1], precision=matmul_mode
    ) - jnp.einsum("qr,serc->seqc", sin_row, spectra[0], precision=matmul_mode)
    prod_real = spec_real[0] * spec_real[1] - spec_imag[0] * spec_imag[1]
    prod_imag = spec_real[0] * spec_imag[1] + spec_imag[0] * spec_real[1]
    back_real = jnp.einsum("qr,eqc->erc", cos_row, prod_real, precision=matmul_mode) - jnp.einsum(
        "qr,eqc->erc", sin_row, prod_imag, precision=matmul_mode
    )
    back_imag = jnp.einsum("qr,eqc->erc", cos_row, prod_imag, precision=matmul_mode) + jnp.einsum(
        "qr,eqc->erc", sin_row, prod_real, precision=matmul_mode
    )
    own_waves = 2 * place + jnp.arange(2, dtype=jnp.int32)
    cos_back, sin_back = phase_pair(own_waves, row_ids, period)
    cos_back = cos_back[:, :, None]
    sin_back = sin_back[:, :, None]
    wound_real = back_real * cos_back - back_imag * sin_back
    wound_imag = back_imag * cos_back + back_real * sin_back
    packed_back = jnp.stack([wound_real, wound_imag]).reshape(2, 2, groups, slab, width)
    returned = lax.all_to_all(packed_back, "ctx", split_axis=2, concat_axis=1, tiled=True).reshape(
        2, double, slab, width
    )
    joined = (
        jnp.einsum("kj,kbc->jbc", cos_block, returned[0], precision=matmul_mode)
        - jnp.einsum("kj,kbc->jbc", sin_block, returned[1], precision=matmul_mode)
    ) / period
    conv = lax.all_to_all(joined, "ctx", split_axis=0, concat_axis=0, tiled=True).reshape(
        rows_dev, width
    )
    inner = conv + skip[None, :] * gated.astype(jnp.float32)
    mixed = (gate_out.astype(jnp.float32) * inner).astype(jnp.bfloat16)
    partial_out = jnp.dot(mixed, w_out, preferred_element_type=jnp.float32)
    summed = lax.psum_scatter(partial_out, "chan", scatter_dimension=1, tiled=True)
    return summed.astype(jnp.bfloat16)


def solution(mesh):
    placed = (
        P("ctx", "chan"),
        P("ctx", "chan"),
        P("ctx", "chan"),
        P("ctx", "chan"),
        P("chan"),
        P("chan", None),
    )
    return jax.shard_map(
        per_device, mesh=mesh, in_specs=placed, out_specs=P("ctx", "chan"), check_vma=False
    )
```

profile of v0, /device:TPU:16, one launch (start us, length us, event | category | flops | bytes accessed | tf_op | source)
XLA Modules:
  0.0 565.7 jit_solution(5518186590199367498)
XLA Ops:
  6.5 1.3 multiply_convert_fusion
  7.9 1.1 pad_maximum_fusion.2
  9.0 1.1 copy.58
  10.1 11.6 %all-to-all-start = ((bf16[2,32,16,512]{3,2,0,1:T(8,128)(2,1)}), bf16[2,32,16,512]{3,2,0,1:T(8,128)(2,1)S(1)}, u32[]{:S(2)}, u32[]{:S(2)}) async-start(bf16[2,32,16,512]{3,2,0,1:T(8,128)(2,1)} %copy.58), calls=%async_computation | async-start | bytes 2097152 | tf_op jit(solution)/shard_map/all_to_all | solution.py:31
  21.7 0.1 fusion.86
  21.8 28.8 %all-to-all-done = bf16[2,32,16,512]{3,2,0,1:T(8,128)(2,1)S(1)} async-done(((bf16[2,32,16,512]{3,2,0,1:T(8,128)(2,1)}), bf16[2,32,16,512]{3,2,0,1:T(8,128)(2,1)S(1)}, u32[]{:S(2)}, u32[]{:S(2)}) %all-to-all-start) | async-done | bytes 1048608 | tf_op jit(solution)/shard_map/all_to_all | solution.py:31
  50.6 1.9 fusion.46
  52.5 3.0 fusion.1
  55.5 1.8 pad_maximum_fusion
  57.3 8.1 %copy.61 = f32[2,2,64,16,512]{4,3,1,0,2:T(8,128)} copy(f32[2,2,64,16,512]{4,2,3,1,0:T(8,128)S(1)} %pad_maximum_fusion) | data formatting | bytes 16777216 | tf_op jit(solution)/shard_map/stack | solution.py:42
  65.4 5.0 all-to-all-start.1
  70.4 0.5 reduce-scatter.2.cloned.1.call-start
  71.0 0.2 fusion.88
  71.1 181.6 %all-to-all-done.1 = f32[2,2,64,16,512]{4,3,1,0,2:T(8,128)} async-done(((f32[2,2,64,16,512]{4,3,1,0,2:T(8,128)}), f32[2,2,64,16,512]{4,3,1,0,2:T(8,128)}, u32[]{:S(2)}, u32[]{:S(2)}) %all-to-all-start.1) | async-done | bytes 8388640 | tf_op jit(solution)/shard_map/all_to_all | solution.py:43
  252.7 4.4 copy.62
  257.1 1.9 fusion.137
  259.1 0.4 copy.63
  259.5 7.0 %fusion.41 = f32[2,2,512,512]{3,2,1,0:T(8,128)S(1)} fusion(f32[2,2,512,512]{3,2,1,0:T(8,128)S(1)} %bitcast.114), kind=kOutput, calls=%fused_computation.50 | convolution fusion | flops 3224895488 | bytes 8388608 | tf_op jit(solution)/shard_map/qr,serc->seqc/dot_general | solution.py:44
  266.5 0.4 copy.66
  267.0 7.2 %fusion.39 = f32[2,2,512,512]{3,2,1,0:T(8,128)S(1)} fusion(f32[2,2,512,512]{3,2,1,0:T(8,128)S(1)} %bitcast.116), kind=kOutput, calls=%fused_computation.48 | convolution fusion | flops 3224895488 | bytes 8388608 | tf_op jit(solution)/shard_map/qr,serc->seqc/dot_general | solution.py:47
  274.2 7.3 %add_bitcast_fusion = f32[2,2,512,512]{2,3,1,0:T(8,128)S(1)} fusion(f32[2,2,512,512]{3,2,1,0:T(8,128)S(1)} %fusion.41, f32[2,2,512,512]{3,2,1,0:T(8,128)S(1)} %bitcast.117), kind=kOutput, calls=%fused_computation.11 | convolution fusion | flops 3225944064 | bytes 12582912 | tf_op jit(solution)/shard_map/qr,serc->seqc/dot_general | solution.py:46
  281.5 7.1 %subtract_bitcast_fusion = f32[2,2,512,512]{2,3,1,0:T(8,128)S(1)} fusion(f32[2,2,512,512]{3,2,1,0:T(8,128)S(1)} %fusion.39, f32[2,2,512,512]{3,2,1,0:T(8,128)S(1)} %bitcast.115), kind=kOutput, calls=%fused_computation.10 | convolution fusion | flops 3225944064 | bytes 12582912 | tf_op jit(solution)/shard_map/qr,serc->seqc/dot_general | solution.py:49
  288.6 1.0 multiply_subtract_fusion.1
  289.7 6.0 %fusion.10 = f32[2,512,512]{1,2,0:T(8,128)S(1)} fusion(f32[1,2,512,512]{2,3,1,0:T(8,128)S(1)} %get-tuple-element.8), kind=kOutput, calls=%fused_computation.18 | convolution fusion | flops 1614282752 | bytes 4194304 | tf_op jit(solution)/shard_map/qr,eqc->erc/dot_general | solution.py:52
  295.7 5.5 fusion.8
  301.2 5.7 %fusion.16 = f32[2,512,512]{1,2,0:T(8,128)S(1)} fusion(f32[2,512,512]{1,2,0:T(8,128)S(1)} %fusion.10, f32[1,2,512,512]{2,3,1,0:T(8,128)S(1)} %get-tuple-element.7), kind=kOutput, calls=%fused_computation.28 | convolution fusion | flops 1614807040 | bytes 6291456 | tf_op jit(solution)/shard_map/qr,eqc->erc/dot_general | solution.py:52
  306.9 5.9 %multiply_subtract_fusion = (f32[2,512,512]{1,2,0:T(8,128)S(1)}, f32[2,512,512]{1,2,0:T(8,128)S(1)}) fusion(f32[2,512,512]{1,2,0:T(8,128)S(1)} %fusion.16, f32[2,512]{1,0:T(2,128)S(1)} %get-tuple-element.16, f32[2,512]{1,0:T(2,128)S(1)} %get-tuple-element.15, f32[2,512,512]{1,2,0:T(8,128)S(1)} %fusion.8, f32[1,2,512,512]{2,3,1,0:T(8,128)S(1)} %get-tuple-element.7), kind=kOutput, calls=%fused_computation.25 | convolution fusion | flops 1617952768 | bytes 10493952 | tf_op jit(solution)/shard_map/qr,eqc->erc/dot_general | solution.py:55
  312.9 0.8 pad_maximum_fusion.1
  313.7 0.8 copy.100
  314.5 105.9 %all_to_all.40 = f32[2,2,32,16,512]{4,3,1,0,2:T(8,128)S(1)} all-to-all(f32[2,2,32,16,512]{4,3,1,0,2:T(8,128)S(1)} %copy.100), channel_id=1, replica_groups=mesh['chan'=8,'ctx'=32] {'ctx'}, dimensions={2} | all-to-all | bytes 8388608 | tf_op jit(solution)/shard_map/all_to_all | solution.py:65
  420.5 0.8 fusion.138
  421.3 1.8 fusion.4
  423.2 0.0 copy-start.1
  423.2 0.0 copy-start.2
  423.2 1.8 fusion.25
  425.0 0.0 copy-start
  425.0 0.6 copy.81
  425.6 33.9 %all_to_all.41 = f32[32,16,512]{2,1,0:T(8,128)S(1)} all-to-all(f32[32,16,512]{2,1,0:T(8,128)S(1)} %copy.81), channel_id=1, replica_groups=mesh['chan'=8,'ctx'=32] {'ctx'}, dimensions={0} | all-to-all | bytes 2097152 | tf_op jit(solution)/shard_map/all_to_all | solution.py:72
  459.5 0.0 copy-done.1
  459.5 0.0 copy-done.2
  459.5 0.2 fusion.32
  459.8 0.0 copy-done
  459.8 5.6 fusion.143
  465.3 0.0 reduce-scatter.2.cloned.1.call-update
  465.4 91.2 %reduce-scatter.2.cloned.1.call-done = f32[512,512]{1,0:T(8,128)} async-done(((f32[512,4096]{1,0:T(8,128)}), f32[512,512]{1,0:T(8,128)}) %reduce-scatter.2.cloned.1.call-update) | async-done | bytes 1048592 | tf_op jit(solution)/shard_map/reduce_scatter | solution.py:78
  556.6 2.1 convert_element_type.78
  (2 shorter events, 0.0 us)
Async XLA Ops:
  10.1 40.5 %all-to-all-start = ((bf16[2,32,16,512]{3,2,0,1:T(8,128)(2,1)}), bf16[2,32,16,512]{3,2,0,1:T(8,128)(2,1)S(1)}, u32[]{:S(2)}, u32[]{:S(2)}) async-start(bf16[2,32,16,512]{3,2,0,1:T(8,128)(2,1)} %copy.58), calls=%async_computation | async-start | bytes 2097152 | tf_op jit(solution)/shard_map/all_to_all | solution.py:31
  65.4 187.3 %all-to-all-start.1 = ((f32[2,2,64,16,512]{4,3,1,0,2:T(8,128)}), f32[2,2,64,16,512]{4,3,1,0,2:T(8,128)}, u32[]{:S(2)}, u32[]{:S(2)}) async-start(f32[2,2,64,16,512]{4,3,1,0,2:T(8,128)} %copy.61), calls=%async_computation.1 | async-start | bytes 16777216 | tf_op jit(solution)/shard_map/all_to_all | solution.py:43
  70.4 486.1 %reduce-scatter.2.cloned.1.call-start = ((), (), s32[]{:S(2)}) async-start(), calls=%async_computation.5 | async-start | bytes 9437184 | tf_op jit(solution)/shard_map/reduce_scatter | solution.py:78
  423.2 36.4 %copy-start.1 = (bf16[512,512]{1,0:T(8,128)(2,1)S(1)}, bf16[512,512]{1,0:T(8,128)(2,1)}, u32[]{:S(2)}) copy-start(bf16[512,512]{1,0:T(8,128)(2,1)} %param.8) | copy-start | bytes 1572868
  423.2 36.3 %copy-start.2 = (f32[512]{0:T(512)S(1)}, f32[512]{0:T(512)}, u32[]{:S(2)}) copy-start(f32[512]{0:T(512)} %param.10) | copy-start | bytes 6148
  425.0 34.7 %copy-start = (bf16[512,4096]{1,0:T(8,128)(2,1)S(1)}, bf16[512,4096]{1,0:T(8,128)(2,1)}, u32[]{:S(2)}) copy-start(bf16[512,4096]{1,0:T(8,128)(2,1)} %param.11) | copy-start | bytes 12582916
Sparse Core Ops, SparseCore 0:
  465.5 91.0 reduce-scatter.1
where the time goes:
time: 576 us; the launch traced here: 566 us
  waiting for transfers between devices  302 us (52%)
  blocking collectives  140 us (24%)
  matrix products  65.9 us (11%)
  local copies, waits for them, and re-layouts  18.7 us (3%)
  starting transfers between devices  17.1 us (3%)
  between operations  13.9 us (2%)
  other arithmetic  8.73 us (2%)
    all_to_all x1, waiting for transfers between devices, per_device(): lax.all_to_all(packed, 'ctx', split_axis=2, concat_axis=3, tiled=True)  182 us
    all_to_all x1, blocking collectives, per_device(): lax.all_to_all(packed_back, 'ctx', split_axis=2, concat_axis=1, tiled=True)  106 us
    reduce_scatter x1, waiting for transfers between devices, per_device(): lax.psum_scatter(partial_out, 'chan', scatter_dimension=1, tiled=True)  91.2 us
    all_to_all x1, blocking collectives, per_device(): lax.all_to_all(joined, 'ctx', split_axis=0, concat_axis=0, tiled=True)  33.9 us
    all_to_all x1, waiting for transfers between devices, per_device(): lax.all_to_all(signals, 'ctx', split_axis=1, concat_axis=1, tiled=True)  28.8 us
    all_to_all x1, starting transfers between devices, per_device(): lax.all_to_all(signals, 'ctx', split_axis=1, concat_axis=1, tiled=True)  11.6 us
  transfers between devices with their start and end apart: 3, of which 3 were waited for; matrix products, arithmetic and copies ran while one was open for 0% of the time, Pallas kernels for 0%

commit v1 on v0

v1 whole, which is shorter than its diff:
```python
import functools

import jax
import jax.numpy as jnp
import numpy as np
from jax import lax
from jax.experimental import pallas as pl
from jax.experimental.pallas import tpu as pltpu
from jax.sharding import PartitionSpec as P

EDGE = 128
VMEM = 48 * 1024 * 1024


def split_table(table):
    high = table.astype(jnp.bfloat16)
    low = (table - high.astype(np.float64)).astype(jnp.bfloat16)
    return high, low


@functools.cache
def transform_tables():
    steps = np.arange(EDGE)
    slow = 2.0 * np.pi * np.outer(steps + 0.25, steps) / EDGE
    fast = 2.0 * np.pi * np.outer(steps, steps) / EDGE
    turn = 2.0 * np.pi * np.outer(steps + 0.25, steps) / (EDGE * EDGE)
    first = np.concatenate([np.cos(slow), -np.sin(slow)], 0)
    second = np.block([[np.cos(fast), -np.sin(fast)], [np.sin(fast), np.cos(fast)]])
    third = np.block([[np.cos(fast), np.sin(fast)], [-np.sin(fast), np.cos(fast)]]) / EDGE
    last = np.concatenate([np.cos(slow).T, -np.sin(slow).T], 1) / EDGE
    first_high, first_low = split_table(first)
    return (
        np.concatenate([first_high, first_low], 1),
        np.cos(turn).astype(np.float32),
        np.sin(turn).astype(np.float32),
        *split_table(second),
        *split_table(third),
        *split_table(last),
    )


def halves(array):
    high = array.astype(jnp.bfloat16)
    return high, (array - high.astype(jnp.float32)).astype(jnp.bfloat16)


def dot(a, b):
    return jnp.dot(a, b, preferred_element_type=jnp.float32)


def pack_kernel(value_ref, gate_ref, filt_ref, out_ref):
    gated = (gate_ref[...].astype(jnp.float32) * value_ref[...].astype(jnp.float32)).astype(
        jnp.bfloat16
    )
    chans = out_ref.shape[3]
    peers = EDGE // chans
    for which, array in enumerate((gated, filt_ref[...])):
        for part in range(array.shape[1] // EDGE):
            turned = array[:, part * EDGE : (part + 1) * EDGE].T
            out_ref[part * peers : (part + 1) * peers, 0, which] = turned.reshape(
                peers, chans, EDGE
            )


def conv_kernel(
    chans, in_ref, w1, cos_ref, sin_ref, w2h, w2l, w3h, w3l, w4h, w4l, out_ref, wide, back
):
    wide[...] = in_ref[...].astype(jnp.float32)
    cos, sin = cos_ref[...], sin_ref[...]

    @pl.loop(0, chans)
    def _(chan):
        both = jnp.concatenate(
            [
                wide[pl.ds(which * chans + chan, EDGE, stride=2 * chans), :].astype(jnp.bfloat16)
                for which in range(2)
            ],
            axis=1,
        )
        slow = dot(w1[...], jnp.concatenate([both, both], axis=0))
        rows = []
        for which in range(2):
            real = slow[:EDGE, which * EDGE : (which + 1) * EDGE]
            imag = slow[EDGE:, which * EDGE : (which + 1) * EDGE]
            rows.append(
                jnp.concatenate([real * cos + imag * sin, imag * cos - real * sin], axis=1)
            )
        high, low = halves(jnp.concatenate(rows, axis=0))
        spectra = dot(high, w2h[...]) + dot(low, w2h[...]) + dot(high, w2l[...])
        ar, ai = spectra[:EDGE, :EDGE], spectra[:EDGE, EDGE:]
        br, bi = spectra[EDGE:, :EDGE], spectra[EDGE:, EDGE:]
        high, low = halves(jnp.concatenate([ar * br - ai * bi, ar * bi + ai * br], axis=1))
        wound = dot(high, w3h[...]) + dot(low, w3h[...]) + dot(high, w3l[...])
        real, imag = wound[:, :EDGE], wound[:, EDGE:]
        high, low = halves(
            jnp.concatenate([real * cos - imag * sin, imag * cos + real * sin], axis=0)
        )
        conv = dot(w4h[...], high) + dot(w4h[...], low) + dot(w4l[...], high)
        back[pl.ds(chan, EDGE, stride=chans), :] = conv

    out_ref[...] = back[...].astype(jnp.bfloat16)


def mix_kernel(conv_ref, value_ref, gate_ref, gate_out_ref, skip_ref, out_ref):
    peers = EDGE // conv_ref.shape[2]
    for part in range(out_ref.shape[1] // EDGE):
        cols = slice(part * EDGE, (part + 1) * EDGE)
        conv = conv_ref[part * peers : (part + 1) * peers, 0].reshape(EDGE, EDGE).T
        gated = (
            gate_ref[:, cols].astype(jnp.float32) * value_ref[:, cols].astype(jnp.float32)
        ).astype(jnp.bfloat16)
        inner = conv.astype(jnp.float32) + skip_ref[:, cols] * gated.astype(jnp.float32)
        out_ref[:, cols] = (gate_out_ref[:, cols].astype(jnp.float32) * inner).astype(
            jnp.bfloat16
        )


def pack(value, gate_in, filt, groups):
    rows, width = value.shape
    chans = width // groups
    block = pl.BlockSpec((EDGE, width), lambda i: (i, 0))
    return pl.pallas_call(
        pack_kernel,
        grid=(rows // EDGE,),
        in_specs=[block] * 3,
        out_specs=pl.BlockSpec((groups, 1, 2, chans, EDGE), lambda i: (0, i, 0, 0, 0)),
        out_shape=jax.ShapeDtypeStruct((groups, rows // EDGE, 2, chans, EDGE), jnp.bfloat16),
        compiler_params=pltpu.CompilerParams(vmem_limit_bytes=VMEM),
        name="pack",
    )(value, gate_in, filt)


def convolve(spread):
    groups, slabs, _, chans, _ = spread.shape
    tables = transform_tables()
    rows = groups * slabs * chans
    whole = pl.BlockSpec(memory_space=pltpu.VMEM)
    conv = pl.pallas_call(
        functools.partial(conv_kernel, chans),
        in_specs=[whole] * (1 + len(tables)),
        out_specs=whole,
        out_shape=jax.ShapeDtypeStruct((rows, EDGE), jnp.bfloat16),
        scratch_shapes=[
            pltpu.VMEM((2 * rows, EDGE), jnp.float32),
            pltpu.VMEM((rows, EDGE), jnp.float32),
        ],
        compiler_params=pltpu.CompilerParams(vmem_limit_bytes=VMEM),
        name="convolve",
    )(spread.reshape(2 * rows, EDGE), *(jnp.asarray(table) for table in tables))
    return conv.reshape(groups, slabs, chans, EDGE)


def mix(conv, value, gate_in, gate_out, skip):
    rows, width = value.shape
    groups, _, chans, _ = conv.shape
    block = pl.BlockSpec((EDGE, width), lambda i: (i, 0))
    return pl.pallas_call(
        mix_kernel,
        grid=(rows // EDGE,),
        in_specs=[
            pl.BlockSpec((groups, 1, chans, EDGE), lambda i: (0, i, 0, 0)),
            block,
            block,
            block,
            pl.BlockSpec((1, width), lambda i: (0, 0)),
        ],
        out_specs=block,
        out_shape=jax.ShapeDtypeStruct((rows, width), jnp.bfloat16),
        compiler_params=pltpu.CompilerParams(vmem_limit_bytes=VMEM),
        name="mix",
    )(conv, value, gate_in, gate_out, skip[None])


def per_device(value, gate_in, gate_out, filt, skip, w_out):
    groups = lax.axis_size("ctx")
    packed = pack(value, gate_in, filt, groups)
    spread = lax.all_to_all(packed, "ctx", split_axis=0, concat_axis=0, tiled=True)
    conv = convolve(spread)
    returned = lax.all_to_all(conv, "ctx", split_axis=0, concat_axis=0, tiled=True)
    mixed = mix(returned, value, gate_in, gate_out, skip)
    partial_out = jnp.dot(mixed, w_out, preferred_element_type=jnp.float32)
    summed = lax.psum_scatter(partial_out, "chan", scatter_dimension=1, tiled=True)
    return summed.astype(jnp.bfloat16)


def solution(mesh):
    placed = (
        P("ctx", "chan"),
        P("ctx", "chan"),
        P("ctx", "chan"),
        P("ctx", "chan"),
        P("chan"),
        P("chan", None),
    )
    return jax.shard_map(
        per_device, mesh=mesh, in_specs=placed, out_specs=P("ctx", "chan"), check_vma=False
    )
```

time: 576 us -> 198 us (0.34); the launches traced: 566 us -> 196 us
  waiting for transfers between devices: 302 us -> 91.3 us
  blocking collectives: 140 us -> 63.1 us
  matrix products: 65.9 us -> 5.65 us
  Pallas kernels: 0 us -> 17.1 us
  starting transfers between devices: 17.1 us -> 0.01 us
  local copies, waits for them, and re-layouts: 18.7 us -> 3.2 us
  other arithmetic: 8.73 us -> 2.08 us
    all_to_all x2 -> x0, waiting for transfers between devices: 210 us -> none  [the longest x1 182 us: per_device(): lax.all_to_all(packed, 'ctx', split_axis=2, concat_axis=3, tiled=True)]
    all_to_all x2, blocking collectives: 140 us -> 63.1 us  [the longest x1 40.6 us: per_device(): lax.all_to_all(packed, 'ctx', split_axis=0, concat_axis=0, tiled=True)]
    dot_general x12 -> x0, matrix products: 60.3 us -> none  [the longest x1 7.34 us: per_device(): jnp.einsum('qr,serc->seqc', sin_row, spectra[1], precision=matmul_mode)]
    pallas_call x0 -> x3, Pallas kernels: none -> 17.1 us  [the longest x1 15.9 us: convolve(): pl.pallas_call(functools.partial(conv_kernel, chans), in_specs=[whole] *...]
    all_to_all x2 -> x0, starting transfers between devices: 16.6 us -> none  [the longest x1 11.6 us: per_device(): lax.all_to_all(signals, 'ctx', split_axis=1, concat_axis=1, tiled=True)]
    another operation x3 -> x0, local copies, waits for them, and re-layouts: 10 us -> none  [the longest x1 8.1 us: per_device(): packed = jnp.stack([turned_real, turned_imag])]
  transfers between devices with their start and end apart: 3 -> 1, of which waited for: 3 -> 1; matrix products, arithmetic and copies ran while one was open for 0% -> 0% of each run, Pallas kernels for 0% -> 0%
where the time goes in v1:
time: 198 us; the launch traced here: 196 us
  waiting for transfers between devices  91.3 us (46%)
  blocking collectives  63.1 us (32%)
  Pallas kernels  17.1 us (9%)
  between operations  13.6 us (7%)
  matrix products  5.65 us (3%)
  local copies, waits for them, and re-layouts  3.2 us (2%)
  other arithmetic  2.08 us (1%)
    reduce_scatter x1, waiting for transfers between devices, per_device(): lax.psum_scatter(partial_out, 'chan', scatter_dimension=1, tiled=True)  91.2 us
    all_to_all x1, blocking collectives, per_device(): lax.all_to_all(packed, 'ctx', split_axis=0, concat_axis=0, tiled=True)  40.6 us
    all_to_all x1, blocking collectives, per_device(): lax.all_to_all(conv, 'ctx', split_axis=0, concat_axis=0, tiled=True)  22.5 us
    pallas_call x1, Pallas kernels, convolve(): pl.pallas_call(functools.partial(conv_kernel, chans), in_specs=[whole] *...  15.9 us
    dot_general x1, matrix products, per_device(): partial_out = jnp.dot(mixed, w_out, preferred_element_type=jnp.float32)  5.65 us
  transfers between devices with their start and end apart: 1, of which 1 were waited for; matrix products, arithmetic and copies ran while one was open for 0% of the time, Pallas kernels for 0%

profile of v1, /device:TPU:16, one launch (start us, length us, event | category | flops | bytes accessed | tf_op | source)
XLA Modules:
  0.0 196.0 jit_solution(5293307943748873760)
XLA Ops:
  6.5 0.0 reduce-scatter.2.cloned.1.call-start
  6.5 0.0 copy-start
  6.5 1.0 copy-done
  7.6 0.0 copy-start.2
  7.6 1.0 copy-done.2
  8.6 0.0 copy-start.4
  8.6 1.0 copy-done.4
  9.7 0.0 copy-start.6
  9.7 0.0 copy-start.7
  9.7 0.0 copy-start.8
  9.7 0.0 copy-start.9
  9.7 0.0 copy-start.10
  9.7 0.0 copy-start.11
  9.7 0.0 copy-start.12
  9.7 0.0 copy-start.13
  9.7 0.0 copy-start.14
  9.7 0.0 copy-start.1
  9.7 0.0 copy-start.3
  9.8 0.0 copy-start.5
  9.8 0.0 copy-start.15
  9.8 0.6 pack.1
  10.4 0.0 copy-start.16
  10.4 40.6 %all_to_all.10 = bf16[32,4,2,16,128]{4,3,2,1,0:T(8,128)(2,1)S(1)} all-to-all(bf16[32,4,2,16,128]{4,3,2,1,0:T(8,128)(2,1)S(1)} %pack.1), channel_id=1, replica_groups=mesh['chan'=8,'ctx'=32] {'ctx'}, dimensions={0} | all-to-all | bytes 2097152 | tf_op jit(solution)/shard_map/all_to_all | solution.py:177
  51.0 0.0 copy-done.6
  51.0 0.0 copy-done.7
  51.0 0.0 copy-done.8
  51.0 0.0 copy-done.9
  51.0 0.0 copy-done.10
  51.0 0.0 copy-done.11
  51.1 0.0 copy-done.12
  51.1 0.0 copy-done.13
  51.1 0.0 copy-done.14
  51.1 15.9 %convolve.1 = bf16[2048,128]{1,0:T(8,128)(2,1)S(1)} custom-call(bf16[4096,128]{1,0:T(8,128)(2,1)S(1)} %bitcast.5, bf16[256,256]{1,0:T(8,128)(2,1)S(1)} %copy-done.10, f32[128,128]{1,0:T(8,128)S(1)} %copy-done.14, f32[128,128]{1,0:T(8,128)S(1)} %copy-done.13, bf16[256,256]{1,0:T(8,128)(2,1)S(1)} %copy-done.9, bf16[256,256]{1,0:T(8,128)(2,1)S(1)} %copy-done.8, ...), custom_call_target="tpu_custom_call" | custom-call | tf_op jit(solution)/shard_map/convolve/pallas_call | solution.py:138
  67.0 22.5 %all_to_all.11.conv_ref = bf16[32,4,16,128]{3,2,1,0:T(8,128)(2,1)S(1)} all-to-all(bf16[32,4,16,128]{3,2,1,0:T(8,128)(2,1)S(1)} %bitcast.6), channel_id=1, replica_groups=mesh['chan'=8,'ctx'=32] {'ctx'}, dimensions={0} | all-to-all | bytes 1048576 | tf_op jit(solution)/shard_map/all_to_all | solution.py:179
  89.5 0.0 copy-done.1
  89.5 0.0 copy-done.3
  89.5 0.0 copy-done.5
  89.5 0.0 copy-done.15
  89.5 0.6 mix.1
  90.1 0.0 copy-done.16
  90.1 5.7 %fusion = f32[512,4096]{1,0:T(8,128)} fusion(bf16[512,512]{1,0:T(8,128)(2,1)S(1)} %mix.1, bf16[512,4096]{1,0:T(8,128)(2,1)S(1)} %copy-done.16), kind=kOutput, calls=%fused_computation | convolution fusion | flops 2147483648 | bytes 13107200 | tf_op jit(solution)/shard_map/dot_general | solution.py:181
  95.8 0.0 reduce-scatter.2.cloned.1.call-update
  95.8 91.2 %reduce-scatter.2.cloned.1.call-done = f32[512,512]{1,0:T(8,128)} async-done(((f32[512,4096]{1,0:T(8,128)}), f32[512,512]{1,0:T(8,128)}) %reduce-scatter.2.cloned.1.call-update) | async-done | bytes 1048592 | tf_op jit(solution)/shard_map/reduce_scatter | solution.py:182
  187.0 2.1 %convert_element_type.3 = bf16[512,512]{1,0:T(8,128)(2,1)} convert(f32[512,512]{1,0:T(8,128)} %reduce-scatter.2.cloned.1.call-done) | non-fusion elementwise | flops 262144 | bytes 1572864 | tf_op jit(solution)/shard_map/convert_element_type | solution.py:183
Async XLA Ops:
  6.5 180.5 %reduce-scatter.2.cloned.1.call-start = ((), (), s32[]{:S(2)}) async-start(), calls=%async_computation.3 | async-start | bytes 9437184 | tf_op jit(solution)/shard_map/reduce_scatter | solution.py:182
  6.5 1.0 copy-start
  7.6 1.0 copy-start.2
  8.6 1.0 copy-start.4
  9.7 41.4 %copy-start.6 = (bf16[256,256]{1,0:T(8,128)(2,1)S(1)}, bf16[256,256]{1,0:T(8,128)(2,1)}, u32[]{:S(2)}) copy-start(bf16[256,256]{1,0:T(8,128)(2,1)} %constant.24.clone.w3l) | copy-start | bytes 393220
  9.7 41.4 %copy-start.7 = (bf16[256,256]{1,0:T(8,128)(2,1)S(1)}, bf16[256,256]{1,0:T(8,128)(2,1)}, u32[]{:S(2)}) copy-start(bf16[256,256]{1,0:T(8,128)(2,1)} %constant.23.clone.w3h) | copy-start | bytes 393220
  9.7 41.4 %copy-start.8 = (bf16[256,256]{1,0:T(8,128)(2,1)S(1)}, bf16[256,256]{1,0:T(8,128)(2,1)}, u32[]{:S(2)}) copy-start(bf16[256,256]{1,0:T(8,128)(2,1)} %constant.22.clone.w2l) | copy-start | bytes 393220
  9.7 41.4 %copy-start.9 = (bf16[256,256]{1,0:T(8,128)(2,1)S(1)}, bf16[256,256]{1,0:T(8,128)(2,1)}, u32[]{:S(2)}) copy-start(bf16[256,256]{1,0:T(8,128)(2,1)} %constant.21.clone.w2h) | copy-start | bytes 393220
  9.7 41.4 %copy-start.10 = (bf16[256,256]{1,0:T(8,128)(2,1)S(1)}, bf16[256,256]{1,0:T(8,128)(2,1)}, u32[]{:S(2)}) copy-start(bf16[256,256]{1,0:T(8,128)(2,1)} %constant.18.clone.w1) | copy-start | bytes 393220
  9.7 41.4 %copy-start.11 = (bf16[128,256]{1,0:T(8,128)(2,1)S(1)}, bf16[128,256]{1,0:T(8,128)(2,1)}, u32[]{:S(2)}) copy-start(bf16[128,256]{1,0:T(8,128)(2,1)} %constant.26.clone.w4l) | copy-start | bytes 196612
  9.7 41.4 %copy-start.12 = (bf16[128,256]{1,0:T(8,128)(2,1)S(1)}, bf16[128,256]{1,0:T(8,128)(2,1)}, u32[]{:S(2)}) copy-start(bf16[128,256]{1,0:T(8,128)(2,1)} %constant.25.clone.w4h) | copy-start | bytes 196612
  9.7 41.4 %copy-start.13 = (f32[128,128]{1,0:T(8,128)S(1)}, f32[128,128]{1,0:T(8,128)}, u32[]{:S(2)}) copy-start(f32[128,128]{1,0:T(8,128)} %constant.20.clone.sin_ref) | copy-start | bytes 196612
  9.7 41.4 %copy-start.14 = (f32[128,128]{1,0:T(8,128)S(1)}, f32[128,128]{1,0:T(8,128)}, u32[]{:S(2)}) copy-start(f32[128,128]{1,0:T(8,128)} %constant.19.clone.cos_ref) | copy-start | bytes 196612
  9.7 79.7 %copy-start.1 = (bf16[512,512]{1,0:T(8,128)(2,1)S(1)}, bf16[512,512]{1,0:T(8,128)(2,1)}, u32[]{:S(2)}) copy-start(bf16[512,512]{1,0:T(8,128)(2,1)} %value_ref.3) | copy-start | bytes 1572868
  9.7 79.7 %copy-start.3 = (bf16[512,512]{1,0:T(8,128)(2,1)S(1)}, bf16[512,512]{1,0:T(8,128)(2,1)}, u32[]{:S(2)}) copy-start(bf16[512,512]{1,0:T(8,128)(2,1)} %gate_ref.3) | copy-start | bytes 1572868
  9.8 79.7 %copy-start.5 = (bf16[512,512]{1,0:T(8,128)(2,1)S(1)}, bf16[512,512]{1,0:T(8,128)(2,1)}, u32[]{:S(2)}) copy-start(bf16[512,512]{1,0:T(8,128)(2,1)} %gate_out_ref.1) | copy-start | bytes 1572868
  9.8 79.7 %copy-start.15 = (f32[512]{0:T(512)S(1)}, f32[512]{0:T(512)}, u32[]{:S(2)}) copy-start(f32[512]{0:T(512)} %param.19) | copy-start | bytes 6148
  10.4 79.7 %copy-start.16 = (bf16[512,4096]{1,0:T(8,128)(2,1)S(1)}, bf16[512,4096]{1,0:T(8,128)(2,1)}, u32[]{:S(2)}) copy-start(bf16[512,4096]{1,0:T(8,128)(2,1)} %param.20) | copy-start | bytes 12582916
Sparse Core Ops, SparseCore 0:
  95.9 91.0 reduce-scatter.1

commit v2 on v1

v2 whole, which is shorter than its diff:
```python
import functools

import jax
import jax.numpy as jnp
import numpy as np
from jax import lax
from jax.experimental import pallas as pl
from jax.experimental.pallas import tpu as pltpu
from jax.sharding import PartitionSpec as P

EDGE = 128
VMEM = 48 * 1024 * 1024
ALONG_X = 4
CHUNKS = 2
BATCH = 8


def split_table(table):
    high = table.astype(jnp.bfloat16)
    low = (table - high.astype(np.float64)).astype(jnp.bfloat16)
    return high, low


@functools.cache
def transform_tables():
    steps = np.arange(EDGE)
    slow = 2.0 * np.pi * np.outer(steps + 0.25, steps) / EDGE
    fast = 2.0 * np.pi * np.outer(steps, steps) / EDGE
    turn = 2.0 * np.pi * np.outer(steps + 0.25, steps) / (EDGE * EDGE)
    first = np.concatenate([np.cos(slow), -np.sin(slow)], 0)
    second = np.block([[np.cos(fast), -np.sin(fast)], [np.sin(fast), np.cos(fast)]])
    third = np.block([[np.cos(fast), np.sin(fast)], [-np.sin(fast), np.cos(fast)]]) / EDGE
    last = np.concatenate([np.cos(slow).T, -np.sin(slow).T], 1) / EDGE
    first_high, first_low = split_table(first)
    stacked = [np.concatenate([first_high, first_low], 1)]
    for table in (second, third, last):
        stacked.extend(split_table(table))
    return (
        np.concatenate(stacked, 0),
        np.stack([np.cos(turn), np.sin(turn)]).astype(np.float32),
    )


def halves(array):
    high = array.astype(jnp.bfloat16)
    return high, (array - high.astype(jnp.float32)).astype(jnp.bfloat16)


def dot(a, b):
    return jnp.dot(a, b, preferred_element_type=jnp.float32)


def pack_kernel(value_hbm, gate_hbm, filt_hbm, out_ref, held, arrived):
    slabs = out_ref.shape[1]

    def fetch(which, slab):
        array = (value_hbm, gate_hbm, filt_hbm)[which]
        rows = pl.ds(slab * EDGE, EDGE)
        return pltpu.make_async_copy(
            array.at[rows, :], held.at[which, rows, :], arrived.at[which, slab]
        )

    for slab in range(slabs):
        for which in range(3):
            fetch(which, slab).start()
    chans = out_ref.shape[3]
    peers = EDGE // chans
    for slab in range(slabs):
        rows = slice(slab * EDGE, (slab + 1) * EDGE)
        for which in range(3):
            fetch(which, slab).wait()
        gated = held[0, rows].astype(jnp.float32) * held[1, rows].astype(jnp.float32)
        for which, array in enumerate((gated.astype(jnp.bfloat16), held[2, rows])):
            for part in range(array.shape[1] // EDGE):
                turned = array[:, part * EDGE : (part + 1) * EDGE].T
                out_ref[part * peers : (part + 1) * peers, slab, which] = turned.reshape(
                    peers, chans, EDGE
                )


def conv_kernel(chans, in_ref, tables, turns, out_ref, wide, back):
    wide[...] = in_ref[...].astype(jnp.float32)
    cos, sin = turns[0], turns[1]

    def table(index, rows=2 * EDGE):
        start = min(index, 5) * 2 * EDGE + max(index - 5, 0) * EDGE
        return tables[start : start + rows, :]

    def thrice(high, low, index):
        top = table(index)
        return dot(high, top) + dot(low, top) + dot(high, table(index + 1))

    @pl.loop(0, chans // BATCH)
    def _(step):
        first = step * BATCH
        signals = [
            wide[pl.ds(which * chans + first + k, EDGE, stride=2 * chans), :].astype(jnp.bfloat16)
            for k in range(BATCH)
            for which in range(2)
        ]
        both = jnp.concatenate(signals, axis=1)
        slow = dot(table(0), jnp.concatenate([both, both], axis=0))
        rows = []
        for k in range(2 * BATCH):
            cols = slice(k * EDGE, (k + 1) * EDGE)
            real, imag = slow[:EDGE, cols], slow[EDGE:, cols]
            rows.append(
                jnp.concatenate([real * cos + imag * sin, imag * cos - real * sin], axis=1)
            )
        spectra = thrice(*halves(jnp.concatenate(rows, axis=0)), 1)
        rows = []
        for k in range(BATCH):
            ours = spectra[2 * k * EDGE : (2 * k + 1) * EDGE]
            taps = spectra[(2 * k + 1) * EDGE : (2 * k + 2) * EDGE]
            ar, ai, br, bi = ours[:, :EDGE], ours[:, EDGE:], taps[:, :EDGE], taps[:, EDGE:]
            rows.append(jnp.concatenate([ar * br - ai * bi, ar * bi + ai * br], axis=1))
        wound = thrice(*halves(jnp.concatenate(rows, axis=0)), 3)
        cols = []
        for k in range(BATCH):
            real = wound[k * EDGE : (k + 1) * EDGE, :EDGE]
            imag = wound[k * EDGE : (k + 1) * EDGE, EDGE:]
            cols.append(
                jnp.concatenate([real * cos - imag * sin, imag * cos + real * sin], axis=0)
            )
        high, low = halves(jnp.concatenate(cols, axis=1))
        top = table(5, EDGE)
        conv = dot(top, high) + dot(top, low) + dot(table(6, EDGE), high)
        for k in range(BATCH):
            back[pl.ds(first + k, EDGE, stride=chans), :] = conv[:, k * EDGE : (k + 1) * EDGE]

    out_ref[...] = back[...].astype(jnp.bfloat16)


def mix_kernel(_, conv_ref, value_ref, gate_ref, gate_out_ref, skip_ref, out_ref):
    peers = EDGE // conv_ref.shape[2]
    for part in range(out_ref.shape[1] // EDGE):
        cols = slice(part * EDGE, (part + 1) * EDGE)
        conv = conv_ref[part * peers : (part + 1) * peers, 0].reshape(EDGE, EDGE).T
        gated = (
            gate_ref[:, cols].astype(jnp.float32) * value_ref[:, cols].astype(jnp.float32)
        ).astype(jnp.bfloat16)
        inner = conv.astype(jnp.float32) + skip_ref[:, cols] * gated.astype(jnp.float32)
        out_ref[:, cols] = (gate_out_ref[:, cols].astype(jnp.float32) * inner).astype(
            jnp.bfloat16
        )


def deal_kernel(place, w_hbm, own_ref, *rest):
    pieces, done = rest[:-1], rest[-1]
    x, y, core = place[0], place[1], place[2]
    width = own_ref.shape[-1]
    half = width // 2

    def block(row_half, col_half, target):
        col = (lax.rem(y + col_half, 2) * ALONG_X + target) * width
        return w_hbm.at[
            pl.ds(pl.multiple_of(row_half * half, half), half),
            pl.ds(pl.multiple_of(col, width), width),
        ]

    copies = []
    for shift in range(ALONG_X):
        target = lax.rem(x + shift, ALONG_X)
        for col_half in range(2):
            for row_half in range(1 if shift else 2):
                rows = pl.ds(row_half * half, half)
                into = pieces[shift - 1] if shift else own_ref
                copies.append(
                    pltpu.make_async_copy(
                        block(lax.rem(core + row_half, 2), col_half, target),
                        into.at[col_half, rows, :],
                        done.at[len(copies)],
                    )
                )
    for copy in copies:
        copy.start()
    for copy in copies:
        copy.wait()


def project_kernel(col_half, *refs):
    parts, weights, out_ref = refs[:ALONG_X], refs[ALONG_X:-1], refs[-1]
    half = parts[0].shape[1] // 2
    total = dot(parts[0][...], weights[0][col_half])
    for shift in range(1, ALONG_X):
        for row_half in range(2):
            total = total + dot(
                parts[shift][:, row_half * half : (row_half + 1) * half],
                weights[2 * shift - 1 + row_half][col_half],
            )
    out_ref[...] = total.astype(out_ref.dtype)


def pack(value, gate_in, filt, groups):
    rows, width = value.shape
    slabs, chans = rows // EDGE, width // groups
    return pl.pallas_call(
        pack_kernel,
        in_specs=[pl.BlockSpec(memory_space=pl.ANY)] * 3,
        out_specs=pl.BlockSpec(memory_space=pltpu.VMEM),
        out_shape=jax.ShapeDtypeStruct((groups, slabs, 2, chans, EDGE), jnp.bfloat16),
        scratch_shapes=[
            pltpu.VMEM((3, rows, width), jnp.bfloat16),
            pltpu.SemaphoreType.DMA((3, slabs)),
        ],
        compiler_params=pltpu.CompilerParams(vmem_limit_bytes=VMEM),
        name="pack",
    )(value, gate_in, filt)


def convolve(spread):
    groups, slabs, _, chans, _ = spread.shape
    tables = transform_tables()
    rows = groups * slabs * chans
    whole = pl.BlockSpec(memory_space=pltpu.VMEM)
    conv = pl.pallas_call(
        functools.partial(conv_kernel, chans),
        in_specs=[whole] * (1 + len(tables)),
        out_specs=whole,
        out_shape=jax.ShapeDtypeStruct((rows, EDGE), jnp.bfloat16),
        scratch_shapes=[
            pltpu.VMEM((2 * rows, EDGE), jnp.float32),
            pltpu.VMEM((rows, EDGE), jnp.float32),
        ],
        compiler_params=pltpu.CompilerParams(vmem_limit_bytes=VMEM),
        cost_estimate=pl.CostEstimate(
            flops=6 * 10**9, bytes_accessed=2 * 10**6, transcendentals=0
        ),
        name="convolve",
    )(spread.reshape(2 * rows, EDGE), *(jnp.asarray(table) for table in tables))
    return conv.reshape(groups, slabs, chans, EDGE)


def mix(conv, value, gate_in, gate_out, skip, core):
    rows, width = value.shape
    groups, _, chans, _ = conv.shape
    block = pl.BlockSpec((EDGE, width // 2), lambda i, j, core: (i, j))
    return pl.pallas_call(
        mix_kernel,
        grid_spec=pltpu.PrefetchScalarGridSpec(
            num_scalar_prefetch=1,
            grid=(rows // EDGE, 2),
            in_specs=[
                pl.BlockSpec((groups // 2, 1, chans, EDGE), lambda i, j, core: (j, i, 0, 0)),
                block,
                block,
                block,
                pl.BlockSpec((1, width // 2), lambda i, j, core: (0, j)),
            ],
            out_specs=pl.BlockSpec(
                (EDGE, width // 2), lambda i, j, core: (i, lax.rem(j + core[0], 2))
            ),
        ),
        out_shape=jax.ShapeDtypeStruct((rows, width), jnp.bfloat16),
        compiler_params=pltpu.CompilerParams(vmem_limit_bytes=VMEM),
        name="mix",
    )(core, conv, value, gate_in, gate_out, skip[None])


def deal(w_out, place, width):
    whole = pl.BlockSpec(memory_space=pltpu.VMEM)
    shapes = [(2, width, width)] + [(2, width // 2, width)] * (ALONG_X - 1)
    return pl.pallas_call(
        deal_kernel,
        in_specs=[
            pl.BlockSpec(memory_space=pltpu.SMEM),
            pl.BlockSpec(memory_space=pl.ANY),
        ],
        out_specs=[whole] * ALONG_X,
        out_shape=[jax.ShapeDtypeStruct(shape, jnp.bfloat16) for shape in shapes],
        scratch_shapes=[pltpu.SemaphoreType.DMA((2 * ALONG_X + 2,))],
        compiler_params=pltpu.CompilerParams(vmem_limit_bytes=VMEM),
        name="deal",
    )(place, w_out)


def project_half(parts, weights, col_half, dtype):
    rows, width = parts[0].shape
    whole = pl.BlockSpec(memory_space=pltpu.VMEM)
    return pl.pallas_call(
        functools.partial(project_kernel, col_half),
        in_specs=[whole] * (len(parts) + len(weights)),
        out_specs=whole,
        out_shape=jax.ShapeDtypeStruct((rows, width), dtype),
        compiler_params=pltpu.CompilerParams(vmem_limit_bytes=VMEM),
        cost_estimate=pl.CostEstimate(
            flops=2 * rows * ALONG_X * width * width, bytes_accessed=3 * 10**6, transcendentals=0
        ),
        name="project",
    )(*parts, *weights)


def along_x(shift):
    return [
        (i, i // ALONG_X * ALONG_X + (i + shift) % ALONG_X) for i in range(2 * ALONG_X)
    ]


def across_y():
    return [(i, (i + ALONG_X) % (2 * ALONG_X)) for i in range(2 * ALONG_X)]


def project(mixed, weights):
    rows, width = mixed.shape
    depth = rows // CHUNKS
    parts, theirs, outs = [], [], []
    for chunk in range(CHUNKS):
        own = mixed[chunk * depth : (chunk + 1) * depth]
        parts.append(
            [own]
            + [lax.ppermute(own, "chan", along_x(shift)) for shift in range(1, ALONG_X)]
        )
    for chunk in range(CHUNKS):
        share = project_half(parts[chunk], weights, 1, jnp.bfloat16)
        theirs.append(lax.ppermute(share, "chan", across_y()))
    for chunk in range(CHUNKS):
        mine = project_half(parts[chunk], weights, 0, jnp.float32)
        outs.append((mine + theirs[chunk].astype(jnp.float32)).astype(jnp.bfloat16))
    return jnp.concatenate(outs, axis=0)


def per_device(value, gate_in, gate_out, filt, skip, w_out):
    groups = lax.axis_size("ctx")
    place = lax.axis_index("chan")
    core = lax.rem(lax.axis_index("ctx"), 2)
    where = jnp.stack([lax.rem(place, ALONG_X), lax.div(place, ALONG_X), core])
    own, *pieces = deal(w_out, where, value.shape[1])
    pieces = [lax.ppermute(piece, "chan", along_x(i + 1)) for i, piece in enumerate(pieces)]
    packed = pack(value, gate_in, filt, groups)
    spread = lax.all_to_all(packed, "ctx", split_axis=0, concat_axis=0, tiled=True)
    spread, *pieces = lax.optimization_barrier((spread, *pieces))
    other = [(i, i ^ 1) for i in range(groups)]
    halves_of_core = [lax.ppermute(piece, "ctx", other) for piece in pieces]
    conv = convolve(spread)
    conv, *halves_of_core = lax.optimization_barrier((conv, *halves_of_core))
    returned = lax.all_to_all(conv, "ctx", split_axis=0, concat_axis=0, tiled=True)
    mixed = mix(returned, value, gate_in, gate_out, skip, core[None])
    weights = [own]
    for ours, theirs in zip(pieces, halves_of_core):
        weights += [ours, theirs]
    return project(mixed, weights)


def solution(mesh):
    placed = (
        P("ctx", "chan"),
        P("ctx", "chan"),
        P("ctx", "chan"),
        P("ctx", "chan"),
        P("chan"),
        P("chan", None),
    )
    return jax.shard_map(
        per_device, mesh=mesh, in_specs=placed, out_specs=P("ctx", "chan"), check_vma=False
    )
```

time: 198 us -> 125 us (0.63)
  waiting for transfers between devices: 91.3 us -> 44.1 us
  blocking collectives: 63.1 us -> 27.3 us
  starting transfers between devices: 0.01 us -> 29.5 us
  between operations: 13.6 us -> 0.19 us
  matrix products: 5.65 us -> 0 us
    reduce_scatter x1 -> x0, waiting for transfers between devices: 91.2 us -> none  [per_device(): lax.psum_scatter(partial_out, 'chan', scatter_dimension=1, tiled=True)]
    ppermute x0 -> x14, waiting for transfers between devices: none -> 44.1 us  [the longest x3 21.8 us: per_device(): lax.ppermute(piece, 'chan', along_x(i + 1))]
    all_to_all x1 -> x0, blocking collectives: 40.6 us -> none  [per_device(): lax.all_to_all(packed, 'ctx', split_axis=0, concat_axis=0, tiled=True)]
    ppermute x0 -> x14, starting transfers between devices: none -> 17.9 us  [the longest x6 8.81 us: project(): lax.ppermute(own, 'chan', along_x(shift))]
    all_to_all x0 -> x1, starting transfers between devices: none -> 11.7 us  [per_device(): lax.all_to_all(packed, 'ctx', split_axis=0, concat_axis=0, tiled=True)]
    pallas_call x2 -> x7, Pallas kernels: 1.22 us -> 9.92 us  [the longest x1 3.6 us: pack(): pl.pallas_call(pack_kernel, in_specs=[pl.BlockSpec(memory_space=pl.ANY)]...]
    pallas_call x1, Pallas kernels: 15.9 us -> 8.85 us  [convolve(): pl.pallas_call(functools.partial(conv_kernel, chans), in_specs=[whole] *...]
    dot_general x1 -> x0, matrix products: 5.65 us -> none  [per_device(): partial_out = jnp.dot(mixed, w_out, preferred_element_type=jnp.float32)]
  transfers between devices with their start and end apart: 1 -> 15, of which waited for: 1 -> 8; matrix products, arithmetic and copies ran while one was open for 0% -> 0% of each run, Pallas kernels for 0% -> 11%
where the time goes in v2:
time: 125 us; the launch traced here: 124 us
  waiting for transfers between devices  44.1 us (35%)
  starting transfers between devices  29.5 us (24%)
  blocking collectives  27.3 us (22%)
  Pallas kernels  18.8 us (15%)
  local copies, waits for them, and re-layouts  3.19 us (3%)
    all_to_all x1, blocking collectives, per_device(): lax.all_to_all(conv, 'ctx', split_axis=0, concat_axis=0, tiled=True)  27.3 us
    ppermute x3, waiting for transfers between devices, per_device(): lax.ppermute(piece, 'chan', along_x(i + 1))  21.8 us
    ppermute x6, waiting for transfers between devices, project(): lax.ppermute(own, 'chan', along_x(shift))  17 us
    all_to_all x1, starting transfers between devices, per_device(): lax.all_to_all(packed, 'ctx', split_axis=0, concat_axis=0, tiled=True)  11.7 us
    pallas_call x1, Pallas kernels, convolve(): pl.pallas_call(functools.partial(conv_kernel, chans), in_specs=[whole] *...  8.85 us
    ppermute x6, starting transfers between devices, project(): lax.ppermute(own, 'chan', along_x(shift))  8.81 us
    ppermute x3, starting transfers between devices, per_device(): lax.ppermute(piece, 'chan', along_x(i + 1))  5.73 us
    ppermute x2, waiting for transfers between devices, project(): theirs.append(lax.ppermute(share, 'chan', across_y()))  5.34 us
  transfers between devices with their start and end apart: 15, of which 8 were waited for; matrix products, arithmetic and copies ran while one was open for 0% of the time, Pallas kernels for 11%

profile of v2, /device:TPU:16, one launch (start us, length us, event | category | flops | bytes accessed | tf_op | source)
XLA Modules:
  0.0 124.1 jit_solution(9277122474212980557)
XLA Ops:
  0.0 0.0 copy-start
  0.0 1.0 copy-done
  1.0 0.0 copy-start.2
  1.0 1.0 copy-done.2
  2.1 0.0 copy-start.4
  2.1 1.0 copy-done.4
  3.1 0.0 copy-start.7
  3.1 0.0 copy-start.8
  3.1 3.6 %pack.1 = bf16[32,4,2,16,128]{4,3,2,1,0:T(8,128)(2,1)} custom-call(bf16[512,512]{1,0:T(8,128)(2,1)S(1)} %copy-done, bf16[512,512]{1,0:T(8,128)(2,1)S(1)} %copy-done.2, bf16[512,512]{1,0:T(8,128)(2,1)S(1)} %copy-done.4), custom_call_target="tpu_custom_call" | custom-call | tf_op jit(solution)/shard_map/pack/pallas_call | solution.py:197
  6.7 11.7 %all-to-all-start = ((bf16[32,4,2,16,128]{4,3,2,1,0:T(8,128)(2,1)}), bf16[32,4,2,16,128]{4,3,2,1,0:T(8,128)(2,1)}, u32[]{:S(2)}, u32[]{:S(2)}) async-start(bf16[32,4,2,16,128]{4,3,2,1,0:T(8,128)(2,1)} %pack.1), calls=%async_computation | async-start | bytes 2097152 | tf_op jit(solution)/shard_map/all_to_all | solution.py:330
  18.4 0.1 pad_add_fusion.place
  18.5 2.3 %deal.1 = (bf16[2,512,512]{2,1,0:T(8,128)(2,1)S(1)}, bf16[2,256,512]{2,1,0:T(8,128)(2,1)S(1)}, bf16[2,256,512]{2,1,0:T(8,128)(2,1)S(1)}, bf16[2,256,512]{2,1,0:T(8,128)(2,1)S(1)}) custom-call(s32[3]{0:T(128)S(1)} %pad_add_fusion.place, bf16[512,4096]{1,0:T(8,128)(2,1)} %w_hbm.1), custom_call_target="tpu_custom_call" | custom-call | tf_op jit(solution)/shard_map/deal/pallas_call | solution.py:263
  20.8 1.6 %collective-permute-start = (bf16[2,256,512]{2,1,0:T(8,128)(2,1)S(1)}, bf16[2,256,512]{2,1,0:T(8,128)(2,1)S(1)}, u32[]{:S(2)}, u32[]{:S(2)}) collective-permute-start(bf16[2,256,512]{2,1,0:T(8,128)(2,1)S(1)} %get-tuple-element.17), channel_id=1, source_target_pairs={{0,32},{32,64},{64,96},{96,0},{128,160},{160,192},{192,224},{224,1... | collective-permute-start | bytes 1572872 | tf_op jit(solution)/shard_map/ppermute | solution.py:328
  22.4 2.7 %collective-permute-start.1 = (bf16[2,256,512]{2,1,0:T(8,128)(2,1)S(1)}, bf16[2,256,512]{2,1,0:T(8,128)(2,1)S(1)}, u32[]{:S(2)}, u32[]{:S(2)}) collective-permute-start(bf16[2,256,512]{2,1,0:T(8,128)(2,1)S(1)} %get-tuple-element.18), channel_id=1, source_target_pairs={{0,64},{32,96},{64,0},{96,32},{128,192},{160,224},{192,128},{224,1... | collective-permute-start | bytes 1572872 | tf_op jit(solution)/shard_map/ppermute | solution.py:328
  25.1 1.4 %collective-permute-start.2 = (bf16[2,256,512]{2,1,0:T(8,128)(2,1)S(1)}, bf16[2,256,512]{2,1,0:T(8,128)(2,1)S(1)}, u32[]{:S(2)}, u32[]{:S(2)}) collective-permute-start(bf16[2,256,512]{2,1,0:T(8,128)(2,1)S(1)} %get-tuple-element.19), channel_id=1, source_target_pairs={{0,96},{32,0},{64,32},{96,64},{128,224},{160,128},{192,160},{224,1... | collective-permute-start | bytes 1572872 | tf_op jit(solution)/shard_map/ppermute | solution.py:328
  26.6 9.5 %collective-permute-done.refs_5_ = bf16[2,256,512]{2,1,0:T(8,128)(2,1)S(1)} collective-permute-done((bf16[2,256,512]{2,1,0:T(8,128)(2,1)S(1)}, bf16[2,256,512]{2,1,0:T(8,128)(2,1)S(1)}, u32[]{:S(2)}, u32[]{:S(2)}) %collective-permute-start) | collective-permute-done | bytes 524320 | tf_op jit(solution)/shard_map/ppermute | solution.py:328
  36.1 12.2 %collective-permute-done.1.refs_7_ = bf16[2,256,512]{2,1,0:T(8,128)(2,1)S(1)} collective-permute-done((bf16[2,256,512]{2,1,0:T(8,128)(2,1)S(1)}, bf16[2,256,512]{2,1,0:T(8,128)(2,1)S(1)}, u32[]{:S(2)}, u32[]{:S(2)}) %collective-permute-start.1) | collective-permute-done | bytes 524320 | tf_op jit(solution)/shard_map/ppermute | solution.py:328
  48.3 0.0 collective-permute-done.2.refs_9_
  48.3 0.0 all-to-all-done
  48.3 0.0 collective-permute-start.3
  48.3 0.5 collective-permute-start.4
  48.8 0.1 collective-permute-start.5
  48.9 0.0 copy-done.7
  48.9 0.0 copy-done.8
  48.9 0.0 copy-start.1
  48.9 0.0 copy-start.3
  48.9 0.0 copy-start.5
  48.9 0.0 copy-start.6
  49.0 8.9 %convolve.1 = bf16[2048,128]{1,0:T(8,128)(2,1)S(1)} custom-call(bf16[4096,128]{1,0:T(8,128)(2,1)} %bitcast.3.in_ref, bf16[1536,256]{1,0:T(8,128)(2,1)S(1)} %copy-done.7, f32[2,128,128]{2,1,0:T(8,128)S(1)} %copy-done.8), custom_call_target="tpu_custom_call" | custom-call | flops 6000000000 | bytes 2000000 | tf_op jit(solution)/shard_map/convolve/pallas_call | solution.py:216
  57.8 0.0 collective-permute-done.3.refs_6_
  57.8 0.0 collective-permute-done.4.refs_8_
  57.8 0.0 collective-permute-done.5.refs_10_
  57.8 27.3 %all_to_all.10.conv_ref = bf16[32,4,16,128]{3,2,1,0:T(8,128)(2,1)S(1)} all-to-all(bf16[32,4,16,128]{3,2,1,0:T(8,128)(2,1)S(1)} %bitcast.6), channel_id=1, replica_groups=mesh['chan'=8,'ctx'=32] {'ctx'}, dimensions={0} | all-to-all | bytes 1048576 | tf_op jit(solution)/shard_map/all_to_all | solution.py:336
  85.2 0.0 copy-done.1
  85.2 0.0 copy-done.3
  85.2 0.0 copy-done.5
  85.2 0.0 copy-done.6
  85.2 1.2 mix.1
  86.4 2.3 %collective-permute-start.8 = (bf16[256,512]{1,0:T(8,128)(2,1)S(1)}, bf16[256,512]{1,0:T(8,128)(2,1)S(1)}, u32[]{:S(2)}, u32[]{:S(2)}) collective-permute-start(bf16[256,512]{1,0:T(8,128)(2,1)S(1)} %get-tuple-element.29.refs_0_), channel_id=1, source_target_pairs={{0,96},{32,0},{64,32},{96,64},{128,224},{160,128},{192,160},{224,1... | collective-permute-start | bytes 786440 | tf_op jit(solution)/shard_map/ppermute | solution.py:311
  88.8 1.1 collective-permute-start.7
  89.9 0.7 collective-permute-start.6
  90.6 2.6 %collective-permute-start.12 = (bf16[256,512]{1,0:T(8,128)(2,1)S(1)}, bf16[256,512]{1,0:T(8,128)(2,1)S(1)}, u32[]{:S(2)}, u32[]{:S(2)}) collective-permute-start(bf16[256,512]{1,0:T(8,128)(2,1)S(1)} %get-tuple-element.30.refs_0_), channel_id=1, source_target_pairs={{0,96},{32,0},{64,32},{96,64},{128,224},{160,128},{192,160},{224,1... | collective-permute-start | bytes 786440 | tf_op jit(solution)/shard_map/ppermute | solution.py:311
  93.1 1.2 collective-permute-start.11
  94.3 6.7 %collective-permute-done.8.refs_3_ = bf16[256,512]{1,0:T(8,128)(2,1)S(1)} collective-permute-done((bf16[256,512]{1,0:T(8,128)(2,1)S(1)}, bf16[256,512]{1,0:T(8,128)(2,1)S(1)}, u32[]{:S(2)}, u32[]{:S(2)}) %collective-permute-start.8) | collective-permute-done | bytes 262176 | tf_op jit(solution)/shard_map/ppermute | solution.py:311
  101.0 0.9 collective-permute-start.10
  101.9 0.0 collective-permute-done.7.refs_2_
  101.9 3.3 %collective-permute-done.6.refs_1_ = bf16[256,512]{1,0:T(8,128)(2,1)S(1)} collective-permute-done((bf16[256,512]{1,0:T(8,128)(2,1)S(1)}, bf16[256,512]{1,0:T(8,128)(2,1)S(1)}, u32[]{:S(2)}, u32[]{:S(2)}) %collective-permute-start.6) | collective-permute-done | bytes 262176 | tf_op jit(solution)/shard_map/ppermute | solution.py:311
  105.2 0.7 project.5
  105.9 1.4 %collective-permute-start.9 = (bf16[256,512]{1,0:T(8,128)(2,1)S(1)}, bf16[256,512]{1,0:T(8,128)(2,1)S(1)}, u32[]{:S(2)}, u32[]{:S(2)}) collective-permute-start(bf16[256,512]{1,0:T(8,128)(2,1)S(1)} %project.5), channel_id=1, source_target_pairs={{0,128},{32,160},{64,192},{96,224},{128,0},{160,32},{192,64},{224,... | collective-permute-start | bytes 786440 | tf_op jit(solution)/shard_map/ppermute | solution.py:315
  107.3 3.3 %collective-permute-done.12.refs_3_ = bf16[256,512]{1,0:T(8,128)(2,1)S(1)} collective-permute-done((bf16[256,512]{1,0:T(8,128)(2,1)S(1)}, bf16[256,512]{1,0:T(8,128)(2,1)S(1)}, u32[]{:S(2)}, u32[]{:S(2)}) %collective-permute-start.12) | collective-permute-done | bytes 262176 | tf_op jit(solution)/shard_map/ppermute | solution.py:311
  110.6 0.2 collective-permute-done.11.refs_2_
  110.8 3.5 %collective-permute-done.10.refs_1_ = bf16[256,512]{1,0:T(8,128)(2,1)S(1)} collective-permute-done((bf16[256,512]{1,0:T(8,128)(2,1)S(1)}, bf16[256,512]{1,0:T(8,128)(2,1)S(1)}, u32[]{:S(2)}, u32[]{:S(2)}) %collective-permute-start.10) | collective-permute-done | bytes 262176 | tf_op jit(solution)/shard_map/ppermute | solution.py:311
  114.3 0.7 project.7
  115.0 1.4 %collective-permute-start.13 = (bf16[256,512]{1,0:T(8,128)(2,1)S(1)}, bf16[256,512]{1,0:T(8,128)(2,1)S(1)}, u32[]{:S(2)}, u32[]{:S(2)}) collective-permute-start(bf16[256,512]{1,0:T(8,128)(2,1)S(1)} %project.7), channel_id=1, source_target_pairs={{0,128},{32,160},{64,192},{96,224},{128,0},{160,32},{192,64},{224,... | collective-permute-start | bytes 786440 | tf_op jit(solution)/shard_map/ppermute | solution.py:315
  116.4 0.7 project.4
  117.1 0.7 project.6
  117.8 0.0 collective-permute-done.9
  117.8 0.1 add_convert_fusion.1
  117.9 5.3 %collective-permute-done.13 = bf16[256,512]{1,0:T(8,128)(2,1)S(1)} collective-permute-done((bf16[256,512]{1,0:T(8,128)(2,1)S(1)}, bf16[256,512]{1,0:T(8,128)(2,1)S(1)}, u32[]{:S(2)}, u32[]{:S(2)}) %collective-permute-start.13) | collective-permute-done | bytes 262176 | tf_op jit(solution)/shard_map/ppermute | solution.py:315
  123.2 0.1 add_convert_fusion
  123.3 0.8 pad_maximum_fusion
  (1 shorter events, 0.0 us)
Async XLA Ops:
  0.0 1.0 copy-start
  1.0 1.0 copy-start.2
  2.1 1.0 copy-start.4
  3.1 45.8 %copy-start.7 = (bf16[1536,256]{1,0:T(8,128)(2,1)S(1)}, bf16[1536,256]{1,0:T(8,128)(2,1)}, u32[]{:S(2)}) copy-start(bf16[1536,256]{1,0:T(8,128)(2,1)} %constant.25.clone.tables) | copy-start | bytes 2359300
  3.1 45.8 %copy-start.8 = (f32[2,128,128]{2,1,0:T(8,128)S(1)}, f32[2,128,128]{2,1,0:T(8,128)}, u32[]{:S(2)}) copy-start(f32[2,128,128]{2,1,0:T(8,128)} %constant.26.clone.turns) | copy-start | bytes 393220
  6.7 41.6 %all-to-all-start = ((bf16[32,4,2,16,128]{4,3,2,1,0:T(8,128)(2,1)}), bf16[32,4,2,16,128]{4,3,2,1,0:T(8,128)(2,1)}, u32[]{:S(2)}, u32[]{:S(2)}) async-start(bf16[32,4,2,16,128]{4,3,2,1,0:T(8,128)(2,1)} %pack.1), calls=%async_computation | async-start | bytes 2097152 | tf_op jit(solution)/shard_map/all_to_all | solution.py:330
  20.8 15.3 %collective-permute-start = (bf16[2,256,512]{2,1,0:T(8,128)(2,1)S(1)}, bf16[2,256,512]{2,1,0:T(8,128)(2,1)S(1)}, u32[]{:S(2)}, u32[]{:S(2)}) collective-permute-start(bf16[2,256,512]{2,1,0:T(8,128)(2,1)S(1)} %get-tuple-element.17), channel_id=1, source_target_pairs={{0,32},{32,64},{64,96},{96,0},{128,160},{160,192},{192,224},{224,1... | collective-permute-start | bytes 1572872 | tf_op jit(solution)/shard_map/ppermute | solution.py:328
  22.4 25.9 %collective-permute-start.1 = (bf16[2,256,512]{2,1,0:T(8,128)(2,1)S(1)}, bf16[2,256,512]{2,1,0:T(8,128)(2,1)S(1)}, u32[]{:S(2)}, u32[]{:S(2)}) collective-permute-start(bf16[2,256,512]{2,1,0:T(8,128)(2,1)S(1)} %get-tuple-element.18), channel_id=1, source_target_pairs={{0,64},{32,96},{64,0},{96,32},{128,192},{160,224},{192,128},{224,1... | collective-permute-start | bytes 1572872 | tf_op jit(solution)/shard_map/ppermute | solution.py:328
  25.1 23.2 %collective-permute-start.2 = (bf16[2,256,512]{2,1,0:T(8,128)(2,1)S(1)}, bf16[2,256,512]{2,1,0:T(8,128)(2,1)S(1)}, u32[]{:S(2)}, u32[]{:S(2)}) collective-permute-start(bf16[2,256,512]{2,1,0:T(8,128)(2,1)S(1)} %get-tuple-element.19), channel_id=1, source_target_pairs={{0,96},{32,0},{64,32},{96,64},{128,224},{160,128},{192,160},{224,1... | collective-permute-start | bytes 1572872 | tf_op jit(solution)/shard_map/ppermute | solution.py:328
  48.3 9.5 %collective-permute-start.3 = (bf16[2,256,512]{2,1,0:T(8,128)(2,1)S(1)}, bf16[2,256,512]{2,1,0:T(8,128)(2,1)S(1)}, u32[]{:S(2)}, u32[]{:S(2)}) collective-permute-start(bf16[2,256,512]{2,1,0:T(8,128)(2,1)S(1)} %collective-permute-done.refs_5_), channel_id=1, source_target_pairs={{0,1},{1,0},{2,3},{3,2},{4,5},{5,4},{6,7},{7,6},{8,9},{9,8},{10,11... | collective-permute-start | bytes 1572872 | tf_op jit(solution)/shard_map/ppermute | solution.py:333
  48.3 9.5 %collective-permute-start.4 = (bf16[2,256,512]{2,1,0:T(8,128)(2,1)S(1)}, bf16[2,256,512]{2,1,0:T(8,128)(2,1)S(1)}, u32[]{:S(2)}, u32[]{:S(2)}) collective-permute-start(bf16[2,256,512]{2,1,0:T(8,128)(2,1)S(1)} %collective-permute-done.1.refs_7_), channel_id=1, source_target_pairs={{0,1},{1,0},{2,3},{3,2},{4,5},{5,4},{6,7},{7,6},{8,9},{9,8},{10,11... | collective-permute-start | bytes 1572872 | tf_op jit(solution)/shard_map/ppermute | solution.py:333
  48.8 9.0 %collective-permute-start.5 = (bf16[2,256,512]{2,1,0:T(8,128)(2,1)S(1)}, bf16[2,256,512]{2,1,0:T(8,128)(2,1)S(1)}, u32[]{:S(2)}, u32[]{:S(2)}) collective-permute-start(bf16[2,256,512]{2,1,0:T(8,128)(2,1)S(1)} %collective-permute-done.2.refs_9_), channel_id=1, source_target_pairs={{0,1},{1,0},{2,3},{3,2},{4,5},{5,4},{6,7},{7,6},{8,9},{9,8},{10,11... | collective-permute-start | bytes 1572872 | tf_op jit(solution)/shard_map/ppermute | solution.py:333
  48.9 36.2 %copy-start.1 = (bf16[512,512]{1,0:T(8,128)(2,1)S(1)}, bf16[512,512]{1,0:T(8,128)(2,1)}, u32[]{:S(2)}) copy-start(bf16[512,512]{1,0:T(8,128)(2,1)} %value_ref.1) | copy-start | bytes 1572868
  48.9 36.2 %copy-start.3 = (bf16[512,512]{1,0:T(8,128)(2,1)S(1)}, bf16[512,512]{1,0:T(8,128)(2,1)}, u32[]{:S(2)}) copy-start(bf16[512,512]{1,0:T(8,128)(2,1)} %gate_ref.1) | copy-start | bytes 1572868
  48.9 36.2 %copy-start.5 = (bf16[512,512]{1,0:T(8,128)(2,1)S(1)}, bf16[512,512]{1,0:T(8,128)(2,1)}, u32[]{:S(2)}) copy-start(bf16[512,512]{1,0:T(8,128)(2,1)} %gate_out_ref.1) | copy-start | bytes 1572868
  48.9 36.2 %copy-start.6 = (f32[512]{0:T(512)S(1)}, f32[512]{0:T(512)}, u32[]{:S(2)}) copy-start(f32[512]{0:T(512)} %param.12) | copy-start | bytes 6148
  86.4 14.6 %collective-permute-start.8 = (bf16[256,512]{1,0:T(8,128)(2,1)S(1)}, bf16[256,512]{1,0:T(8,128)(2,1)S(1)}, u32[]{:S(2)}, u32[]{:S(2)}) collective-permute-start(bf16[256,512]{1,0:T(8,128)(2,1)S(1)} %get-tuple-element.29.refs_0_), channel_id=1, source_target_pairs={{0,96},{32,0},{64,32},{96,64},{128,224},{160,128},{192,160},{224,1... | collective-permute-start | bytes 786440 | tf_op jit(solution)/shard_map/ppermute | solution.py:311
  88.8 13.2 %collective-permute-start.7 = (bf16[256,512]{1,0:T(8,128)(2,1)S(1)}, bf16[256,512]{1,0:T(8,128)(2,1)S(1)}, u32[]{:S(2)}, u32[]{:S(2)}) collective-permute-start(bf16[256,512]{1,0:T(8,128)(2,1)S(1)} %get-tuple-element.29.refs_0_), channel_id=1, source_target_pairs={{0,64},{32,96},{64,0},{96,32},{128,192},{160,224},{192,128},{224,1... | collective-permute-start | bytes 786440 | tf_op jit(solution)/shard_map/ppermute | solution.py:311
  89.9 15.3 %collective-permute-start.6 = (bf16[256,512]{1,0:T(8,128)(2,1)S(1)}, bf16[256,512]{1,0:T(8,128)(2,1)S(1)}, u32[]{:S(2)}, u32[]{:S(2)}) collective-permute-start(bf16[256,512]{1,0:T(8,128)(2,1)S(1)} %get-tuple-element.29.refs_0_), channel_id=1, source_target_pairs={{0,32},{32,64},{64,96},{96,0},{128,160},{160,192},{192,224},{224,1... | collective-permute-start | bytes 786440 | tf_op jit(solution)/shard_map/ppermute | solution.py:311
  90.6 20.1 %collective-permute-start.12 = (bf16[256,512]{1,0:T(8,128)(2,1)S(1)}, bf16[256,512]{1,0:T(8,128)(2,1)S(1)}, u32[]{:S(2)}, u32[]{:S(2)}) collective-permute-start(bf16[256,512]{1,0:T(8,128)(2,1)S(1)} %get-tuple-element.30.refs_0_), channel_id=1, source_target_pairs={{0,96},{32,0},{64,32},{96,64},{128,224},{160,128},{192,160},{224,1... | collective-permute-start | bytes 786440 | tf_op jit(solution)/shard_map/ppermute | solution.py:311
  93.1 17.7 %collective-permute-start.11 = (bf16[256,512]{1,0:T(8,128)(2,1)S(1)}, bf16[256,512]{1,0:T(8,128)(2,1)S(1)}, u32[]{:S(2)}, u32[]{:S(2)}) collective-permute-start(bf16[256,512]{1,0:T(8,128)(2,1)S(1)} %get-tuple-element.30.refs_0_), channel_id=1, source_target_pairs={{0,64},{32,96},{64,0},{96,32},{128,192},{160,224},{192,128},{224,1... | collective-permute-start | bytes 786440 | tf_op jit(solution)/shard_map/ppermute | solution.py:311
  101.0 13.3 %collective-permute-start.10 = (bf16[256,512]{1,0:T(8,128)(2,1)S(1)}, bf16[256,512]{1,0:T(8,128)(2,1)S(1)}, u32[]{:S(2)}, u32[]{:S(2)}) collective-permute-start(bf16[256,512]{1,0:T(8,128)(2,1)S(1)} %get-tuple-element.30.refs_0_), channel_id=1, source_target_pairs={{0,32},{32,64},{64,96},{96,0},{128,160},{160,192},{192,224},{224,1... | collective-permute-start | bytes 786440 | tf_op jit(solution)/shard_map/ppermute | solution.py:311
  105.9 11.9 %collective-permute-start.9 = (bf16[256,512]{1,0:T(8,128)(2,1)S(1)}, bf16[256,512]{1,0:T(8,128)(2,1)S(1)}, u32[]{:S(2)}, u32[]{:S(2)}) collective-permute-start(bf16[256,512]{1,0:T(8,128)(2,1)S(1)} %project.5), channel_id=1, source_target_pairs={{0,128},{32,160},{64,192},{96,224},{128,0},{160,32},{192,64},{224,... | collective-permute-start | bytes 786440 | tf_op jit(solution)/shard_map/ppermute | solution.py:315
  115.0 8.2 %collective-permute-start.13 = (bf16[256,512]{1,0:T(8,128)(2,1)S(1)}, bf16[256,512]{1,0:T(8,128)(2,1)S(1)}, u32[]{:S(2)}, u32[]{:S(2)}) collective-permute-start(bf16[256,512]{1,0:T(8,128)(2,1)S(1)} %project.7), channel_id=1, source_target_pairs={{0,128},{32,160},{64,192},{96,224},{128,0},{160,32},{192,64},{224,... | collective-permute-start | bytes 786440 | tf_op jit(solution)/shard_map/ppermute | solution.py:315

commit v3 on v2

v3 whole, which is shorter than its diff:
```python
import functools

import jax
import jax.numpy as jnp
import numpy as np
from jax import lax
from jax.experimental import pallas as pl
from jax.experimental.pallas import tpu as pltpu
from jax.sharding import PartitionSpec as P

EDGE = 128
WIDE = 48 * 1024 * 1024
ALONG_X = 4
FIRST_SLABS = 2
BATCH = 8


def split_table(table):
    high = table.astype(jnp.bfloat16)
    low = (table - high.astype(np.float64)).astype(jnp.bfloat16)
    return high, low


@functools.cache
def transform_tables():
    steps = np.arange(EDGE)
    slow = 2.0 * np.pi * np.outer(steps + 0.25, steps) / EDGE
    fast = 2.0 * np.pi * np.outer(steps, steps) / EDGE
    turn = 2.0 * np.pi * np.outer(steps + 0.25, steps) / (EDGE * EDGE)
    first = np.concatenate([np.cos(slow), -np.sin(slow)], 0)
    second = np.block([[np.cos(fast), -np.sin(fast)], [np.sin(fast), np.cos(fast)]])
    third = np.block([[np.cos(fast), np.sin(fast)], [-np.sin(fast), np.cos(fast)]]) / EDGE
    last = np.concatenate([np.cos(slow).T, -np.sin(slow).T], 1) / EDGE
    first_high, first_low = split_table(first)
    stacked = [np.concatenate([first_high, first_low], 1)]
    for table in (second, third):
        stacked.extend(split_table(table))
    return (
        np.concatenate(stacked, 0),
        np.concatenate(split_table(last), 1),
        np.stack([np.cos(turn), np.sin(turn)]).astype(np.float32),
    )


def thirds(array, axis):
    high = array.astype(jnp.bfloat16)
    low = (array - high.astype(jnp.float32)).astype(jnp.bfloat16)
    return jnp.concatenate([high, low, high], axis=axis)


def dot(a, b):
    return jnp.dot(a, b, preferred_element_type=jnp.float32)


def pack_kernel(value_hbm, gate_hbm, filt_hbm, out_ref, held, arrived):
    slabs, _, chans, _ = out_ref.shape[1:]
    arrays = (value_hbm, gate_hbm, filt_hbm)

    def fetch(which, slab):
        rows = pl.ds(slab * EDGE, EDGE)
        return pltpu.make_async_copy(
            arrays[which].at[rows, :], held.at[which, rows, :], arrived.at[which, slab]
        )

    for slab in range(slabs):
        for which in range(3):
            fetch(which, slab).start()
    peers = EDGE // chans
    for slab in range(slabs):
        rows = slice(slab * EDGE, (slab + 1) * EDGE)
        for which in range(3):
            fetch(which, slab).wait()
        gated = held[0, rows].astype(jnp.float32) * held[1, rows].astype(jnp.float32)
        gated = gated.astype(jnp.bfloat16)
        for which, array in enumerate((gated, held[2, rows])):
            for part in range(array.shape[1] // EDGE):
                turned = array[:, part * EDGE : (part + 1) * EDGE].T
                out_ref[part * peers : (part + 1) * peers, slab, which] = turned.reshape(
                    peers, chans, EDGE
                )


def copy_all(copies):
    for copy in copies:
        copy.start()
    for copy in copies:
        copy.wait()


def deal_kernel(place, w_hbm, *rest):
    pieces, done = rest[:-1], rest[-1]
    copies = []
    for i, piece in enumerate(pieces):
        _, height, width = piece.shape
        target = lax.rem(place[0] + i + 1, ALONG_X)
        for side in range(2):
            col = (lax.rem(place[1] + side, 2) * ALONG_X + target) * width
            block = w_hbm.at[:, pl.ds(pl.multiple_of(col, width), width)]
            copies.append(pltpu.make_async_copy(block, piece.at[side], done.at[i, side]))
    for copy in copies:
        copy.start()
    for copy in copies:
        copy.wait()


def conv_kernel(chans, in_ref, tables, last, turns, out_ref, wide, back):
    wide[...] = in_ref[...].astype(jnp.float32)
    cos, sin = turns[0], turns[1]

    def three(index):
        high = tables[2 * EDGE * index : 2 * EDGE * (index + 1), :]
        low = tables[2 * EDGE * (index + 1) : 2 * EDGE * (index + 2), :]
        return jnp.concatenate([high, high, low], axis=0)

    def last_three():
        high, low = last[:, : 2 * EDGE], last[:, 2 * EDGE :]
        return jnp.concatenate([high, high, low], axis=1)


    @pl.loop(0, chans // BATCH)
    def _(step):
        first = step * BATCH
        signals = [
            wide[pl.ds(which * chans + first + k, EDGE, stride=2 * chans), :].astype(jnp.bfloat16)
            for k in range(BATCH)
            for which in range(2)
        ]
        both = jnp.concatenate(signals, axis=1)
        slow = dot(tables[: 2 * EDGE, :], jnp.concatenate([both, both], axis=0))
        rows = []
        for k in range(2 * BATCH):
            cols = slice(k * EDGE, (k + 1) * EDGE)
            real, imag = slow[:EDGE, cols], slow[EDGE:, cols]
            rows.append(
                jnp.concatenate([real * cos + imag * sin, imag * cos - real * sin], axis=1)
            )
        spectra = dot(thirds(jnp.concatenate(rows, axis=0), 1), three(1))
        rows = []
        for k in range(BATCH):
            ours = spectra[2 * k * EDGE : (2 * k + 1) * EDGE]
            taps = spectra[(2 * k + 1) * EDGE : (2 * k + 2) * EDGE]
            ar, ai, br, bi = ours[:, :EDGE], ours[:, EDGE:], taps[:, :EDGE], taps[:, EDGE:]
            rows.append(jnp.concatenate([ar * br - ai * bi, ar * bi + ai * br], axis=1))
        wound = dot(thirds(jnp.concatenate(rows, axis=0), 1), three(3))
        cols = []
        for k in range(BATCH):
            real = wound[k * EDGE : (k + 1) * EDGE, :EDGE]
            imag = wound[k * EDGE : (k + 1) * EDGE, EDGE:]
            cols.append(
                jnp.concatenate([real * cos - imag * sin, imag * cos + real * sin], axis=0)
            )
        conv = dot(last_three(), thirds(jnp.concatenate(cols, axis=1), 0))
        for k in range(BATCH):
            back[pl.ds(first + k, EDGE, stride=chans), :] = conv[:, k * EDGE : (k + 1) * EDGE]

    out_ref[...] = back[...].astype(jnp.bfloat16)


def mix_kernel(conv_ref, value_ref, gate_ref, gate_out_ref, skip_ref, *outs):
    slabs, chans = conv_ref.shape[1:3]
    width = value_ref.shape[1]
    peers = EDGE // chans
    for slab in range(slabs):
        rows = slice(slab * EDGE, (slab + 1) * EDGE)
        out_ref, first = outs[0], slab
        if slab >= FIRST_SLABS:
            out_ref, first = outs[1], slab - FIRST_SLABS
        out_rows = slice(first * EDGE, (first + 1) * EDGE)
        for part in range(width // EDGE):
            cols = slice(part * EDGE, (part + 1) * EDGE)
            conv = conv_ref[part * peers : (part + 1) * peers, slab].reshape(EDGE, EDGE).T
            gated = gate_ref[rows, cols].astype(jnp.float32) * value_ref[rows, cols].astype(
                jnp.float32
            )
            gated = gated.astype(jnp.bfloat16).astype(jnp.float32)
            inner = conv.astype(jnp.float32) + skip_ref[:, cols] * gated
            mixed = gate_out_ref[rows, cols].astype(jnp.float32) * inner
            out_ref[out_rows, cols] = mixed.astype(jnp.bfloat16)


def project_kernel(n_parts, *refs):
    parts, weights, out_ref = refs[:n_parts], refs[n_parts:-1], refs[-1]

    def product(part, shift):
        return dot(part[...], weights[shift][0])

    total = product(parts[0], 0) + product(parts[1], 1) + product(parts[-1], ALONG_X - 1)
    across = jnp.concatenate([product(part, 2) for part in parts[2:-1]], axis=0)
    out_ref[...] = (total + across).astype(out_ref.dtype)


def pack(value, gate_in, filt, groups):
    rows, width = value.shape
    slabs, chans = rows // EDGE, width // groups
    return pl.pallas_call(
        pack_kernel,
        in_specs=[pl.BlockSpec(memory_space=pl.ANY)] * 3,
        out_specs=pl.BlockSpec(memory_space=pltpu.VMEM),
        out_shape=jax.ShapeDtypeStruct((groups, slabs, 2, chans, EDGE), jnp.bfloat16),
        scratch_shapes=[
            pltpu.VMEM((3, rows, width), jnp.bfloat16),
            pltpu.SemaphoreType.DMA((3, slabs)),
        ],
        name="pack",
    )(value, gate_in, filt)


def deal(w_out, place, width):
    shape = jax.ShapeDtypeStruct((2, w_out.shape[0], width), jnp.bfloat16)
    return pl.pallas_call(
        deal_kernel,
        in_specs=[pl.BlockSpec(memory_space=pltpu.SMEM), pl.BlockSpec(memory_space=pl.ANY)],
        out_specs=[pl.BlockSpec(memory_space=pltpu.VMEM)] * ALONG_X,
        out_shape=[shape] * ALONG_X,
        scratch_shapes=[pltpu.SemaphoreType.DMA((ALONG_X, 2))],
        compiler_params=pltpu.CompilerParams(vmem_limit_bytes=WIDE),
        name="deal",
    )(place, w_out)


def convolve(spread, tables):
    groups, slabs, _, chans, _ = spread.shape
    rows = groups * slabs * chans
    whole = pl.BlockSpec(memory_space=pltpu.VMEM)
    conv = pl.pallas_call(
        functools.partial(conv_kernel, chans),
        in_specs=[whole] * (1 + len(tables)),
        out_specs=whole,
        out_shape=jax.ShapeDtypeStruct((rows, EDGE), jnp.bfloat16),
        scratch_shapes=[
            pltpu.VMEM((2 * rows, EDGE), jnp.float32),
            pltpu.VMEM((rows, EDGE), jnp.float32),
        ],
        compiler_params=pltpu.CompilerParams(vmem_limit_bytes=WIDE),
        cost_estimate=pl.CostEstimate(
            flops=6 * 10**9, bytes_accessed=2 * 10**6, transcendentals=0
        ),
        name="convolve",
    )(spread.reshape(2 * rows, EDGE), *tables)
    return conv.reshape(groups, slabs, chans, EDGE)


def mix(conv, value, gate_in, gate_out, skip):
    rows, width = value.shape
    first = FIRST_SLABS * EDGE
    whole = pl.BlockSpec(memory_space=pltpu.VMEM)
    return pl.pallas_call(
        mix_kernel,
        in_specs=[whole] * 5,
        out_specs=[whole] * 2,
        out_shape=[
            jax.ShapeDtypeStruct((count, width), jnp.bfloat16) for count in (first, rows - first)
        ],
        compiler_params=pltpu.CompilerParams(vmem_limit_bytes=WIDE),
        name="mix",
    )(conv, value, gate_in, gate_out, skip)


def project_half(parts, weights, side, dtype):
    rows, width = parts[0].shape
    return pl.pallas_call(
        functools.partial(project_kernel, len(parts)),
        grid=(1,),
        in_specs=[pl.BlockSpec(part.shape, lambda i: (0, 0)) for part in parts]
        + [pl.BlockSpec((1, *weight.shape[1:]), lambda i: (side, 0, 0)) for weight in weights],
        out_specs=pl.BlockSpec((rows, width), lambda i: (0, 0)),
        out_shape=jax.ShapeDtypeStruct((rows, width), dtype),
        compiler_params=pltpu.CompilerParams(vmem_limit_bytes=WIDE),
        cost_estimate=pl.CostEstimate(
            flops=2 * rows * ALONG_X * width * width, bytes_accessed=3 * 10**6, transcendentals=0
        ),
        name="project",
    )(*parts, *weights)


def along_x(shift):
    return [
        (i, i // ALONG_X * ALONG_X + (i + shift) % ALONG_X) for i in range(2 * ALONG_X)
    ]


def across_y():
    return [(i, (i + ALONG_X) % (2 * ALONG_X)) for i in range(2 * ALONG_X)]


def gather_x(own):
    def send(rows, shift):
        return lax.ppermute(rows, "chan", along_x(shift))

    before, after = send(own, 1), send(own, ALONG_X - 1)
    half = own.shape[0] // 2
    return [own, before, send(before[:half], 1), send(after[half:], ALONG_X - 1), after]


def per_device(value, gate_in, gate_out, filt, skip, w_out):
    groups = lax.axis_size("ctx")
    place = lax.axis_index("chan")
    where = jnp.stack([lax.rem(place, ALONG_X), lax.div(place, ALONG_X)])
    packed = pack(value, gate_in, filt, groups)
    *pieces, own = deal(w_out, where, value.shape[1])
    pieces = [lax.ppermute(piece, "chan", along_x(i + 1)) for i, piece in enumerate(pieces)]
    spread = lax.all_to_all(packed, "ctx", split_axis=0, concat_axis=0, tiled=True)
    tables = [jnp.asarray(table) for table in transform_tables()]
    conv = convolve(spread, tables)
    returned = lax.all_to_all(conv, "ctx", split_axis=0, concat_axis=0, tiled=True)
    mixed = mix(returned, value, gate_in, gate_out, skip[None])
    mixed, pieces = lax.optimization_barrier((mixed, pieces))
    weights = [own, *pieces]
    parts = [gather_x(rows) for rows in mixed]
    theirs, outs = [], []
    for part in parts:
        share = project_half(part, weights, 1, jnp.bfloat16)
        theirs.append(lax.ppermute(share, "chan", across_y()))
    for part, arrived in zip(parts, theirs):
        mine = project_half(part, weights, 0, jnp.float32)
        outs.append((mine + arrived.astype(jnp.float32)).astype(jnp.bfloat16))
    return jnp.concatenate(outs, axis=0)


def solution(mesh):
    placed = (
        P("ctx", "chan"),
        P("ctx", "chan"),
        P("ctx", "chan"),
        P("ctx", "chan"),
        P("chan"),
        P("chan", None),
    )
    return jax.shard_map(
        per_device, mesh=mesh, in_specs=placed, out_specs=P("ctx", "chan"), check_vma=False
    )
```

time: 125 us -> 111 us (0.89)
  waiting for transfers between devices: 44.1 us -> 28.8 us
  blocking collectives: 27.3 us -> 22.5 us
  starting transfers between devices: 29.5 us -> 34.1 us
  Pallas kernels: 18.8 us -> 23.3 us
  local copies, waits for them, and re-layouts: 3.19 us -> 1.15 us
    ppermute x3, waiting for transfers between devices: 21.8 us -> 0.01 us  [per_device(): lax.ppermute(piece, 'chan', along_x(i + 1))]
    all_to_all x1, waiting for transfers between devices: 0.01 us -> 18.7 us  [per_device(): lax.all_to_all(packed, 'ctx', split_axis=0, concat_axis=0, tiled=True)]
    ppermute x11 -> x10, waiting for transfers between devices: 22.3 us -> 10.1 us  [the longest x8 7.75 us: send(): return lax.ppermute(rows, 'chan', along_x(shift))]
    all_to_all x1, blocking collectives: 27.3 us -> 22.5 us  [per_device(): lax.all_to_all(conv, 'ctx', split_axis=0, concat_axis=0, tiled=True)]
    ppermute x11 -> x10, starting transfers between devices: 12.1 us -> 16.7 us  [the longest x8 14 us: send(): return lax.ppermute(rows, 'chan', along_x(shift))]
    pallas_call x5, Pallas kernels: 4 us -> 7.36 us  [the longest x4 6.96 us: project_half(): pl.pallas_call(functools.partial(project_kernel, len(parts)), grid=(1,),...]
    pallas_call x1, Pallas kernels: 2.32 us -> 4.45 us  [deal(): pl.pallas_call(deal_kernel, in_specs=[pl.BlockSpec(memory_space=pltpu.SME...]
    unnamed x18 -> x14, local copies, waits for them, and re-layouts: 3.15 us -> 1.11 us
  transfers between devices with their start and end apart: 15 -> 14, of which waited for: 8 -> 6; matrix products, arithmetic and copies ran while one was open for 0% -> 0% of each run, Pallas kernels for 11% -> 19%
where the time goes in v3:
time: 111 us
  starting transfers between devices  34.1 us (31%)
  waiting for transfers between devices  28.8 us (26%)
  Pallas kernels  23.3 us (21%)
  blocking collectives  22.5 us (20%)
  local copies, waits for them, and re-layouts  1.15 us (1%)
    all_to_all x1, blocking collectives, per_device(): lax.all_to_all(conv, 'ctx', split_axis=0, concat_axis=0, tiled=True)  22.5 us
    all_to_all x1, waiting for transfers between devices, per_device(): lax.all_to_all(packed, 'ctx', split_axis=0, concat_axis=0, tiled=True)  18.7 us
    ppermute x8, starting transfers between devices, send(): return lax.ppermute(rows, 'chan', along_x(shift))  14 us
    all_to_all x1, starting transfers between devices, per_device(): lax.all_to_all(packed, 'ctx', split_axis=0, concat_axis=0, tiled=True)  11.7 us
    pallas_call x1, Pallas kernels, convolve(): pl.pallas_call(functools.partial(conv_kernel, chans), in_specs=[whole] *...  8.75 us
    ppermute x8, waiting for transfers between devices, send(): return lax.ppermute(rows, 'chan', along_x(shift))  7.75 us
    pallas_call x4, Pallas kernels, project_half(): pl.pallas_call(functools.partial(project_kernel, len(parts)), grid=(1,),...  6.96 us
    ppermute x3, starting transfers between devices, per_device(): lax.ppermute(piece, 'chan', along_x(i + 1))  5.73 us
  transfers between devices with their start and end apart: 14, of which 6 were waited for; matrix products, arithmetic and copies ran while one was open for 0% of the time, Pallas kernels for 19%

profile of v3, /device:TPU:16, one launch (start us, length us, event | category | flops | bytes accessed | tf_op | source)
XLA Modules:
  0.0 111.0 jit_solution(12699850079443385634)
XLA Ops:
  0.0 0.0 copy-start.5
  0.0 0.0 copy-start.6
  0.0 2.7 %pack.1 = bf16[32,4,2,16,128]{4,3,2,1,0:T(8,128)(2,1)} custom-call(bf16[512,512]{1,0:T(8,128)(2,1)} %value_ref.1, bf16[512,512]{1,0:T(8,128)(2,1)} %gate_ref.1, bf16[512,512]{1,0:T(8,128)(2,1)} %filt_hbm.1), custom_call_target="tpu_custom_call" | custom-call | tf_op jit(solution)/shard_map/pack/pallas_call | solution.py:195
  2.7 11.7 %all-to-all-start = ((bf16[32,4,2,16,128]{4,3,2,1,0:T(8,128)(2,1)}), bf16[32,4,2,16,128]{4,3,2,1,0:T(8,128)(2,1)}, u32[]{:S(2)}, u32[]{:S(2)}) async-start(bf16[32,4,2,16,128]{4,3,2,1,0:T(8,128)(2,1)} %pack.1), calls=%async_computation | async-start | bytes 2097152 | tf_op jit(solution)/shard_map/all_to_all | solution.py:302
  14.4 0.1 pad_add_fusion.place
  14.4 4.5 %deal.1 = (bf16[2,512,512]{2,1,0:T(8,128)(2,1)}, bf16[2,512,512]{2,1,0:T(8,128)(2,1)}, bf16[2,512,512]{2,1,0:T(8,128)(2,1)}, bf16[2,512,512]{2,1,0:T(8,128)(2,1)S(1)}) custom-call(s32[2]{0:T(128)S(1)} %pad_add_fusion.place, bf16[512,4096]{1,0:T(8,128)(2,1)} %w_hbm.1), custom_call_target="tpu_custom_call" | custom-call | tf_op jit(solution)/shard_map/deal/pallas_call | solution.py:210
  18.9 1.6 %collective-permute-start = (bf16[2,512,512]{2,1,0:T(8,128)(2,1)}, bf16[2,512,512]{2,1,0:T(8,128)(2,1)S(1)}, u32[]{:S(2)}, u32[]{:S(2)}) collective-permute-start(bf16[2,512,512]{2,1,0:T(8,128)(2,1)} %get-tuple-element.18), channel_id=1, source_target_pairs={{0,32},{32,64},{64,96},{96,0},{128,160},{160,192},{192,224},{224,1... | collective-permute-start | bytes 3145736 | tf_op jit(solution)/shard_map/ppermute | solution.py:301
  20.5 2.7 %collective-permute-start.1 = (bf16[2,512,512]{2,1,0:T(8,128)(2,1)}, bf16[2,512,512]{2,1,0:T(8,128)(2,1)S(1)}, u32[]{:S(2)}, u32[]{:S(2)}) collective-permute-start(bf16[2,512,512]{2,1,0:T(8,128)(2,1)} %get-tuple-element.19), channel_id=1, source_target_pairs={{0,64},{32,96},{64,0},{96,32},{128,192},{160,224},{192,128},{224,1... | collective-permute-start | bytes 3145736 | tf_op jit(solution)/shard_map/ppermute | solution.py:301
  23.2 1.4 %collective-permute-start.2 = (bf16[2,512,512]{2,1,0:T(8,128)(2,1)}, bf16[2,512,512]{2,1,0:T(8,128)(2,1)}, u32[]{:S(2)}, u32[]{:S(2)}) collective-permute-start(bf16[2,512,512]{2,1,0:T(8,128)(2,1)} %get-tuple-element.20), channel_id=1, source_target_pairs={{0,96},{32,0},{64,32},{96,64},{128,224},{160,128},{192,160},{224,1... | collective-permute-start | bytes 3145736 | tf_op jit(solution)/shard_map/ppermute | solution.py:301
  24.6 18.7 %all-to-all-done = bf16[32,4,2,16,128]{4,3,2,1,0:T(8,128)(2,1)} async-done(((bf16[32,4,2,16,128]{4,3,2,1,0:T(8,128)(2,1)}), bf16[32,4,2,16,128]{4,3,2,1,0:T(8,128)(2,1)}, u32[]{:S(2)}, u32[]{:S(2)}) %all-to-all-start) | async-done | bytes 1048608 | tf_op jit(solution)/shard_map/all_to_all | solution.py:302
  43.4 0.0 copy-done.5
  43.4 0.0 copy-done.6
  43.4 0.0 copy-start.4
  43.4 1.1 copy-done.4
  44.5 0.0 copy-start
  44.5 0.0 copy-start.1
  44.5 0.0 copy-start.2
  44.5 0.0 copy-start.3
  44.5 8.7 %convolve.1 = bf16[2048,128]{1,0:T(8,128)(2,1)S(1)} custom-call(bf16[4096,128]{1,0:T(8,128)(2,1)} %bitcast.in_ref, bf16[1280,256]{1,0:T(8,128)(2,1)S(1)} %copy-done.4, bf16[128,512]{1,0:T(8,128)(2,1)S(1)} %copy-done.6, f32[2,128,128]{2,1,0:T(8,128)S(1)} %copy-done.5), custom_call_target="tpu_custom_call" | custom-call | flops 6000000000 | bytes 2000000 | tf_op jit(solution)/shard_map/convolve/pallas_call | solution.py:225
  53.2 22.5 %all_to_all.10.conv_ref = bf16[32,4,16,128]{3,2,1,0:T(8,128)(2,1)S(1)} all-to-all(bf16[32,4,16,128]{3,2,1,0:T(8,128)(2,1)S(1)} %bitcast.5), channel_id=1, replica_groups=mesh['chan'=8,'ctx'=32] {'ctx'}, dimensions={0} | all-to-all | bytes 1048576 | tf_op jit(solution)/shard_map/all_to_all | solution.py:305
  75.7 0.0 copy-done
  75.7 0.0 copy-done.1
  75.7 0.0 copy-done.2
  75.7 0.0 copy-done.3
  75.7 0.4 mix.1
  76.1 0.0 collective-permute-done.refs_6_
  76.1 0.0 collective-permute-done.1.refs_7_
  76.2 0.0 collective-permute-done.2.refs_8_
  76.2 2.8 %collective-permute-start.5 = (bf16[256,512]{1,0:T(8,128)(2,1)S(1)}, bf16[256,512]{1,0:T(8,128)(2,1)S(1)}, u32[]{:S(2)}, u32[]{:S(2)}) collective-permute-start(bf16[256,512]{1,0:T(8,128)(2,1)S(1)} %get-tuple-element.21.refs_0_), channel_id=1, source_target_pairs={{0,96},{32,0},{64,32},{96,64},{128,224},{160,128},{192,160},{224,1... | collective-permute-start | bytes 786440 | tf_op jit(solution)/shard_map/ppermute | solution.py:288
  79.0 0.0 collective-permute-start.3
  79.0 3.2 %collective-permute-start.10 = (bf16[256,512]{1,0:T(8,128)(2,1)S(1)}, bf16[256,512]{1,0:T(8,128)(2,1)S(1)}, u32[]{:S(2)}, u32[]{:S(2)}) collective-permute-start(bf16[256,512]{1,0:T(8,128)(2,1)S(1)} %get-tuple-element.26.refs_0_), channel_id=1, source_target_pairs={{0,96},{32,0},{64,32},{96,64},{128,224},{160,128},{192,160},{224,1... | collective-permute-start | bytes 786440 | tf_op jit(solution)/shard_map/ppermute | solution.py:288
  82.2 0.0 collective-permute-start.8
  82.2 3.5 %collective-permute-done.5.refs_4_ = bf16[256,512]{1,0:T(8,128)(2,1)S(1)} collective-permute-done((bf16[256,512]{1,0:T(8,128)(2,1)S(1)}, bf16[256,512]{1,0:T(8,128)(2,1)S(1)}, u32[]{:S(2)}, u32[]{:S(2)}) %collective-permute-start.5) | collective-permute-done | bytes 262176 | tf_op jit(solution)/shard_map/ppermute | solution.py:288
  85.8 3.8 %collective-permute-start.6 = (bf16[128,512]{1,0:T(8,128)(2,1)S(1)}, bf16[128,512]{1,0:T(8,128)(2,1)S(1)}, u32[]{:S(2)}, u32[]{:S(2)}) collective-permute-start(bf16[128,512]{1,0:T(8,128)(2,1)S(1)} %slice.17), channel_id=1, source_target_pairs={{0,96},{32,0},{64,32},{96,64},{128,224},{160,128},{192,160},{224,1... | collective-permute-start | bytes 393224 | tf_op jit(solution)/shard_map/ppermute | solution.py:288
  89.5 0.0 collective-permute-done.3.refs_1_
  89.6 0.3 collective-permute-start.4
  89.8 1.2 %collective-permute-done.10.refs_4_ = bf16[256,512]{1,0:T(8,128)(2,1)S(1)} collective-permute-done((bf16[256,512]{1,0:T(8,128)(2,1)S(1)}, bf16[256,512]{1,0:T(8,128)(2,1)S(1)}, u32[]{:S(2)}, u32[]{:S(2)}) %collective-permute-start.10) | collective-permute-done | bytes 262176 | tf_op jit(solution)/shard_map/ppermute | solution.py:288
  91.0 3.8 %collective-permute-start.11 = (bf16[128,512]{1,0:T(8,128)(2,1)S(1)}, bf16[128,512]{1,0:T(8,128)(2,1)S(1)}, u32[]{:S(2)}, u32[]{:S(2)}) collective-permute-start(bf16[128,512]{1,0:T(8,128)(2,1)S(1)} %slice.19), channel_id=1, source_target_pairs={{0,96},{32,0},{64,32},{96,64},{128,224},{160,128},{192,160},{224,1... | collective-permute-start | bytes 393224 | tf_op jit(solution)/shard_map/ppermute | solution.py:288
  94.8 0.0 collective-permute-done.8.refs_1_
  94.8 0.1 collective-permute-start.9
  94.9 0.0 collective-permute-done.6.refs_3_
  94.9 1.7 %collective-permute-done.4.refs_2_ = bf16[128,512]{1,0:T(8,128)(2,1)S(1)} collective-permute-done((bf16[128,512]{1,0:T(8,128)(2,1)S(1)}, bf16[128,512]{1,0:T(8,128)(2,1)S(1)}, u32[]{:S(2)}, u32[]{:S(2)}) %collective-permute-start.4) | collective-permute-done | bytes 131104 | tf_op jit(solution)/shard_map/ppermute | solution.py:288
  96.7 1.7 %project.5 = bf16[256,512]{1,0:T(8,128)(2,1)S(1)} custom-call(bf16[256,512]{1,0:T(8,128)(2,1)S(1)} %get-tuple-element.21.refs_0_, bf16[256,512]{1,0:T(8,128)(2,1)S(1)} %collective-permute-done.3.refs_1_, bf16[128,512]{1,0:T(8,128)(2,1)S(1)} %collective-permute-done.4.refs_2_, bf16[128,512]{1,0:T(8,128)(2,1)S(1)} %collective-permute-done.6.refs_3_, ...), custom_call_target="tpu_custom_call" | custom-call | flops 536870912 | bytes 3000000 | tf_op jit(solution)/shard_map/project/pallas_call | solution.py:261
  98.4 1.4 %collective-permute-start.7 = (bf16[256,512]{1,0:T(8,128)(2,1)S(1)}, bf16[256,512]{1,0:T(8,128)(2,1)S(1)}, u32[]{:S(2)}, u32[]{:S(2)}) collective-permute-start(bf16[256,512]{1,0:T(8,128)(2,1)S(1)} %project.5), channel_id=1, source_target_pairs={{0,128},{32,160},{64,192},{96,224},{128,0},{160,32},{192,64},{224,... | collective-permute-start | bytes 786440 | tf_op jit(solution)/shard_map/ppermute | solution.py:313
  99.8 0.0 collective-permute-done.11.refs_3_
  99.8 1.3 %collective-permute-done.9.refs_2_ = bf16[128,512]{1,0:T(8,128)(2,1)S(1)} collective-permute-done((bf16[128,512]{1,0:T(8,128)(2,1)S(1)}, bf16[128,512]{1,0:T(8,128)(2,1)S(1)}, u32[]{:S(2)}, u32[]{:S(2)}) %collective-permute-start.9) | collective-permute-done | bytes 131104 | tf_op jit(solution)/shard_map/ppermute | solution.py:288
  101.1 1.7 %project.7 = bf16[256,512]{1,0:T(8,128)(2,1)S(1)} custom-call(bf16[256,512]{1,0:T(8,128)(2,1)S(1)} %get-tuple-element.26.refs_0_, bf16[256,512]{1,0:T(8,128)(2,1)S(1)} %collective-permute-done.8.refs_1_, bf16[128,512]{1,0:T(8,128)(2,1)S(1)} %collective-permute-done.9.refs_2_, bf16[128,512]{1,0:T(8,128)(2,1)S(1)} %collective-permute-done.11.refs_3_, ...), custom_call_target="tpu_custom_call" | custom-call | flops 536870912 | bytes 3000000 | tf_op jit(solution)/shard_map/project/pallas_call | solution.py:261
  102.8 1.4 %collective-permute-start.12 = (bf16[256,512]{1,0:T(8,128)(2,1)S(1)}, bf16[256,512]{1,0:T(8,128)(2,1)S(1)}, u32[]{:S(2)}, u32[]{:S(2)}) collective-permute-start(bf16[256,512]{1,0:T(8,128)(2,1)S(1)} %project.7), channel_id=1, source_target_pairs={{0,128},{32,160},{64,192},{96,224},{128,0},{160,32},{192,64},{224,... | collective-permute-start | bytes 786440 | tf_op jit(solution)/shard_map/ppermute | solution.py:313
  104.2 1.7 %project.4 = f32[256,512]{1,0:T(8,128)S(1)} custom-call(bf16[256,512]{1,0:T(8,128)(2,1)S(1)} %get-tuple-element.21.refs_0_, bf16[256,512]{1,0:T(8,128)(2,1)S(1)} %collective-permute-done.3.refs_1_, bf16[128,512]{1,0:T(8,128)(2,1)S(1)} %collective-permute-done.4.refs_2_, bf16[128,512]{1,0:T(8,128)(2,1)S(1)} %collective-permute-done.6.refs_3_, ...), custom_call_target="tpu_custom_call" | custom-call | flops 536870912 | bytes 3000000 | tf_op jit(solution)/shard_map/project/pallas_call | solution.py:261
  105.9 1.7 %project.6 = f32[256,512]{1,0:T(8,128)S(1)} custom-call(bf16[256,512]{1,0:T(8,128)(2,1)S(1)} %get-tuple-element.26.refs_0_, bf16[256,512]{1,0:T(8,128)(2,1)S(1)} %collective-permute-done.8.refs_1_, bf16[128,512]{1,0:T(8,128)(2,1)S(1)} %collective-permute-done.9.refs_2_, bf16[128,512]{1,0:T(8,128)(2,1)S(1)} %collective-permute-done.11.refs_3_, ...), custom_call_target="tpu_custom_call" | custom-call | flops 536870912 | bytes 3000000 | tf_op jit(solution)/shard_map/project/pallas_call | solution.py:261
  107.7 0.0 collective-permute-done.7
  107.7 0.1 add_convert_fusion.1
  107.8 2.3 %collective-permute-done.12 = bf16[256,512]{1,0:T(8,128)(2,1)S(1)} collective-permute-done((bf16[256,512]{1,0:T(8,128)(2,1)S(1)}, bf16[256,512]{1,0:T(8,128)(2,1)S(1)}, u32[]{:S(2)}, u32[]{:S(2)}) %collective-permute-start.12) | collective-permute-done | bytes 262176 | tf_op jit(solution)/shard_map/ppermute | solution.py:313
  110.1 0.1 add_convert_fusion
  110.2 0.8 pad_maximum_fusion
  (4 shorter events, 0.0 us)
Async XLA Ops:
  0.0 43.4 %copy-start.5 = (f32[2,128,128]{2,1,0:T(8,128)S(1)}, f32[2,128,128]{2,1,0:T(8,128)}, u32[]{:S(2)}) copy-start(f32[2,128,128]{2,1,0:T(8,128)} %constant.22.clone.turns) | copy-start | bytes 393220
  0.0 43.4 %copy-start.6 = (bf16[128,512]{1,0:T(8,128)(2,1)S(1)}, bf16[128,512]{1,0:T(8,128)(2,1)}, u32[]{:S(2)}) copy-start(bf16[128,512]{1,0:T(8,128)(2,1)} %constant.21.clone.last) | copy-start | bytes 393220
  2.7 40.7 %all-to-all-start = ((bf16[32,4,2,16,128]{4,3,2,1,0:T(8,128)(2,1)}), bf16[32,4,2,16,128]{4,3,2,1,0:T(8,128)(2,1)}, u32[]{:S(2)}, u32[]{:S(2)}) async-start(bf16[32,4,2,16,128]{4,3,2,1,0:T(8,128)(2,1)} %pack.1), calls=%async_computation | async-start | bytes 2097152 | tf_op jit(solution)/shard_map/all_to_all | solution.py:302
  18.9 57.2 %collective-permute-start = (bf16[2,512,512]{2,1,0:T(8,128)(2,1)}, bf16[2,512,512]{2,1,0:T(8,128)(2,1)S(1)}, u32[]{:S(2)}, u32[]{:S(2)}) collective-permute-start(bf16[2,512,512]{2,1,0:T(8,128)(2,1)} %get-tuple-element.18), channel_id=1, source_target_pairs={{0,32},{32,64},{64,96},{96,0},{128,160},{160,192},{192,224},{224,1... | collective-permute-start | bytes 3145736 | tf_op jit(solution)/shard_map/ppermute | solution.py:301
  20.5 55.7 %collective-permute-start.1 = (bf16[2,512,512]{2,1,0:T(8,128)(2,1)}, bf16[2,512,512]{2,1,0:T(8,128)(2,1)S(1)}, u32[]{:S(2)}, u32[]{:S(2)}) collective-permute-start(bf16[2,512,512]{2,1,0:T(8,128)(2,1)} %get-tuple-element.19), channel_id=1, source_target_pairs={{0,64},{32,96},{64,0},{96,32},{128,192},{160,224},{192,128},{224,1... | collective-permute-start | bytes 3145736 | tf_op jit(solution)/shard_map/ppermute | solution.py:301
  23.2 52.9 %collective-permute-start.2 = (bf16[2,512,512]{2,1,0:T(8,128)(2,1)}, bf16[2,512,512]{2,1,0:T(8,128)(2,1)}, u32[]{:S(2)}, u32[]{:S(2)}) collective-permute-start(bf16[2,512,512]{2,1,0:T(8,128)(2,1)} %get-tuple-element.20), channel_id=1, source_target_pairs={{0,96},{32,0},{64,32},{96,64},{128,224},{160,128},{192,160},{224,1... | collective-permute-start | bytes 3145736 | tf_op jit(solution)/shard_map/ppermute | solution.py:301
  43.4 1.1 copy-start.4
  44.5 31.3 %copy-start = (bf16[512,512]{1,0:T(8,128)(2,1)S(1)}, bf16[512,512]{1,0:T(8,128)(2,1)}, u32[]{:S(2)}) copy-start(bf16[512,512]{1,0:T(8,128)(2,1)} %value_ref.1) | copy-start | bytes 1572868
  44.5 31.3 %copy-start.1 = (bf16[512,512]{1,0:T(8,128)(2,1)S(1)}, bf16[512,512]{1,0:T(8,128)(2,1)}, u32[]{:S(2)}) copy-start(bf16[512,512]{1,0:T(8,128)(2,1)} %gate_ref.1) | copy-start | bytes 1572868
  44.5 31.3 %copy-start.2 = (bf16[512,512]{1,0:T(8,128)(2,1)S(1)}, bf16[512,512]{1,0:T(8,128)(2,1)}, u32[]{:S(2)}) copy-start(bf16[512,512]{1,0:T(8,128)(2,1)} %gate_out_ref.1) | copy-start | bytes 1572868
  44.5 31.3 %copy-start.3 = (f32[512]{0:T(512)S(1)}, f32[512]{0:T(512)}, u32[]{:S(2)}) copy-start(f32[512]{0:T(512)} %param.13) | copy-start | bytes 6148
  76.2 9.6 %collective-permute-start.5 = (bf16[256,512]{1,0:T(8,128)(2,1)S(1)}, bf16[256,512]{1,0:T(8,128)(2,1)S(1)}, u32[]{:S(2)}, u32[]{:S(2)}) collective-permute-start(bf16[256,512]{1,0:T(8,128)(2,1)S(1)} %get-tuple-element.21.refs_0_), channel_id=1, source_target_pairs={{0,96},{32,0},{64,32},{96,64},{128,224},{160,128},{192,160},{224,1... | collective-permute-start | bytes 786440 | tf_op jit(solution)/shard_map/ppermute | solution.py:288
  79.0 10.5 %collective-permute-start.3 = (bf16[256,512]{1,0:T(8,128)(2,1)S(1)}, bf16[256,512]{1,0:T(8,128)(2,1)S(1)}, u32[]{:S(2)}, u32[]{:S(2)}) collective-permute-start(bf16[256,512]{1,0:T(8,128)(2,1)S(1)} %get-tuple-element.21.refs_0_), channel_id=1, source_target_pairs={{0,32},{32,64},{64,96},{96,0},{128,160},{160,192},{192,224},{224,1... | collective-permute-start | bytes 786440 | tf_op jit(solution)/shard_map/ppermute | solution.py:288
  79.0 12.0 %collective-permute-start.10 = (bf16[256,512]{1,0:T(8,128)(2,1)S(1)}, bf16[256,512]{1,0:T(8,128)(2,1)S(1)}, u32[]{:S(2)}, u32[]{:S(2)}) collective-permute-start(bf16[256,512]{1,0:T(8,128)(2,1)S(1)} %get-tuple-element.26.refs_0_), channel_id=1, source_target_pairs={{0,96},{32,0},{64,32},{96,64},{128,224},{160,128},{192,160},{224,1... | collective-permute-start | bytes 786440 | tf_op jit(solution)/shard_map/ppermute | solution.py:288
  82.2 12.6 %collective-permute-start.8 = (bf16[256,512]{1,0:T(8,128)(2,1)S(1)}, bf16[256,512]{1,0:T(8,128)(2,1)S(1)}, u32[]{:S(2)}, u32[]{:S(2)}) collective-permute-start(bf16[256,512]{1,0:T(8,128)(2,1)S(1)} %get-tuple-element.26.refs_0_), channel_id=1, source_target_pairs={{0,32},{32,64},{64,96},{96,0},{128,160},{160,192},{192,224},{224,1... | collective-permute-start | bytes 786440 | tf_op jit(solution)/shard_map/ppermute | solution.py:288
  85.8 9.1 %collective-permute-start.6 = (bf16[128,512]{1,0:T(8,128)(2,1)S(1)}, bf16[128,512]{1,0:T(8,128)(2,1)S(1)}, u32[]{:S(2)}, u32[]{:S(2)}) collective-permute-start(bf16[128,512]{1,0:T(8,128)(2,1)S(1)} %slice.17), channel_id=1, source_target_pairs={{0,96},{32,0},{64,32},{96,64},{128,224},{160,128},{192,160},{224,1... | collective-permute-start | bytes 393224 | tf_op jit(solution)/shard_map/ppermute | solution.py:288
  89.6 7.1 %collective-permute-start.4 = (bf16[128,512]{1,0:T(8,128)(2,1)S(1)}, bf16[128,512]{1,0:T(8,128)(2,1)S(1)}, u32[]{:S(2)}, u32[]{:S(2)}) collective-permute-start(bf16[128,512]{1,0:T(8,128)(2,1)S(1)} %slice.16), channel_id=1, source_target_pairs={{0,32},{32,64},{64,96},{96,0},{128,160},{160,192},{192,224},{224,1... | collective-permute-start | bytes 393224 | tf_op jit(solution)/shard_map/ppermute | solution.py:288
  91.0 8.7 %collective-permute-start.11 = (bf16[128,512]{1,0:T(8,128)(2,1)S(1)}, bf16[128,512]{1,0:T(8,128)(2,1)S(1)}, u32[]{:S(2)}, u32[]{:S(2)}) collective-permute-start(bf16[128,512]{1,0:T(8,128)(2,1)S(1)} %slice.19), channel_id=1, source_target_pairs={{0,96},{32,0},{64,32},{96,64},{128,224},{160,128},{192,160},{224,1... | collective-permute-start | bytes 393224 | tf_op jit(solution)/shard_map/ppermute | solution.py:288
  94.8 6.3 %collective-permute-start.9 = (bf16[128,512]{1,0:T(8,128)(2,1)S(1)}, bf16[128,512]{1,0:T(8,128)(2,1)S(1)}, u32[]{:S(2)}, u32[]{:S(2)}) collective-permute-start(bf16[128,512]{1,0:T(8,128)(2,1)S(1)} %slice.18), channel_id=1, source_target_pairs={{0,32},{32,64},{64,96},{96,0},{128,160},{160,192},{192,224},{224,1... | collective-permute-start | bytes 393224 | tf_op jit(solution)/shard_map/ppermute | solution.py:288
  98.4 9.3 %collective-permute-start.7 = (bf16[256,512]{1,0:T(8,128)(2,1)S(1)}, bf16[256,512]{1,0:T(8,128)(2,1)S(1)}, u32[]{:S(2)}, u32[]{:S(2)}) collective-permute-start(bf16[256,512]{1,0:T(8,128)(2,1)S(1)} %project.5), channel_id=1, source_target_pairs={{0,128},{32,160},{64,192},{96,224},{128,0},{160,32},{192,64},{224,... | collective-permute-start | bytes 786440 | tf_op jit(solution)/shard_map/ppermute | solution.py:313
  102.8 7.3 %collective-permute-start.12 = (bf16[256,512]{1,0:T(8,128)(2,1)S(1)}, bf16[256,512]{1,0:T(8,128)(2,1)S(1)}, u32[]{:S(2)}, u32[]{:S(2)}) collective-permute-start(bf16[256,512]{1,0:T(8,128)(2,1)S(1)} %project.7), channel_id=1, source_target_pairs={{0,128},{32,160},{64,192},{96,224},{128,0},{160,32},{192,64},{224,... | collective-permute-start | bytes 786440 | tf_op jit(solution)/shard_map/ppermute | solution.py:313

commit v4 on v3

--- a/solution.py
+++ b/solution.py
@@ -10,8 +10,10 @@
 
 EDGE = 128
 WIDE = 48 * 1024 * 1024
+MEDIUM = 32 * 1024 * 1024
+SMALL = 16 * 1024 * 1024
 ALONG_X = 4
-FIRST_SLABS = 2
+RUNS = (2, 2)
 BATCH = 8
 
 
@@ -28,18 +30,37 @@
     fast = 2.0 * np.pi * np.outer(steps, steps) / EDGE
     turn = 2.0 * np.pi * np.outer(steps + 0.25, steps) / (EDGE * EDGE)
     first = np.concatenate([np.cos(slow), -np.sin(slow)], 0)
-    second = np.block([[np.cos(fast), -np.sin(fast)], [np.sin(fast), np.cos(fast)]])
-    third = np.block([[np.cos(fast), np.sin(fast)], [-np.sin(fast), np.cos(fast)]]) / EDGE
-    last = np.concatenate([np.cos(slow).T, -np.sin(slow).T], 1) / EDGE
-    first_high, first_low = split_table(first)
-    stacked = [np.concatenate([first_high, first_low], 1)]
-    for table in (second, third):
-        stacked.extend(split_table(table))
+    second = np.concatenate([np.cos(fast), np.sin(fast)], 1)
     return (
-        np.concatenate(stacked, 0),
-        np.concatenate(split_table(last), 1),
+        np.concatenate(split_table(first), 1),
+        np.concatenate(split_table(second), 1),
         np.stack([np.cos(turn), np.sin(turn)]).astype(np.float32),
     )
+
+
+def build_tables(first, base, second, third, last):
+    for part in range(2):
+        cos = base[:, 2 * part * EDGE : (2 * part + 1) * EDGE]
+        sin = base[:, (2 * part + 1) * EDGE : (2 * part + 2) * EDGE]
+        ahead = jnp.concatenate(
+            [jnp.concatenate([cos, -sin], axis=1), jnp.concatenate([sin, cos], axis=1)], axis=0
+        )
+        back = jnp.concatenate(
+            [jnp.concatenate([cos, sin], axis=1), jnp.concatenate([-sin, cos], axis=1)], axis=0
+        )
+        end = jnp.concatenate(
+            [
+                first[half * EDGE : (half + 1) * EDGE, part * EDGE : (part + 1) * EDGE].T
+                for half in range(2)
+            ],
+            axis=1,
+        )
+        scale = jnp.bfloat16(1.0 / EDGE)
+        for place in ((0, 1), (2,))[part]:
+            rows = slice(2 * place * EDGE, 2 * (place + 1) * EDGE)
+            second[rows, :] = ahead
+            third[rows, :] = back * scale
+            last[:, rows] = end * scale
 
 
 def thirds(array, axis):
@@ -103,21 +124,14 @@
         copy.wait()
 
 
-def conv_kernel(chans, in_ref, tables, last, turns, out_ref, wide, back):
+def conv_kernel(
+    chans, in_ref, first_table, base, turns, out_ref, wide, back, second, third, last
+):
+    build_tables(first_table, base, second, third, last)
     wide[...] = in_ref[...].astype(jnp.float32)
     cos, sin = turns[0], turns[1]
 
-    def three(index):
-        high = tables[2 * EDGE * index : 2 * EDGE * (index + 1), :]
-        low = tables[2 * EDGE * (index + 1) : 2 * EDGE * (index + 2), :]
-        return jnp.concatenate([high, high, low], axis=0)
-
-    def last_three():
-        high, low = last[:, : 2 * EDGE], last[:, 2 * EDGE :]
-        return jnp.concatenate([high, high, low], axis=1)
-
-
-    @pl.loop(0, chans // BATCH)
+    @pl.loop(0, chans // BATCH, unroll=True)
     def _(step):
         first = step * BATCH
         signals = [
@@ -126,7 +140,7 @@
             for which in range(2)
         ]
         both = jnp.concatenate(signals, axis=1)
-        slow = dot(tables[: 2 * EDGE, :], jnp.concatenate([both, both], axis=0))
+        slow = dot(first_table[...], jnp.concatenate([both, both], axis=0))
         rows = []
         for k in range(2 * BATCH):
             cols = slice(k * EDGE, (k + 1) * EDGE)
@@ -134,14 +148,14 @@
             rows.append(
                 jnp.concatenate([real * cos + imag * sin, imag * cos - real * sin], axis=1)
             )
-        spectra = dot(thirds(jnp.concatenate(rows, axis=0), 1), three(1))
+        spectra = dot(thirds(jnp.concatenate(rows, axis=0), 1), second[...])
         rows = []
         for k in range(BATCH):
             ours = spectra[2 * k * EDGE : (2 * k + 1) * EDGE]
             taps = spectra[(2 * k + 1) * EDGE : (2 * k + 2) * EDGE]
             ar, ai, br, bi = ours[:, :EDGE], ours[:, EDGE:], taps[:, :EDGE], taps[:, EDGE:]
             rows.append(jnp.concatenate([ar * br - ai * bi, ar * bi + ai * br], axis=1))
-        wound = dot(thirds(jnp.concatenate(rows, axis=0), 1), three(3))
+        wound = dot(thirds(jnp.concatenate(rows, axis=0), 1), third[...])
         cols = []
         for k in range(BATCH):
             real = wound[k * EDGE : (k + 1) * EDGE, :EDGE]
@@ -149,7 +163,7 @@
             cols.append(
                 jnp.concatenate([real * cos - imag * sin, imag * cos + real * sin], axis=0)
             )
-        conv = dot(last_three(), thirds(jnp.concatenate(cols, axis=1), 0))
+        conv = dot(last[...], thirds(jnp.concatenate(cols, axis=1), 0))
         for k in range(BATCH):
             back[pl.ds(first + k, EDGE, stride=chans), :] = conv[:, k * EDGE : (k + 1) * EDGE]
 
@@ -162,9 +176,7 @@
     peers = EDGE // chans
     for slab in range(slabs):
         rows = slice(slab * EDGE, (slab + 1) * EDGE)
-        out_ref, first = outs[0], slab
-        if slab >= FIRST_SLABS:
-            out_ref, first = outs[1], slab - FIRST_SLABS
+        run, first = [(run, k) for run, count in enumerate(RUNS) for k in range(count)][slab]
         out_rows = slice(first * EDGE, (first + 1) * EDGE)
         for part in range(width // EDGE):
             cols = slice(part * EDGE, (part + 1) * EDGE)
@@ -175,14 +187,14 @@
             gated = gated.astype(jnp.bfloat16).astype(jnp.float32)
             inner = conv.astype(jnp.float32) + skip_ref[:, cols] * gated
             mixed = gate_out_ref[rows, cols].astype(jnp.float32) * inner
-            out_ref[out_rows, cols] = mixed.astype(jnp.bfloat16)
-
-
-def project_kernel(n_parts, *refs):
-    parts, weights, out_ref = refs[:n_parts], refs[n_parts:-1], refs[-1]
+            outs[run][out_rows, cols] = mixed.astype(jnp.bfloat16)
+
+
+def project_kernel(*refs):
+    *parts, weights, out_ref = refs
 
     def product(part, shift):
-        return dot(part[...], weights[shift][0])
+        return dot(part[...], weights[shift])
 
     total = product(parts[0], 0) + product(parts[1], 1) + product(parts[-1], ALONG_X - 1)
     across = jnp.concatenate([product(part, 2) for part in parts[2:-1]], axis=0)
@@ -230,8 +242,11 @@
         scratch_shapes=[
             pltpu.VMEM((2 * rows, EDGE), jnp.float32),
             pltpu.VMEM((rows, EDGE), jnp.float32),
+            pltpu.VMEM((6 * EDGE, 2 * EDGE), jnp.bfloat16),
+            pltpu.VMEM((6 * EDGE, 2 * EDGE), jnp.bfloat16),
+            pltpu.VMEM((EDGE, 6 * EDGE), jnp.bfloat16),
         ],
-        compiler_params=pltpu.CompilerParams(vmem_limit_bytes=WIDE),
+        compiler_params=pltpu.CompilerParams(vmem_limit_bytes=MEDIUM),
         cost_estimate=pl.CostEstimate(
             flops=6 * 10**9, bytes_accessed=2 * 10**6, transcendentals=0
         ),
@@ -241,36 +256,57 @@
 
 
 def mix(conv, value, gate_in, gate_out, skip):
-    rows, width = value.shape
-    first = FIRST_SLABS * EDGE
+    width = value.shape[1]
     whole = pl.BlockSpec(memory_space=pltpu.VMEM)
     return pl.pallas_call(
         mix_kernel,
         in_specs=[whole] * 5,
-        out_specs=[whole] * 2,
-        out_shape=[
-            jax.ShapeDtypeStruct((count, width), jnp.bfloat16) for count in (first, rows - first)
-        ],
-        compiler_params=pltpu.CompilerParams(vmem_limit_bytes=WIDE),
+        out_specs=[whole] * len(RUNS),
+        out_shape=[jax.ShapeDtypeStruct((run * EDGE, width), jnp.bfloat16) for run in RUNS],
+        compiler_params=pltpu.CompilerParams(vmem_limit_bytes=SMALL),
         name="mix",
     )(conv, value, gate_in, gate_out, skip)
 
 
-def project_half(parts, weights, side, dtype):
+def stage_kernel(side, *refs):
+    weights, out_ref, done = refs[:-2], refs[-2], refs[-1]
+    copies = [
+        pltpu.make_async_copy(weight.at[side], out_ref.at[shift], done.at[shift])
+        for shift, weight in enumerate(weights)
+    ]
+    for copy in copies:
+        copy.start()
+    for copy in copies:
+        copy.wait()
+
+
+def stage(weights, side):
+    return pl.pallas_call(
+        functools.partial(stage_kernel, side),
+        in_specs=[pl.BlockSpec(memory_space=pl.ANY)] * len(weights),
+        out_specs=pl.BlockSpec(memory_space=pltpu.VMEM),
+        out_shape=jax.ShapeDtypeStruct((len(weights), *weights[0].shape[1:]), jnp.bfloat16),
+        scratch_shapes=[pltpu.SemaphoreType.DMA((len(weights),))],
+        compiler_params=pltpu.CompilerParams(vmem_limit_bytes=SMALL),
+        cost_estimate=pl.CostEstimate(flops=0, bytes_accessed=8 * 10**6, transcendentals=0),
+        name="stage",
+    )(*weights)
+
+
+def project_half(parts, weights, dtype):
     rows, width = parts[0].shape
-    return pl.pallas_call(
-        functools.partial(project_kernel, len(parts)),
-        grid=(1,),
-        in_specs=[pl.BlockSpec(part.shape, lambda i: (0, 0)) for part in parts]
-        + [pl.BlockSpec((1, *weight.shape[1:]), lambda i: (side, 0, 0)) for weight in weights],
-        out_specs=pl.BlockSpec((rows, width), lambda i: (0, 0)),
+    whole = pl.BlockSpec(memory_space=pltpu.VMEM)
+    return pl.pallas_call(
+        project_kernel,
+        in_specs=[whole] * (len(parts) + 1),
+        out_specs=whole,
         out_shape=jax.ShapeDtypeStruct((rows, width), dtype),
-        compiler_params=pltpu.CompilerParams(vmem_limit_bytes=WIDE),
+        compiler_params=pltpu.CompilerParams(vmem_limit_bytes=SMALL),
         cost_estimate=pl.CostEstimate(
             flops=2 * rows * ALONG_X * width * width, bytes_accessed=3 * 10**6, transcendentals=0
         ),
         name="project",
-    )(*parts, *weights)
+    )(*parts, weights)
 
 
 def along_x(shift):
@@ -305,14 +341,16 @@
     returned = lax.all_to_all(conv, "ctx", split_axis=0, concat_axis=0, tiled=True)
     mixed = mix(returned, value, gate_in, gate_out, skip[None])
     mixed, pieces = lax.optimization_barrier((mixed, pieces))
+    parts = [gather_x(rows) for rows in mixed]
     weights = [own, *pieces]
-    parts = [gather_x(rows) for rows in mixed]
-    theirs, outs = [], []
-    for part in parts:
-        share = project_half(part, weights, 1, jnp.bfloat16)
-        theirs.append(lax.ppermute(share, "chan", across_y()))
+    outs = []
+    staged = stage(weights, 1)
+    shares = [project_half(part, staged, jnp.bfloat16) for part in parts]
+    theirs = [lax.ppermute(share, "chan", across_y()) for share in shares]
+    weights, _ = lax.optimization_barrier((weights, shares))
+    staged = stage(weights, 0)
     for part, arrived in zip(parts, theirs):
-        mine = project_half(part, weights, 0, jnp.float32)
+        mine = project_half(part, staged, jnp.float32)
         outs.append((mine + arrived.astype(jnp.float32)).astype(jnp.bfloat16))
     return jnp.concatenate(outs, axis=0)
 

time: 111 us -> 109 us (0.982)
  Pallas kernels: 23.3 us -> 21.1 us
    pallas_call x5 -> x7, Pallas kernels: 7.36 us -> 5.56 us  [the longest x4 2.8 us: project_half(): pl.pallas_call(project_kernel, in_specs=[whole] * (len(parts) + 1), out_s...]
  transfers between devices with their start and end apart: 14 -> 14, of which waited for: 6 -> 7; matrix products, arithmetic and copies ran while one was open for 0% -> 0% of each run, Pallas kernels for 19% -> 17%
where the time goes in v4:
time: 109 us; the launch traced here: 108 us
  starting transfers between devices  33.9 us (31%)
  waiting for transfers between devices  29.5 us (27%)
  blocking collectives  22.5 us (21%)
  Pallas kernels  21.1 us (19%)
    all_to_all x1, blocking collectives, per_device(): lax.all_to_all(conv, 'ctx', split_axis=0, concat_axis=0, tiled=True)  22.5 us
    all_to_all x1, waiting for transfers between devices, per_device(): lax.all_to_all(packed, 'ctx', split_axis=0, concat_axis=0, tiled=True)  18.7 us
    ppermute x8, starting transfers between devices, send(): return lax.ppermute(rows, 'chan', along_x(shift))  13.8 us
    all_to_all x1, starting transfers between devices, per_device(): lax.all_to_all(packed, 'ctx', split_axis=0, concat_axis=0, tiled=True)  11.7 us
    pallas_call x1, Pallas kernels, convolve(): pl.pallas_call(functools.partial(conv_kernel, chans), in_specs=[whole] *...  8.43 us
    ppermute x8, waiting for transfers between devices, send(): return lax.ppermute(rows, 'chan', along_x(shift))  7.78 us
    ppermute x3, starting transfers between devices, per_device(): lax.ppermute(piece, 'chan', along_x(i + 1))  5.73 us
    pallas_call x1, Pallas kernels, deal(): pl.pallas_call(deal_kernel, in_specs=[pl.BlockSpec(memory_space=pltpu.SME...  4.45 us
  transfers between devices with their start and end apart: 14, of which 7 were waited for; matrix products, arithmetic and copies ran while one was open for 0% of the time, Pallas kernels for 17%

profile of v4, /device:TPU:16, one launch (start us, length us, event | category | flops | bytes accessed | tf_op | source)
XLA Modules:
  0.0 108.4 jit_solution(9868954544289480699)
XLA Ops:
  0.0 2.7 %pack.1 = bf16[32,4,2,16,128]{4,3,2,1,0:T(8,128)(2,1)} custom-call(bf16[512,512]{1,0:T(8,128)(2,1)} %value_ref.1, bf16[512,512]{1,0:T(8,128)(2,1)} %gate_ref.1, bf16[512,512]{1,0:T(8,128)(2,1)} %filt_hbm.1), custom_call_target="tpu_custom_call" | custom-call | tf_op jit(solution)/shard_map/pack/pallas_call | solution.py:207
  2.7 11.7 %all-to-all-start = ((bf16[32,4,2,16,128]{4,3,2,1,0:T(8,128)(2,1)}), bf16[32,4,2,16,128]{4,3,2,1,0:T(8,128)(2,1)}, u32[]{:S(2)}, u32[]{:S(2)}) async-start(bf16[32,4,2,16,128]{4,3,2,1,0:T(8,128)(2,1)} %pack.1), calls=%async_computation | async-start | bytes 2097152 | tf_op jit(solution)/shard_map/all_to_all | solution.py:338
  14.3 0.1 pad_add_fusion.place
  14.4 0.0 copy-start.4
  14.4 0.0 copy-start.5
  14.4 0.0 copy-start.6
  14.4 4.5 %deal.1 = (bf16[2,512,512]{2,1,0:T(8,128)(2,1)}, bf16[2,512,512]{2,1,0:T(8,128)(2,1)}, bf16[2,512,512]{2,1,0:T(8,128)(2,1)}, bf16[2,512,512]{2,1,0:T(8,128)(2,1)S(1)}) custom-call(s32[2]{0:T(128)S(1)} %pad_add_fusion.place, bf16[512,4096]{1,0:T(8,128)(2,1)} %w_hbm.1), custom_call_target="tpu_custom_call" | custom-call | tf_op jit(solution)/shard_map/deal/pallas_call | solution.py:222
  18.9 1.6 %collective-permute-start = (bf16[2,512,512]{2,1,0:T(8,128)(2,1)}, bf16[2,512,512]{2,1,0:T(8,128)(2,1)S(1)}, u32[]{:S(2)}, u32[]{:S(2)}) collective-permute-start(bf16[2,512,512]{2,1,0:T(8,128)(2,1)} %get-tuple-element.22), channel_id=1, source_target_pairs={{0,32},{32,64},{64,96},{96,0},{128,160},{160,192},{192,224},{224,1... | collective-permute-start | bytes 3145736 | tf_op jit(solution)/shard_map/ppermute | solution.py:337
  20.4 2.7 %collective-permute-start.1 = (bf16[2,512,512]{2,1,0:T(8,128)(2,1)}, bf16[2,512,512]{2,1,0:T(8,128)(2,1)S(1)}, u32[]{:S(2)}, u32[]{:S(2)}) collective-permute-start(bf16[2,512,512]{2,1,0:T(8,128)(2,1)} %get-tuple-element.23), channel_id=1, source_target_pairs={{0,64},{32,96},{64,0},{96,32},{128,192},{160,224},{192,128},{224,1... | collective-permute-start | bytes 3145736 | tf_op jit(solution)/shard_map/ppermute | solution.py:337
  23.2 1.4 %collective-permute-start.2 = (bf16[2,512,512]{2,1,0:T(8,128)(2,1)}, bf16[2,512,512]{2,1,0:T(8,128)(2,1)}, u32[]{:S(2)}, u32[]{:S(2)}) collective-permute-start(bf16[2,512,512]{2,1,0:T(8,128)(2,1)} %get-tuple-element.24), channel_id=1, source_target_pairs={{0,96},{32,0},{64,32},{96,64},{128,224},{160,128},{192,160},{224,1... | collective-permute-start | bytes 3145736 | tf_op jit(solution)/shard_map/ppermute | solution.py:337
  24.6 18.7 %all-to-all-done = bf16[32,4,2,16,128]{4,3,2,1,0:T(8,128)(2,1)} async-done(((bf16[32,4,2,16,128]{4,3,2,1,0:T(8,128)(2,1)}), bf16[32,4,2,16,128]{4,3,2,1,0:T(8,128)(2,1)}, u32[]{:S(2)}, u32[]{:S(2)}) %all-to-all-start) | async-done | bytes 1048608 | tf_op jit(solution)/shard_map/all_to_all | solution.py:338
  43.3 0.0 copy-done.4
  43.3 0.0 copy-done.5
  43.3 0.0 copy-done.6
  43.3 0.0 copy-start
  43.3 0.0 copy-start.1
  43.3 0.0 copy-start.2
  43.4 0.0 copy-start.3
  43.4 8.4 %convolve.1 = bf16[2048,128]{1,0:T(8,128)(2,1)S(1)} custom-call(bf16[4096,128]{1,0:T(8,128)(2,1)} %bitcast.in_ref, bf16[256,256]{1,0:T(8,128)(2,1)S(1)} %copy-done.6, bf16[128,512]{1,0:T(8,128)(2,1)S(1)} %copy-done.5, f32[2,128,128]{2,1,0:T(8,128)S(1)} %copy-done.4), custom_call_target="tpu_custom_call" | custom-call | flops 6000000000 | bytes 2000000 | tf_op jit(solution)/shard_map/convolve/pallas_call | solution.py:237
  51.8 22.5 %all_to_all.10.conv_ref = bf16[32,4,16,128]{3,2,1,0:T(8,128)(2,1)S(1)} all-to-all(bf16[32,4,16,128]{3,2,1,0:T(8,128)(2,1)S(1)} %bitcast.5), channel_id=1, replica_groups=mesh['chan'=8,'ctx'=32] {'ctx'}, dimensions={0} | all-to-all | bytes 1048576 | tf_op jit(solution)/shard_map/all_to_all | solution.py:341
  74.3 0.0 copy-done
  74.3 0.0 copy-done.1
  74.3 0.0 copy-done.2
  74.3 0.0 copy-done.3
  74.3 0.4 mix.1
  74.7 0.0 collective-permute-done.refs_1_
  74.7 0.0 collective-permute-done.1.refs_2_
  74.7 0.0 collective-permute-done.2.refs_3_
  74.7 2.8 %collective-permute-start.5 = (bf16[256,512]{1,0:T(8,128)(2,1)S(1)}, bf16[256,512]{1,0:T(8,128)(2,1)S(1)}, u32[]{:S(2)}, u32[]{:S(2)}) collective-permute-start(bf16[256,512]{1,0:T(8,128)(2,1)S(1)} %get-tuple-element.25.refs_0_), channel_id=1, source_target_pairs={{0,96},{32,0},{64,32},{96,64},{128,224},{160,128},{192,160},{224,1... | collective-permute-start | bytes 786440 | tf_op jit(solution)/shard_map/ppermute | solution.py:324
  77.6 0.0 collective-permute-start.3
  77.6 3.2 %collective-permute-start.9 = (bf16[256,512]{1,0:T(8,128)(2,1)S(1)}, bf16[256,512]{1,0:T(8,128)(2,1)S(1)}, u32[]{:S(2)}, u32[]{:S(2)}) collective-permute-start(bf16[256,512]{1,0:T(8,128)(2,1)S(1)} %get-tuple-element.30.refs_0_), channel_id=1, source_target_pairs={{0,96},{32,0},{64,32},{96,64},{128,224},{160,128},{192,160},{224,1... | collective-permute-start | bytes 786440 | tf_op jit(solution)/shard_map/ppermute | solution.py:324
  80.8 0.0 collective-permute-start.7
  80.8 3.5 %collective-permute-done.5.refs_4_ = bf16[256,512]{1,0:T(8,128)(2,1)S(1)} collective-permute-done((bf16[256,512]{1,0:T(8,128)(2,1)S(1)}, bf16[256,512]{1,0:T(8,128)(2,1)S(1)}, u32[]{:S(2)}, u32[]{:S(2)}) %collective-permute-start.5) | collective-permute-done | bytes 262176 | tf_op jit(solution)/shard_map/ppermute | solution.py:324
  84.4 3.8 %collective-permute-start.6 = (bf16[128,512]{1,0:T(8,128)(2,1)S(1)}, bf16[128,512]{1,0:T(8,128)(2,1)S(1)}, u32[]{:S(2)}, u32[]{:S(2)}) collective-permute-start(bf16[128,512]{1,0:T(8,128)(2,1)S(1)} %slice.17), channel_id=1, source_target_pairs={{0,96},{32,0},{64,32},{96,64},{128,224},{160,128},{192,160},{224,1... | collective-permute-start | bytes 393224 | tf_op jit(solution)/shard_map/ppermute | solution.py:324
  88.1 0.0 collective-permute-done.3.refs_1_
  88.1 0.1 collective-permute-start.4
  88.2 1.2 %stage.2.refs_5_ = bf16[4,512,512]{2,1,0:T(8,128)(2,1)S(1)} custom-call(bf16[2,512,512]{2,1,0:T(8,128)(2,1)S(1)} %get-tuple-element.31.refs_0_, bf16[2,512,512]{2,1,0:T(8,128)(2,1)S(1)} %collective-permute-done.refs_1_, bf16[2,512,512]{2,1,0:T(8,128)(2,1)S(1)} %collective-permute-done.1.refs_2_, bf16[2,512,512]{2,1,0:T(8,128)(2,1)} %collective-permute-done.2.refs_3_), custom_call_target="tpu_custom_call" | custom-call | bytes 8000000 | tf_op jit(solution)/shard_map/stage/pallas_call | solution.py:284
  89.4 0.2 collective-permute-done.9.refs_4_
  89.6 3.8 %collective-permute-start.10 = (bf16[128,512]{1,0:T(8,128)(2,1)S(1)}, bf16[128,512]{1,0:T(8,128)(2,1)S(1)}, u32[]{:S(2)}, u32[]{:S(2)}) collective-permute-start(bf16[128,512]{1,0:T(8,128)(2,1)S(1)} %slice.19), channel_id=1, source_target_pairs={{0,96},{32,0},{64,32},{96,64},{128,224},{160,128},{192,160},{224,1... | collective-permute-start | bytes 393224 | tf_op jit(solution)/shard_map/ppermute | solution.py:324
  93.4 0.0 collective-permute-done.7.refs_1_
  93.4 0.1 collective-permute-start.8
  93.5 0.0 collective-permute-done.6.refs_3_
  93.5 1.3 %collective-permute-done.4.refs_2_ = bf16[128,512]{1,0:T(8,128)(2,1)S(1)} collective-permute-done((bf16[128,512]{1,0:T(8,128)(2,1)S(1)}, bf16[128,512]{1,0:T(8,128)(2,1)S(1)}, u32[]{:S(2)}, u32[]{:S(2)}) %collective-permute-start.4) | collective-permute-done | bytes 131104 | tf_op jit(solution)/shard_map/ppermute | solution.py:324
  94.8 0.7 project.4
  95.5 1.4 %collective-permute-start.11 = (bf16[256,512]{1,0:T(8,128)(2,1)S(1)}, bf16[256,512]{1,0:T(8,128)(2,1)S(1)}, u32[]{:S(2)}, u32[]{:S(2)}) collective-permute-start(bf16[256,512]{1,0:T(8,128)(2,1)S(1)} %project.4), channel_id=1, source_target_pairs={{0,128},{32,160},{64,192},{96,224},{128,0},{160,32},{192,64},{224,... | collective-permute-start | bytes 786440 | tf_op jit(solution)/shard_map/ppermute | solution.py:349
  96.9 0.0 collective-permute-done.10.refs_3_
  96.9 2.8 %collective-permute-done.8.refs_2_ = bf16[128,512]{1,0:T(8,128)(2,1)S(1)} collective-permute-done((bf16[128,512]{1,0:T(8,128)(2,1)S(1)}, bf16[128,512]{1,0:T(8,128)(2,1)S(1)}, u32[]{:S(2)}, u32[]{:S(2)}) %collective-permute-start.8) | collective-permute-done | bytes 131104 | tf_op jit(solution)/shard_map/ppermute | solution.py:324
  99.7 0.7 project.5
  100.4 1.4 %collective-permute-start.12 = (bf16[256,512]{1,0:T(8,128)(2,1)S(1)}, bf16[256,512]{1,0:T(8,128)(2,1)S(1)}, u32[]{:S(2)}, u32[]{:S(2)}) collective-permute-start(bf16[256,512]{1,0:T(8,128)(2,1)S(1)} %project.5), channel_id=1, source_target_pairs={{0,128},{32,160},{64,192},{96,224},{128,0},{160,32},{192,64},{224,... | collective-permute-start | bytes 786440 | tf_op jit(solution)/shard_map/ppermute | solution.py:349
  101.7 1.2 %stage.3.refs_5_ = bf16[4,512,512]{2,1,0:T(8,128)(2,1)S(1)} custom-call(bf16[2,512,512]{2,1,0:T(8,128)(2,1)S(1)} %get-tuple-element.31.refs_0_, bf16[2,512,512]{2,1,0:T(8,128)(2,1)S(1)} %collective-permute-done.refs_1_, bf16[2,512,512]{2,1,0:T(8,128)(2,1)S(1)} %collective-permute-done.1.refs_2_, bf16[2,512,512]{2,1,0:T(8,128)(2,1)} %collective-permute-done.2.refs_3_), custom_call_target="tpu_custom_call" | custom-call | bytes 8000000 | tf_op jit(solution)/shard_map/stage/pallas_call | solution.py:284
  102.9 0.7 project.7
  103.6 0.7 project.6
  104.3 0.3 collective-permute-done.11
  104.7 0.1 add_convert_fusion.1
  104.7 2.7 %collective-permute-done.12 = bf16[256,512]{1,0:T(8,128)(2,1)S(1)} collective-permute-done((bf16[256,512]{1,0:T(8,128)(2,1)S(1)}, bf16[256,512]{1,0:T(8,128)(2,1)S(1)}, u32[]{:S(2)}, u32[]{:S(2)}) %collective-permute-start.12) | collective-permute-done | bytes 262176 | tf_op jit(solution)/shard_map/ppermute | solution.py:349
  107.5 0.1 add_convert_fusion
  107.5 0.8 pad_maximum_fusion
  (4 shorter events, 0.0 us)
Async XLA Ops:
  2.7 40.6 %all-to-all-start = ((bf16[32,4,2,16,128]{4,3,2,1,0:T(8,128)(2,1)}), bf16[32,4,2,16,128]{4,3,2,1,0:T(8,128)(2,1)}, u32[]{:S(2)}, u32[]{:S(2)}) async-start(bf16[32,4,2,16,128]{4,3,2,1,0:T(8,128)(2,1)} %pack.1), calls=%async_computation | async-start | bytes 2097152 | tf_op jit(solution)/shard_map/all_to_all | solution.py:338
  14.4 28.9 %copy-start.4 = (f32[2,128,128]{2,1,0:T(8,128)S(1)}, f32[2,128,128]{2,1,0:T(8,128)}, u32[]{:S(2)}) copy-start(f32[2,128,128]{2,1,0:T(8,128)} %constant.22.clone.turns) | copy-start | bytes 393220
  14.4 28.9 %copy-start.5 = (bf16[128,512]{1,0:T(8,128)(2,1)S(1)}, bf16[128,512]{1,0:T(8,128)(2,1)}, u32[]{:S(2)}) copy-start(bf16[128,512]{1,0:T(8,128)(2,1)} %constant.21.clone.base) | copy-start | bytes 393220
  14.4 28.9 %copy-start.6 = (bf16[256,256]{1,0:T(8,128)(2,1)S(1)}, bf16[256,256]{1,0:T(8,128)(2,1)}, u32[]{:S(2)}) copy-start(bf16[256,256]{1,0:T(8,128)(2,1)} %constant.20.clone.first_table) | copy-start | bytes 393220
  18.9 55.8 %collective-permute-start = (bf16[2,512,512]{2,1,0:T(8,128)(2,1)}, bf16[2,512,512]{2,1,0:T(8,128)(2,1)S(1)}, u32[]{:S(2)}, u32[]{:S(2)}) collective-permute-start(bf16[2,512,512]{2,1,0:T(8,128)(2,1)} %get-tuple-element.22), channel_id=1, source_target_pairs={{0,32},{32,64},{64,96},{96,0},{128,160},{160,192},{192,224},{224,1... | collective-permute-start | bytes 3145736 | tf_op jit(solution)/shard_map/ppermute | solution.py:337
  20.4 54.3 %collective-permute-start.1 = (bf16[2,512,512]{2,1,0:T(8,128)(2,1)}, bf16[2,512,512]{2,1,0:T(8,128)(2,1)S(1)}, u32[]{:S(2)}, u32[]{:S(2)}) collective-permute-start(bf16[2,512,512]{2,1,0:T(8,128)(2,1)} %get-tuple-element.23), channel_id=1, source_target_pairs={{0,64},{32,96},{64,0},{96,32},{128,192},{160,224},{192,128},{224,1... | collective-permute-start | bytes 3145736 | tf_op jit(solution)/shard_map/ppermute | solution.py:337
  23.2 51.6 %collective-permute-start.2 = (bf16[2,512,512]{2,1,0:T(8,128)(2,1)}, bf16[2,512,512]{2,1,0:T(8,128)(2,1)}, u32[]{:S(2)}, u32[]{:S(2)}) collective-permute-start(bf16[2,512,512]{2,1,0:T(8,128)(2,1)} %get-tuple-element.24), channel_id=1, source_target_pairs={{0,96},{32,0},{64,32},{96,64},{128,224},{160,128},{192,160},{224,1... | collective-permute-start | bytes 3145736 | tf_op jit(solution)/shard_map/ppermute | solution.py:337
  43.3 31.0 %copy-start = (bf16[512,512]{1,0:T(8,128)(2,1)S(1)}, bf16[512,512]{1,0:T(8,128)(2,1)}, u32[]{:S(2)}) copy-start(bf16[512,512]{1,0:T(8,128)(2,1)} %value_ref.1) | copy-start | bytes 1572868
  43.3 31.0 %copy-start.1 = (bf16[512,512]{1,0:T(8,128)(2,1)S(1)}, bf16[512,512]{1,0:T(8,128)(2,1)}, u32[]{:S(2)}) copy-start(bf16[512,512]{1,0:T(8,128)(2,1)} %gate_ref.1) | copy-start | bytes 1572868
  43.3 31.0 %copy-start.2 = (bf16[512,512]{1,0:T(8,128)(2,1)S(1)}, bf16[512,512]{1,0:T(8,128)(2,1)}, u32[]{:S(2)}) copy-start(bf16[512,512]{1,0:T(8,128)(2,1)} %gate_out_ref.1) | copy-start | bytes 1572868
  43.4 31.0 %copy-start.3 = (f32[512]{0:T(512)S(1)}, f32[512]{0:T(512)}, u32[]{:S(2)}) copy-start(f32[512]{0:T(512)} %param.13) | copy-start | bytes 6148
  74.7 9.6 %collective-permute-start.5 = (bf16[256,512]{1,0:T(8,128)(2,1)S(1)}, bf16[256,512]{1,0:T(8,128)(2,1)S(1)}, u32[]{:S(2)}, u32[]{:S(2)}) collective-permute-start(bf16[256,512]{1,0:T(8,128)(2,1)S(1)} %get-tuple-element.25.refs_0_), channel_id=1, source_target_pairs={{0,96},{32,0},{64,32},{96,64},{128,224},{160,128},{192,160},{224,1... | collective-permute-start | bytes 786440 | tf_op jit(solution)/shard_map/ppermute | solution.py:324
  77.6 10.5 %collective-permute-start.3 = (bf16[256,512]{1,0:T(8,128)(2,1)S(1)}, bf16[256,512]{1,0:T(8,128)(2,1)S(1)}, u32[]{:S(2)}, u32[]{:S(2)}) collective-permute-start(bf16[256,512]{1,0:T(8,128)(2,1)S(1)} %get-tuple-element.25.refs_0_), channel_id=1, source_target_pairs={{0,32},{32,64},{64,96},{96,0},{128,160},{160,192},{192,224},{224,1... | collective-permute-start | bytes 786440 | tf_op jit(solution)/shard_map/ppermute | solution.py:324
  77.6 12.0 %collective-permute-start.9 = (bf16[256,512]{1,0:T(8,128)(2,1)S(1)}, bf16[256,512]{1,0:T(8,128)(2,1)S(1)}, u32[]{:S(2)}, u32[]{:S(2)}) collective-permute-start(bf16[256,512]{1,0:T(8,128)(2,1)S(1)} %get-tuple-element.30.refs_0_), channel_id=1, source_target_pairs={{0,96},{32,0},{64,32},{96,64},{128,224},{160,128},{192,160},{224,1... | collective-permute-start | bytes 786440 | tf_op jit(solution)/shard_map/ppermute | solution.py:324
  80.8 12.6 %collective-permute-start.7 = (bf16[256,512]{1,0:T(8,128)(2,1)S(1)}, bf16[256,512]{1,0:T(8,128)(2,1)S(1)}, u32[]{:S(2)}, u32[]{:S(2)}) collective-permute-start(bf16[256,512]{1,0:T(8,128)(2,1)S(1)} %get-tuple-element.30.refs_0_), channel_id=1, source_target_pairs={{0,32},{32,64},{64,96},{96,0},{128,160},{160,192},{192,224},{224,1... | collective-permute-start | bytes 786440 | tf_op jit(solution)/shard_map/ppermute | solution.py:324
  84.4 9.1 %collective-permute-start.6 = (bf16[128,512]{1,0:T(8,128)(2,1)S(1)}, bf16[128,512]{1,0:T(8,128)(2,1)S(1)}, u32[]{:S(2)}, u32[]{:S(2)}) collective-permute-start(bf16[128,512]{1,0:T(8,128)(2,1)S(1)} %slice.17), channel_id=1, source_target_pairs={{0,96},{32,0},{64,32},{96,64},{128,224},{160,128},{192,160},{224,1... | collective-permute-start | bytes 393224 | tf_op jit(solution)/shard_map/ppermute | solution.py:324
  88.1 6.7 %collective-permute-start.4 = (bf16[128,512]{1,0:T(8,128)(2,1)S(1)}, bf16[128,512]{1,0:T(8,128)(2,1)S(1)}, u32[]{:S(2)}, u32[]{:S(2)}) collective-permute-start(bf16[128,512]{1,0:T(8,128)(2,1)S(1)} %slice.16), channel_id=1, source_target_pairs={{0,32},{32,64},{64,96},{96,0},{128,160},{160,192},{192,224},{224,1... | collective-permute-start | bytes 393224 | tf_op jit(solution)/shard_map/ppermute | solution.py:324
  89.6 7.3 %collective-permute-start.10 = (bf16[128,512]{1,0:T(8,128)(2,1)S(1)}, bf16[128,512]{1,0:T(8,128)(2,1)S(1)}, u32[]{:S(2)}, u32[]{:S(2)}) collective-permute-start(bf16[128,512]{1,0:T(8,128)(2,1)S(1)} %slice.19), channel_id=1, source_target_pairs={{0,96},{32,0},{64,32},{96,64},{128,224},{160,128},{192,160},{224,1... | collective-permute-start | bytes 393224 | tf_op jit(solution)/shard_map/ppermute | solution.py:324
  93.4 6.3 %collective-permute-start.8 = (bf16[128,512]{1,0:T(8,128)(2,1)S(1)}, bf16[128,512]{1,0:T(8,128)(2,1)S(1)}, u32[]{:S(2)}, u32[]{:S(2)}) collective-permute-start(bf16[128,512]{1,0:T(8,128)(2,1)S(1)} %slice.18), channel_id=1, source_target_pairs={{0,32},{32,64},{64,96},{96,0},{128,160},{160,192},{192,224},{224,1... | collective-permute-start | bytes 393224 | tf_op jit(solution)/shard_map/ppermute | solution.py:324
  95.5 9.1 %collective-permute-start.11 = (bf16[256,512]{1,0:T(8,128)(2,1)S(1)}, bf16[256,512]{1,0:T(8,128)(2,1)S(1)}, u32[]{:S(2)}, u32[]{:S(2)}) collective-permute-start(bf16[256,512]{1,0:T(8,128)(2,1)S(1)} %project.4), channel_id=1, source_target_pairs={{0,128},{32,160},{64,192},{96,224},{128,0},{160,32},{192,64},{224,... | collective-permute-start | bytes 786440 | tf_op jit(solution)/shard_map/ppermute | solution.py:349
  100.4 7.1 %collective-permute-start.12 = (bf16[256,512]{1,0:T(8,128)(2,1)S(1)}, bf16[256,512]{1,0:T(8,128)(2,1)S(1)}, u32[]{:S(2)}, u32[]{:S(2)}) collective-permute-start(bf16[256,512]{1,0:T(8,128)(2,1)S(1)} %project.5), channel_id=1, source_target_pairs={{0,128},{32,160},{64,192},{96,224},{128,0},{160,32},{192,64},{224,... | collective-permute-start | bytes 786440 | tf_op jit(solution)/shard_map/ppermute | solution.py:349

commit v5 on v4

--- a/solution.py
+++ b/solution.py
@@ -196,8 +196,8 @@
     def product(part, shift):
         return dot(part[...], weights[shift])
 
-    total = product(parts[0], 0) + product(parts[1], 1) + product(parts[-1], ALONG_X - 1)
-    across = jnp.concatenate([product(part, 2) for part in parts[2:-1]], axis=0)
+    total = product(parts[0], 0) + product(parts[1], ALONG_X - 1) + product(parts[-1], 1)
+    across = jnp.concatenate([product(part, 2) for part in parts[-2:1:-1]], axis=0)
     out_ref[...] = (total + across).astype(out_ref.dtype)
 
 
@@ -325,7 +325,7 @@
 
     before, after = send(own, 1), send(own, ALONG_X - 1)
     half = own.shape[0] // 2
-    return [own, before, send(before[:half], 1), send(after[half:], ALONG_X - 1), after]
+    return [own, after, send(after[half:], ALONG_X - 1), send(before[:half], 1), before]
 
 
 def per_device(value, gate_in, gate_out, filt, skip, w_out):

time: 109 us -> 107 us (0.982)
  waiting for transfers between devices: 29.5 us -> 27.6 us
    ppermute x8, waiting for transfers between devices: 7.78 us -> 5.4 us  [send(): return lax.ppermute(rows, 'chan', along_x(shift))]
  transfers between devices with their start and end apart: 14 -> 14, of which waited for: 7 -> 6; matrix products, arithmetic and copies ran while one was open for 0% -> 0% of each run, Pallas kernels for 17% -> 17%
where the time goes in v5:
time: 107 us; the launch traced here: 106 us
  starting transfers between devices  33.5 us (31%)
  waiting for transfers between devices  27.6 us (26%)
  blocking collectives  22.5 us (21%)
  Pallas kernels  21.1 us (20%)
    all_to_all x1, blocking collectives, per_device(): lax.all_to_all(conv, 'ctx', split_axis=0, concat_axis=0, tiled=True)  22.5 us
    all_to_all x1, waiting for transfers between devices, per_device(): lax.all_to_all(packed, 'ctx', split_axis=0, concat_axis=0, tiled=True)  18.7 us
    ppermute x8, starting transfers between devices, send(): return lax.ppermute(rows, 'chan', along_x(shift))  13.3 us
    all_to_all x1, starting transfers between devices, per_device(): lax.all_to_all(packed, 'ctx', split_axis=0, concat_axis=0, tiled=True)  11.7 us
    pallas_call x1, Pallas kernels, convolve(): pl.pallas_call(functools.partial(conv_kernel, chans), in_specs=[whole] *...  8.43 us
    ppermute x3, starting transfers between devices, per_device(): lax.ppermute(piece, 'chan', along_x(i + 1))  5.73 us
    ppermute x8, waiting for transfers between devices, send(): return lax.ppermute(rows, 'chan', along_x(shift))  5.4 us
    pallas_call x1, Pallas kernels, deal(): pl.pallas_call(deal_kernel, in_specs=[pl.BlockSpec(memory_space=pltpu.SME...  4.45 us
  transfers between devices with their start and end apart: 14, of which 6 were waited for; matrix products, arithmetic and copies ran while one was open for 0% of the time, Pallas kernels for 17%

profile of v5, /device:TPU:16, one launch (start us, length us, event | category | flops | bytes accessed | tf_op | source)
XLA Modules:
  0.0 106.0 jit_solution(500601291522466566)
XLA Ops:
  0.0 2.7 %pack.1 = bf16[32,4,2,16,128]{4,3,2,1,0:T(8,128)(2,1)} custom-call(bf16[512,512]{1,0:T(8,128)(2,1)} %value_ref.1, bf16[512,512]{1,0:T(8,128)(2,1)} %gate_ref.1, bf16[512,512]{1,0:T(8,128)(2,1)} %filt_hbm.1), custom_call_target="tpu_custom_call" | custom-call | tf_op jit(solution)/shard_map/pack/pallas_call | solution.py:207
  2.7 11.7 %all-to-all-start = ((bf16[32,4,2,16,128]{4,3,2,1,0:T(8,128)(2,1)}), bf16[32,4,2,16,128]{4,3,2,1,0:T(8,128)(2,1)}, u32[]{:S(2)}, u32[]{:S(2)}) async-start(bf16[32,4,2,16,128]{4,3,2,1,0:T(8,128)(2,1)} %pack.1), calls=%async_computation | async-start | bytes 2097152 | tf_op jit(solution)/shard_map/all_to_all | solution.py:338
  14.3 0.1 pad_add_fusion.place
  14.4 0.0 copy-start.4
  14.4 0.0 copy-start.5
  14.4 0.0 copy-start.6
  14.4 4.5 %deal.1 = (bf16[2,512,512]{2,1,0:T(8,128)(2,1)}, bf16[2,512,512]{2,1,0:T(8,128)(2,1)}, bf16[2,512,512]{2,1,0:T(8,128)(2,1)}, bf16[2,512,512]{2,1,0:T(8,128)(2,1)S(1)}) custom-call(s32[2]{0:T(128)S(1)} %pad_add_fusion.place, bf16[512,4096]{1,0:T(8,128)(2,1)} %w_hbm.1), custom_call_target="tpu_custom_call" | custom-call | tf_op jit(solution)/shard_map/deal/pallas_call | solution.py:222
  18.9 1.6 %collective-permute-start = (bf16[2,512,512]{2,1,0:T(8,128)(2,1)}, bf16[2,512,512]{2,1,0:T(8,128)(2,1)S(1)}, u32[]{:S(2)}, u32[]{:S(2)}) collective-permute-start(bf16[2,512,512]{2,1,0:T(8,128)(2,1)} %get-tuple-element.22), channel_id=1, source_target_pairs={{0,32},{32,64},{64,96},{96,0},{128,160},{160,192},{192,224},{224,1... | collective-permute-start | bytes 3145736 | tf_op jit(solution)/shard_map/ppermute | solution.py:337
  20.4 2.7 %collective-permute-start.1 = (bf16[2,512,512]{2,1,0:T(8,128)(2,1)}, bf16[2,512,512]{2,1,0:T(8,128)(2,1)S(1)}, u32[]{:S(2)}, u32[]{:S(2)}) collective-permute-start(bf16[2,512,512]{2,1,0:T(8,128)(2,1)} %get-tuple-element.23), channel_id=1, source_target_pairs={{0,64},{32,96},{64,0},{96,32},{128,192},{160,224},{192,128},{224,1... | collective-permute-start | bytes 3145736 | tf_op jit(solution)/shard_map/ppermute | solution.py:337
  23.2 1.4 %collective-permute-start.2 = (bf16[2,512,512]{2,1,0:T(8,128)(2,1)}, bf16[2,512,512]{2,1,0:T(8,128)(2,1)}, u32[]{:S(2)}, u32[]{:S(2)}) collective-permute-start(bf16[2,512,512]{2,1,0:T(8,128)(2,1)} %get-tuple-element.24), channel_id=1, source_target_pairs={{0,96},{32,0},{64,32},{96,64},{128,224},{160,128},{192,160},{224,1... | collective-permute-start | bytes 3145736 | tf_op jit(solution)/shard_map/ppermute | solution.py:337
  24.6 18.7 %all-to-all-done = bf16[32,4,2,16,128]{4,3,2,1,0:T(8,128)(2,1)} async-done(((bf16[32,4,2,16,128]{4,3,2,1,0:T(8,128)(2,1)}), bf16[32,4,2,16,128]{4,3,2,1,0:T(8,128)(2,1)}, u32[]{:S(2)}, u32[]{:S(2)}) %all-to-all-start) | async-done | bytes 1048608 | tf_op jit(solution)/shard_map/all_to_all | solution.py:338
  43.3 0.0 copy-done.4
  43.3 0.0 copy-done.5
  43.3 0.0 copy-done.6
  43.3 0.0 copy-start
  43.3 0.0 copy-start.1
  43.3 0.0 copy-start.2
  43.4 0.0 copy-start.3
  43.4 8.4 %convolve.1 = bf16[2048,128]{1,0:T(8,128)(2,1)S(1)} custom-call(bf16[4096,128]{1,0:T(8,128)(2,1)} %bitcast.in_ref, bf16[256,256]{1,0:T(8,128)(2,1)S(1)} %copy-done.6, bf16[128,512]{1,0:T(8,128)(2,1)S(1)} %copy-done.5, f32[2,128,128]{2,1,0:T(8,128)S(1)} %copy-done.4), custom_call_target="tpu_custom_call" | custom-call | flops 6000000000 | bytes 2000000 | tf_op jit(solution)/shard_map/convolve/pallas_call | solution.py:237
  51.8 22.5 %all_to_all.10.conv_ref = bf16[32,4,16,128]{3,2,1,0:T(8,128)(2,1)S(1)} all-to-all(bf16[32,4,16,128]{3,2,1,0:T(8,128)(2,1)S(1)} %bitcast.5), channel_id=1, replica_groups=mesh['chan'=8,'ctx'=32] {'ctx'}, dimensions={0} | all-to-all | bytes 1048576 | tf_op jit(solution)/shard_map/all_to_all | solution.py:341
  74.3 0.0 copy-done
  74.3 0.0 copy-done.1
  74.3 0.0 copy-done.2
  74.3 0.0 copy-done.3
  74.3 0.4 mix.1
  74.7 0.0 collective-permute-done.refs_1_
  74.7 0.0 collective-permute-done.1.refs_2_
  74.7 0.0 collective-permute-done.2.refs_3_
  74.7 1.6 %collective-permute-start.5 = (bf16[256,512]{1,0:T(8,128)(2,1)S(1)}, bf16[256,512]{1,0:T(8,128)(2,1)S(1)}, u32[]{:S(2)}, u32[]{:S(2)}) collective-permute-start(bf16[256,512]{1,0:T(8,128)(2,1)S(1)} %get-tuple-element.25.refs_0_), channel_id=1, source_target_pairs={{0,32},{32,64},{64,96},{96,0},{128,160},{160,192},{192,224},{224,1... | collective-permute-start | bytes 786440 | tf_op jit(solution)/shard_map/ppermute | solution.py:324
  76.3 1.7 %collective-permute-start.3 = (bf16[256,512]{1,0:T(8,128)(2,1)S(1)}, bf16[256,512]{1,0:T(8,128)(2,1)S(1)}, u32[]{:S(2)}, u32[]{:S(2)}) collective-permute-start(bf16[256,512]{1,0:T(8,128)(2,1)S(1)} %get-tuple-element.25.refs_0_), channel_id=1, source_target_pairs={{0,96},{32,0},{64,32},{96,64},{128,224},{160,128},{192,160},{224,1... | collective-permute-start | bytes 786440 | tf_op jit(solution)/shard_map/ppermute | solution.py:324
  78.1 0.3 collective-permute-start.9
  78.3 3.0 %collective-permute-start.7 = (bf16[256,512]{1,0:T(8,128)(2,1)S(1)}, bf16[256,512]{1,0:T(8,128)(2,1)S(1)}, u32[]{:S(2)}, u32[]{:S(2)}) collective-permute-start(bf16[256,512]{1,0:T(8,128)(2,1)S(1)} %get-tuple-element.30.refs_0_), channel_id=1, source_target_pairs={{0,96},{32,0},{64,32},{96,64},{128,224},{160,128},{192,160},{224,1... | collective-permute-start | bytes 786440 | tf_op jit(solution)/shard_map/ppermute | solution.py:324
  81.3 4.0 %collective-permute-done.5.refs_4_ = bf16[256,512]{1,0:T(8,128)(2,1)S(1)} collective-permute-done((bf16[256,512]{1,0:T(8,128)(2,1)S(1)}, bf16[256,512]{1,0:T(8,128)(2,1)S(1)}, u32[]{:S(2)}, u32[]{:S(2)}) %collective-permute-start.5) | collective-permute-done | bytes 262176 | tf_op jit(solution)/shard_map/ppermute | solution.py:324
  85.3 0.4 collective-permute-start.6
  85.7 0.0 collective-permute-done.3.refs_1_
  85.7 3.0 %collective-permute-start.4 = (bf16[128,512]{1,0:T(8,128)(2,1)S(1)}, bf16[128,512]{1,0:T(8,128)(2,1)S(1)}, u32[]{:S(2)}, u32[]{:S(2)}) collective-permute-start(bf16[128,512]{1,0:T(8,128)(2,1)S(1)} %slice.16), channel_id=1, source_target_pairs={{0,96},{32,0},{64,32},{96,64},{128,224},{160,128},{192,160},{224,1... | collective-permute-start | bytes 393224 | tf_op jit(solution)/shard_map/ppermute | solution.py:324
  88.7 1.2 %stage.2.refs_5_ = bf16[4,512,512]{2,1,0:T(8,128)(2,1)S(1)} custom-call(bf16[2,512,512]{2,1,0:T(8,128)(2,1)S(1)} %get-tuple-element.31.refs_0_, bf16[2,512,512]{2,1,0:T(8,128)(2,1)S(1)} %collective-permute-done.refs_1_, bf16[2,512,512]{2,1,0:T(8,128)(2,1)S(1)} %collective-permute-done.1.refs_2_, bf16[2,512,512]{2,1,0:T(8,128)(2,1)} %collective-permute-done.2.refs_3_), custom_call_target="tpu_custom_call" | custom-call | bytes 8000000 | tf_op jit(solution)/shard_map/stage/pallas_call | solution.py:284
  89.9 0.6 collective-permute-done.9.refs_4_
  90.6 0.7 collective-permute-start.10
  91.3 0.0 collective-permute-done.7.refs_1_
  91.3 2.7 %collective-permute-start.8 = (bf16[128,512]{1,0:T(8,128)(2,1)S(1)}, bf16[128,512]{1,0:T(8,128)(2,1)S(1)}, u32[]{:S(2)}, u32[]{:S(2)}) collective-permute-start(bf16[128,512]{1,0:T(8,128)(2,1)S(1)} %slice.18), channel_id=1, source_target_pairs={{0,96},{32,0},{64,32},{96,64},{128,224},{160,128},{192,160},{224,1... | collective-permute-start | bytes 393224 | tf_op jit(solution)/shard_map/ppermute | solution.py:324
  94.0 0.0 collective-permute-done.6.refs_3_
  94.0 0.0 collective-permute-done.4.refs_2_
  94.0 0.7 project.4
  94.7 1.4 %collective-permute-start.11 = (bf16[256,512]{1,0:T(8,128)(2,1)S(1)}, bf16[256,512]{1,0:T(8,128)(2,1)S(1)}, u32[]{:S(2)}, u32[]{:S(2)}) collective-permute-start(bf16[256,512]{1,0:T(8,128)(2,1)S(1)} %project.4), channel_id=1, source_target_pairs={{0,128},{32,160},{64,192},{96,224},{128,0},{160,32},{192,64},{224,... | collective-permute-start | bytes 786440 | tf_op jit(solution)/shard_map/ppermute | solution.py:349
  96.0 0.8 collective-permute-done.10.refs_3_
  96.8 0.0 collective-permute-done.8.refs_2_
  96.8 0.7 project.5
  97.5 1.4 %collective-permute-start.12 = (bf16[256,512]{1,0:T(8,128)(2,1)S(1)}, bf16[256,512]{1,0:T(8,128)(2,1)S(1)}, u32[]{:S(2)}, u32[]{:S(2)}) collective-permute-start(bf16[256,512]{1,0:T(8,128)(2,1)S(1)} %project.5), channel_id=1, source_target_pairs={{0,128},{32,160},{64,192},{96,224},{128,0},{160,32},{192,64},{224,... | collective-permute-start | bytes 786440 | tf_op jit(solution)/shard_map/ppermute | solution.py:349
  98.9 1.2 %stage.3.refs_5_ = bf16[4,512,512]{2,1,0:T(8,128)(2,1)S(1)} custom-call(bf16[2,512,512]{2,1,0:T(8,128)(2,1)S(1)} %get-tuple-element.31.refs_0_, bf16[2,512,512]{2,1,0:T(8,128)(2,1)S(1)} %collective-permute-done.refs_1_, bf16[2,512,512]{2,1,0:T(8,128)(2,1)S(1)} %collective-permute-done.1.refs_2_, bf16[2,512,512]{2,1,0:T(8,128)(2,1)} %collective-permute-done.2.refs_3_), custom_call_target="tpu_custom_call" | custom-call | bytes 8000000 | tf_op jit(solution)/shard_map/stage/pallas_call | solution.py:284
  100.1 0.7 project.7
  100.8 0.7 project.6
  101.5 0.8 collective-permute-done.11
  102.3 0.1 add_convert_fusion.1
  102.4 2.7 %collective-permute-done.12 = bf16[256,512]{1,0:T(8,128)(2,1)S(1)} collective-permute-done((bf16[256,512]{1,0:T(8,128)(2,1)S(1)}, bf16[256,512]{1,0:T(8,128)(2,1)S(1)}, u32[]{:S(2)}, u32[]{:S(2)}) %collective-permute-start.12) | collective-permute-done | bytes 262176 | tf_op jit(solution)/shard_map/ppermute | solution.py:349
  105.1 0.1 add_convert_fusion
  105.2 0.8 pad_maximum_fusion
  (4 shorter events, 0.0 us)
Async XLA Ops:
  2.7 40.6 %all-to-all-start = ((bf16[32,4,2,16,128]{4,3,2,1,0:T(8,128)(2,1)}), bf16[32,4,2,16,128]{4,3,2,1,0:T(8,128)(2,1)}, u32[]{:S(2)}, u32[]{:S(2)}) async-start(bf16[32,4,2,16,128]{4,3,2,1,0:T(8,128)(2,1)} %pack.1), calls=%async_computation | async-start | bytes 2097152 | tf_op jit(solution)/shard_map/all_to_all | solution.py:338
  14.4 28.9 %copy-start.4 = (f32[2,128,128]{2,1,0:T(8,128)S(1)}, f32[2,128,128]{2,1,0:T(8,128)}, u32[]{:S(2)}) copy-start(f32[2,128,128]{2,1,0:T(8,128)} %constant.22.clone.turns) | copy-start | bytes 393220
  14.4 28.9 %copy-start.5 = (bf16[128,512]{1,0:T(8,128)(2,1)S(1)}, bf16[128,512]{1,0:T(8,128)(2,1)}, u32[]{:S(2)}) copy-start(bf16[128,512]{1,0:T(8,128)(2,1)} %constant.21.clone.base) | copy-start | bytes 393220
  14.4 28.9 %copy-start.6 = (bf16[256,256]{1,0:T(8,128)(2,1)S(1)}, bf16[256,256]{1,0:T(8,128)(2,1)}, u32[]{:S(2)}) copy-start(bf16[256,256]{1,0:T(8,128)(2,1)} %constant.20.clone.first_table) | copy-start | bytes 393220
  18.9 55.8 %collective-permute-start = (bf16[2,512,512]{2,1,0:T(8,128)(2,1)}, bf16[2,512,512]{2,1,0:T(8,128)(2,1)S(1)}, u32[]{:S(2)}, u32[]{:S(2)}) collective-permute-start(bf16[2,512,512]{2,1,0:T(8,128)(2,1)} %get-tuple-element.22), channel_id=1, source_target_pairs={{0,32},{32,64},{64,96},{96,0},{128,160},{160,192},{192,224},{224,1... | collective-permute-start | bytes 3145736 | tf_op jit(solution)/shard_map/ppermute | solution.py:337
  20.4 54.3 %collective-permute-start.1 = (bf16[2,512,512]{2,1,0:T(8,128)(2,1)}, bf16[2,512,512]{2,1,0:T(8,128)(2,1)S(1)}, u32[]{:S(2)}, u32[]{:S(2)}) collective-permute-start(bf16[2,512,512]{2,1,0:T(8,128)(2,1)} %get-tuple-element.23), channel_id=1, source_target_pairs={{0,64},{32,96},{64,0},{96,32},{128,192},{160,224},{192,128},{224,1... | collective-permute-start | bytes 3145736 | tf_op jit(solution)/shard_map/ppermute | solution.py:337
  23.2 51.6 %collective-permute-start.2 = (bf16[2,512,512]{2,1,0:T(8,128)(2,1)}, bf16[2,512,512]{2,1,0:T(8,128)(2,1)}, u32[]{:S(2)}, u32[]{:S(2)}) collective-permute-start(bf16[2,512,512]{2,1,0:T(8,128)(2,1)} %get-tuple-element.24), channel_id=1, source_target_pairs={{0,96},{32,0},{64,32},{96,64},{128,224},{160,128},{192,160},{224,1... | collective-permute-start | bytes 3145736 | tf_op jit(solution)/shard_map/ppermute | solution.py:337
  43.3 31.0 %copy-start = (bf16[512,512]{1,0:T(8,128)(2,1)S(1)}, bf16[512,512]{1,0:T(8,128)(2,1)}, u32[]{:S(2)}) copy-start(bf16[512,512]{1,0:T(8,128)(2,1)} %value_ref.1) | copy-start | bytes 1572868
  43.3 31.0 %copy-start.1 = (bf16[512,512]{1,0:T(8,128)(2,1)S(1)}, bf16[512,512]{1,0:T(8,128)(2,1)}, u32[]{:S(2)}) copy-start(bf16[512,512]{1,0:T(8,128)(2,1)} %gate_ref.1) | copy-start | bytes 1572868
  43.3 31.0 %copy-start.2 = (bf16[512,512]{1,0:T(8,128)(2,1)S(1)}, bf16[512,512]{1,0:T(8,128)(2,1)}, u32[]{:S(2)}) copy-start(bf16[512,512]{1,0:T(8,128)(2,1)} %gate_out_ref.1) | copy-start | bytes 1572868
  43.4 31.0 %copy-start.3 = (f32[512]{0:T(512)S(1)}, f32[512]{0:T(512)}, u32[]{:S(2)}) copy-start(f32[512]{0:T(512)} %param.13) | copy-start | bytes 6148
  74.7 10.5 %collective-permute-start.5 = (bf16[256,512]{1,0:T(8,128)(2,1)S(1)}, bf16[256,512]{1,0:T(8,128)(2,1)S(1)}, u32[]{:S(2)}, u32[]{:S(2)}) collective-permute-start(bf16[256,512]{1,0:T(8,128)(2,1)S(1)} %get-tuple-element.25.refs_0_), channel_id=1, source_target_pairs={{0,32},{32,64},{64,96},{96,0},{128,160},{160,192},{192,224},{224,1... | collective-permute-start | bytes 786440 | tf_op jit(solution)/shard_map/ppermute | solution.py:324
  76.3 9.3 %collective-permute-start.3 = (bf16[256,512]{1,0:T(8,128)(2,1)S(1)}, bf16[256,512]{1,0:T(8,128)(2,1)S(1)}, u32[]{:S(2)}, u32[]{:S(2)}) collective-permute-start(bf16[256,512]{1,0:T(8,128)(2,1)S(1)} %get-tuple-element.25.refs_0_), channel_id=1, source_target_pairs={{0,96},{32,0},{64,32},{96,64},{128,224},{160,128},{192,160},{224,1... | collective-permute-start | bytes 786440 | tf_op jit(solution)/shard_map/ppermute | solution.py:324
  78.1 12.5 %collective-permute-start.9 = (bf16[256,512]{1,0:T(8,128)(2,1)S(1)}, bf16[256,512]{1,0:T(8,128)(2,1)S(1)}, u32[]{:S(2)}, u32[]{:S(2)}) collective-permute-start(bf16[256,512]{1,0:T(8,128)(2,1)S(1)} %get-tuple-element.30.refs_0_), channel_id=1, source_target_pairs={{0,32},{32,64},{64,96},{96,0},{128,160},{160,192},{192,224},{224,1... | collective-permute-start | bytes 786440 | tf_op jit(solution)/shard_map/ppermute | solution.py:324
  78.3 12.9 %collective-permute-start.7 = (bf16[256,512]{1,0:T(8,128)(2,1)S(1)}, bf16[256,512]{1,0:T(8,128)(2,1)S(1)}, u32[]{:S(2)}, u32[]{:S(2)}) collective-permute-start(bf16[256,512]{1,0:T(8,128)(2,1)S(1)} %get-tuple-element.30.refs_0_), channel_id=1, source_target_pairs={{0,96},{32,0},{64,32},{96,64},{128,224},{160,128},{192,160},{224,1... | collective-permute-start | bytes 786440 | tf_op jit(solution)/shard_map/ppermute | solution.py:324
  85.3 8.7 %collective-permute-start.6 = (bf16[128,512]{1,0:T(8,128)(2,1)S(1)}, bf16[128,512]{1,0:T(8,128)(2,1)S(1)}, u32[]{:S(2)}, u32[]{:S(2)}) collective-permute-start(bf16[128,512]{1,0:T(8,128)(2,1)S(1)} %slice.17), channel_id=1, source_target_pairs={{0,32},{32,64},{64,96},{96,0},{128,160},{160,192},{192,224},{224,1... | collective-permute-start | bytes 393224 | tf_op jit(solution)/shard_map/ppermute | solution.py:324
  85.7 8.3 %collective-permute-start.4 = (bf16[128,512]{1,0:T(8,128)(2,1)S(1)}, bf16[128,512]{1,0:T(8,128)(2,1)S(1)}, u32[]{:S(2)}, u32[]{:S(2)}) collective-permute-start(bf16[128,512]{1,0:T(8,128)(2,1)S(1)} %slice.16), channel_id=1, source_target_pairs={{0,96},{32,0},{64,32},{96,64},{128,224},{160,128},{192,160},{224,1... | collective-permute-start | bytes 393224 | tf_op jit(solution)/shard_map/ppermute | solution.py:324
  90.6 6.3 %collective-permute-start.10 = (bf16[128,512]{1,0:T(8,128)(2,1)S(1)}, bf16[128,512]{1,0:T(8,128)(2,1)S(1)}, u32[]{:S(2)}, u32[]{:S(2)}) collective-permute-start(bf16[128,512]{1,0:T(8,128)(2,1)S(1)} %slice.19), channel_id=1, source_target_pairs={{0,32},{32,64},{64,96},{96,0},{128,160},{160,192},{192,224},{224,1... | collective-permute-start | bytes 393224 | tf_op jit(solution)/shard_map/ppermute | solution.py:324
  91.3 5.5 %collective-permute-start.8 = (bf16[128,512]{1,0:T(8,128)(2,1)S(1)}, bf16[128,512]{1,0:T(8,128)(2,1)S(1)}, u32[]{:S(2)}, u32[]{:S(2)}) collective-permute-start(bf16[128,512]{1,0:T(8,128)(2,1)S(1)} %slice.18), channel_id=1, source_target_pairs={{0,96},{32,0},{64,32},{96,64},{128,224},{160,128},{192,160},{224,1... | collective-permute-start | bytes 393224 | tf_op jit(solution)/shard_map/ppermute | solution.py:324
  94.7 7.6 %collective-permute-start.11 = (bf16[256,512]{1,0:T(8,128)(2,1)S(1)}, bf16[256,512]{1,0:T(8,128)(2,1)S(1)}, u32[]{:S(2)}, u32[]{:S(2)}) collective-permute-start(bf16[256,512]{1,0:T(8,128)(2,1)S(1)} %project.4), channel_id=1, source_target_pairs={{0,128},{32,160},{64,192},{96,224},{128,0},{160,32},{192,64},{224,... | collective-permute-start | bytes 786440 | tf_op jit(solution)/shard_map/ppermute | solution.py:349
  97.5 7.6 %collective-permute-start.12 = (bf16[256,512]{1,0:T(8,128)(2,1)S(1)}, bf16[256,512]{1,0:T(8,128)(2,1)S(1)}, u32[]{:S(2)}, u32[]{:S(2)}) collective-permute-start(bf16[256,512]{1,0:T(8,128)(2,1)S(1)} %project.5), channel_id=1, source_target_pairs={{0,128},{32,160},{64,192},{96,224},{128,0},{160,32},{192,64},{224,... | collective-permute-start | bytes 786440 | tf_op jit(solution)/shard_map/ppermute | solution.py:349

commit v6 on v5

--- a/solution.py
+++ b/solution.py
@@ -131,9 +131,7 @@
     wide[...] = in_ref[...].astype(jnp.float32)
     cos, sin = turns[0], turns[1]
 
-    @pl.loop(0, chans // BATCH, unroll=True)
-    def _(step):
-        first = step * BATCH
+    for first in range(0, chans, BATCH):
         signals = [
             wide[pl.ds(which * chans + first + k, EDGE, stride=2 * chans), :].astype(jnp.bfloat16)
             for k in range(BATCH)

time: 107 us -> 107 us (level)
  no operation moved by 1% of the time
where the time goes in v6:
time: 107 us; the launch traced here: 106 us
  starting transfers between devices  33.5 us (31%)
  waiting for transfers between devices  27.6 us (26%)
  blocking collectives  22.5 us (21%)
  Pallas kernels  21.1 us (20%)
    all_to_all x1, blocking collectives, per_device(): lax.all_to_all(conv, 'ctx', split_axis=0, concat_axis=0, tiled=True)  22.5 us
    all_to_all x1, waiting for transfers between devices, per_device(): lax.all_to_all(packed, 'ctx', split_axis=0, concat_axis=0, tiled=True)  18.7 us
    ppermute x8, starting transfers between devices, send(): return lax.ppermute(rows, 'chan', along_x(shift))  13.3 us
    all_to_all x1, starting transfers between devices, per_device(): lax.all_to_all(packed, 'ctx', split_axis=0, concat_axis=0, tiled=True)  11.7 us
    pallas_call x1, Pallas kernels, convolve(): pl.pallas_call(functools.partial(conv_kernel, chans), in_specs=[whole] *...  8.43 us
    ppermute x3, starting transfers between devices, per_device(): lax.ppermute(piece, 'chan', along_x(i + 1))  5.73 us
    ppermute x8, waiting for transfers between devices, send(): return lax.ppermute(rows, 'chan', along_x(shift))  5.4 us
    pallas_call x1, Pallas kernels, deal(): pl.pallas_call(deal_kernel, in_specs=[pl.BlockSpec(memory_space=pltpu.SME...  4.45 us
  transfers between devices with their start and end apart: 14, of which 6 were waited for; matrix products, arithmetic and copies ran while one was open for 0% of the time, Pallas kernels for 17%

profile of v6, /device:TPU:16, one launch (start us, length us, event | category | flops | bytes accessed | tf_op | source)
XLA Modules:
  0.0 106.0 jit_solution(500601291522466566)
XLA Ops:
  0.0 2.7 %pack.1 = bf16[32,4,2,16,128]{4,3,2,1,0:T(8,128)(2,1)} custom-call(bf16[512,512]{1,0:T(8,128)(2,1)} %value_ref.1, bf16[512,512]{1,0:T(8,128)(2,1)} %gate_ref.1, bf16[512,512]{1,0:T(8,128)(2,1)} %filt_hbm.1), custom_call_target="tpu_custom_call" | custom-call | tf_op jit(solution)/shard_map/pack/pallas_call | solution.py:205
  2.7 11.7 %all-to-all-start = ((bf16[32,4,2,16,128]{4,3,2,1,0:T(8,128)(2,1)}), bf16[32,4,2,16,128]{4,3,2,1,0:T(8,128)(2,1)}, u32[]{:S(2)}, u32[]{:S(2)}) async-start(bf16[32,4,2,16,128]{4,3,2,1,0:T(8,128)(2,1)} %pack.1), calls=%async_computation | async-start | bytes 2097152 | tf_op jit(solution)/shard_map/all_to_all | solution.py:336
  14.3 0.1 pad_add_fusion.place
  14.4 0.0 copy-start.4
  14.4 0.0 copy-start.5
  14.4 0.0 copy-start.6
  14.4 4.5 %deal.1 = (bf16[2,512,512]{2,1,0:T(8,128)(2,1)}, bf16[2,512,512]{2,1,0:T(8,128)(2,1)}, bf16[2,512,512]{2,1,0:T(8,128)(2,1)}, bf16[2,512,512]{2,1,0:T(8,128)(2,1)S(1)}) custom-call(s32[2]{0:T(128)S(1)} %pad_add_fusion.place, bf16[512,4096]{1,0:T(8,128)(2,1)} %w_hbm.1), custom_call_target="tpu_custom_call" | custom-call | tf_op jit(solution)/shard_map/deal/pallas_call | solution.py:220
  18.9 1.6 %collective-permute-start = (bf16[2,512,512]{2,1,0:T(8,128)(2,1)}, bf16[2,512,512]{2,1,0:T(8,128)(2,1)S(1)}, u32[]{:S(2)}, u32[]{:S(2)}) collective-permute-start(bf16[2,512,512]{2,1,0:T(8,128)(2,1)} %get-tuple-element.22), channel_id=1, source_target_pairs={{0,32},{32,64},{64,96},{96,0},{128,160},{160,192},{192,224},{224,1... | collective-permute-start | bytes 3145736 | tf_op jit(solution)/shard_map/ppermute | solution.py:335
  20.4 2.7 %collective-permute-start.1 = (bf16[2,512,512]{2,1,0:T(8,128)(2,1)}, bf16[2,512,512]{2,1,0:T(8,128)(2,1)S(1)}, u32[]{:S(2)}, u32[]{:S(2)}) collective-permute-start(bf16[2,512,512]{2,1,0:T(8,128)(2,1)} %get-tuple-element.23), channel_id=1, source_target_pairs={{0,64},{32,96},{64,0},{96,32},{128,192},{160,224},{192,128},{224,1... | collective-permute-start | bytes 3145736 | tf_op jit(solution)/shard_map/ppermute | solution.py:335
  23.2 1.4 %collective-permute-start.2 = (bf16[2,512,512]{2,1,0:T(8,128)(2,1)}, bf16[2,512,512]{2,1,0:T(8,128)(2,1)}, u32[]{:S(2)}, u32[]{:S(2)}) collective-permute-start(bf16[2,512,512]{2,1,0:T(8,128)(2,1)} %get-tuple-element.24), channel_id=1, source_target_pairs={{0,96},{32,0},{64,32},{96,64},{128,224},{160,128},{192,160},{224,1... | collective-permute-start | bytes 3145736 | tf_op jit(solution)/shard_map/ppermute | solution.py:335
  24.6 18.7 %all-to-all-done = bf16[32,4,2,16,128]{4,3,2,1,0:T(8,128)(2,1)} async-done(((bf16[32,4,2,16,128]{4,3,2,1,0:T(8,128)(2,1)}), bf16[32,4,2,16,128]{4,3,2,1,0:T(8,128)(2,1)}, u32[]{:S(2)}, u32[]{:S(2)}) %all-to-all-start) | async-done | bytes 1048608 | tf_op jit(solution)/shard_map/all_to_all | solution.py:336
  43.3 0.0 copy-done.4
  43.3 0.0 copy-done.5
  43.3 0.0 copy-done.6
  43.3 0.0 copy-start
  43.3 0.0 copy-start.1
  43.3 0.0 copy-start.2
  43.4 0.0 copy-start.3
  43.4 8.4 %convolve.1 = bf16[2048,128]{1,0:T(8,128)(2,1)S(1)} custom-call(bf16[4096,128]{1,0:T(8,128)(2,1)} %bitcast.in_ref, bf16[256,256]{1,0:T(8,128)(2,1)S(1)} %copy-done.6, bf16[128,512]{1,0:T(8,128)(2,1)S(1)} %copy-done.5, f32[2,128,128]{2,1,0:T(8,128)S(1)} %copy-done.4), custom_call_target="tpu_custom_call" | custom-call | flops 6000000000 | bytes 2000000 | tf_op jit(solution)/shard_map/convolve/pallas_call | solution.py:235
  51.8 22.5 %all_to_all.10.conv_ref = bf16[32,4,16,128]{3,2,1,0:T(8,128)(2,1)S(1)} all-to-all(bf16[32,4,16,128]{3,2,1,0:T(8,128)(2,1)S(1)} %bitcast.5), channel_id=1, replica_groups=mesh['chan'=8,'ctx'=32] {'ctx'}, dimensions={0} | all-to-all | bytes 1048576 | tf_op jit(solution)/shard_map/all_to_all | solution.py:339
  74.3 0.0 copy-done
  74.3 0.0 copy-done.1
  74.3 0.0 copy-done.2
  74.3 0.0 copy-done.3
  74.3 0.4 mix.1
  74.7 0.0 collective-permute-done.refs_1_
  74.7 0.0 collective-permute-done.1.refs_2_
  74.7 0.0 collective-permute-done.2.refs_3_
  74.7 1.6 %collective-permute-start.5 = (bf16[256,512]{1,0:T(8,128)(2,1)S(1)}, bf16[256,512]{1,0:T(8,128)(2,1)S(1)}, u32[]{:S(2)}, u32[]{:S(2)}) collective-permute-start(bf16[256,512]{1,0:T(8,128)(2,1)S(1)} %get-tuple-element.25.refs_0_), channel_id=1, source_target_pairs={{0,32},{32,64},{64,96},{96,0},{128,160},{160,192},{192,224},{224,1... | collective-permute-start | bytes 786440 | tf_op jit(solution)/shard_map/ppermute | solution.py:322
  76.3 1.7 %collective-permute-start.3 = (bf16[256,512]{1,0:T(8,128)(2,1)S(1)}, bf16[256,512]{1,0:T(8,128)(2,1)S(1)}, u32[]{:S(2)}, u32[]{:S(2)}) collective-permute-start(bf16[256,512]{1,0:T(8,128)(2,1)S(1)} %get-tuple-element.25.refs_0_), channel_id=1, source_target_pairs={{0,96},{32,0},{64,32},{96,64},{128,224},{160,128},{192,160},{224,1... | collective-permute-start | bytes 786440 | tf_op jit(solution)/shard_map/ppermute | solution.py:322
  78.1 0.3 collective-permute-start.9
  78.3 3.0 %collective-permute-start.7 = (bf16[256,512]{1,0:T(8,128)(2,1)S(1)}, bf16[256,512]{1,0:T(8,128)(2,1)S(1)}, u32[]{:S(2)}, u32[]{:S(2)}) collective-permute-start(bf16[256,512]{1,0:T(8,128)(2,1)S(1)} %get-tuple-element.30.refs_0_), channel_id=1, source_target_pairs={{0,96},{32,0},{64,32},{96,64},{128,224},{160,128},{192,160},{224,1... | collective-permute-start | bytes 786440 | tf_op jit(solution)/shard_map/ppermute | solution.py:322
  81.3 4.0 %collective-permute-done.5.refs_4_ = bf16[256,512]{1,0:T(8,128)(2,1)S(1)} collective-permute-done((bf16[256,512]{1,0:T(8,128)(2,1)S(1)}, bf16[256,512]{1,0:T(8,128)(2,1)S(1)}, u32[]{:S(2)}, u32[]{:S(2)}) %collective-permute-start.5) | collective-permute-done | bytes 262176 | tf_op jit(solution)/shard_map/ppermute | solution.py:322
  85.3 0.4 collective-permute-start.6
  85.7 0.0 collective-permute-done.3.refs_1_
  85.7 3.0 %collective-permute-start.4 = (bf16[128,512]{1,0:T(8,128)(2,1)S(1)}, bf16[128,512]{1,0:T(8,128)(2,1)S(1)}, u32[]{:S(2)}, u32[]{:S(2)}) collective-permute-start(bf16[128,512]{1,0:T(8,128)(2,1)S(1)} %slice.16), channel_id=1, source_target_pairs={{0,96},{32,0},{64,32},{96,64},{128,224},{160,128},{192,160},{224,1... | collective-permute-start | bytes 393224 | tf_op jit(solution)/shard_map/ppermute | solution.py:322
  88.7 1.2 %stage.2.refs_5_ = bf16[4,512,512]{2,1,0:T(8,128)(2,1)S(1)} custom-call(bf16[2,512,512]{2,1,0:T(8,128)(2,1)S(1)} %get-tuple-element.31.refs_0_, bf16[2,512,512]{2,1,0:T(8,128)(2,1)S(1)} %collective-permute-done.refs_1_, bf16[2,512,512]{2,1,0:T(8,128)(2,1)S(1)} %collective-permute-done.1.refs_2_, bf16[2,512,512]{2,1,0:T(8,128)(2,1)} %collective-permute-done.2.refs_3_), custom_call_target="tpu_custom_call" | custom-call | bytes 8000000 | tf_op jit(solution)/shard_map/stage/pallas_call | solution.py:282
  89.9 0.6 collective-permute-done.9.refs_4_
  90.6 0.7 collective-permute-start.10
  91.3 0.0 collective-permute-done.7.refs_1_
  91.3 2.7 %collective-permute-start.8 = (bf16[128,512]{1,0:T(8,128)(2,1)S(1)}, bf16[128,512]{1,0:T(8,128)(2,1)S(1)}, u32[]{:S(2)}, u32[]{:S(2)}) collective-permute-start(bf16[128,512]{1,0:T(8,128)(2,1)S(1)} %slice.18), channel_id=1, source_target_pairs={{0,96},{32,0},{64,32},{96,64},{128,224},{160,128},{192,160},{224,1... | collective-permute-start | bytes 393224 | tf_op jit(solution)/shard_map/ppermute | solution.py:322
  94.0 0.0 collective-permute-done.6.refs_3_
  94.0 0.0 collective-permute-done.4.refs_2_
  94.0 0.7 project.4
  94.7 1.4 %collective-permute-start.11 = (bf16[256,512]{1,0:T(8,128)(2,1)S(1)}, bf16[256,512]{1,0:T(8,128)(2,1)S(1)}, u32[]{:S(2)}, u32[]{:S(2)}) collective-permute-start(bf16[256,512]{1,0:T(8,128)(2,1)S(1)} %project.4), channel_id=1, source_target_pairs={{0,128},{32,160},{64,192},{96,224},{128,0},{160,32},{192,64},{224,... | collective-permute-start | bytes 786440 | tf_op jit(solution)/shard_map/ppermute | solution.py:347
  96.0 0.8 collective-permute-done.10.refs_3_
  96.8 0.0 collective-permute-done.8.refs_2_
  96.8 0.7 project.5
  97.5 1.4 %collective-permute-start.12 = (bf16[256,512]{1,0:T(8,128)(2,1)S(1)}, bf16[256,512]{1,0:T(8,128)(2,1)S(1)}, u32[]{:S(2)}, u32[]{:S(2)}) collective-permute-start(bf16[256,512]{1,0:T(8,128)(2,1)S(1)} %project.5), channel_id=1, source_target_pairs={{0,128},{32,160},{64,192},{96,224},{128,0},{160,32},{192,64},{224,... | collective-permute-start | bytes 786440 | tf_op jit(solution)/shard_map/ppermute | solution.py:347
  98.9 1.2 %stage.3.refs_5_ = bf16[4,512,512]{2,1,0:T(8,128)(2,1)S(1)} custom-call(bf16[2,512,512]{2,1,0:T(8,128)(2,1)S(1)} %get-tuple-element.31.refs_0_, bf16[2,512,512]{2,1,0:T(8,128)(2,1)S(1)} %collective-permute-done.refs_1_, bf16[2,512,512]{2,1,0:T(8,128)(2,1)S(1)} %collective-permute-done.1.refs_2_, bf16[2,512,512]{2,1,0:T(8,128)(2,1)} %collective-permute-done.2.refs_3_), custom_call_target="tpu_custom_call" | custom-call | bytes 8000000 | tf_op jit(solution)/shard_map/stage/pallas_call | solution.py:282
  100.1 0.7 project.7
  100.8 0.7 project.6
  101.5 0.8 collective-permute-done.11
  102.3 0.1 add_convert_fusion.1
  102.4 2.7 %collective-permute-done.12 = bf16[256,512]{1,0:T(8,128)(2,1)S(1)} collective-permute-done((bf16[256,512]{1,0:T(8,128)(2,1)S(1)}, bf16[256,512]{1,0:T(8,128)(2,1)S(1)}, u32[]{:S(2)}, u32[]{:S(2)}) %collective-permute-start.12) | collective-permute-done | bytes 262176 | tf_op jit(solution)/shard_map/ppermute | solution.py:347
  105.1 0.1 add_convert_fusion
  105.2 0.8 pad_maximum_fusion
  (4 shorter events, 0.0 us)
Async XLA Ops:
  2.7 40.6 %all-to-all-start = ((bf16[32,4,2,16,128]{4,3,2,1,0:T(8,128)(2,1)}), bf16[32,4,2,16,128]{4,3,2,1,0:T(8,128)(2,1)}, u32[]{:S(2)}, u32[]{:S(2)}) async-start(bf16[32,4,2,16,128]{4,3,2,1,0:T(8,128)(2,1)} %pack.1), calls=%async_computation | async-start | bytes 2097152 | tf_op jit(solution)/shard_map/all_to_all | solution.py:336
  14.4 28.9 %copy-start.4 = (f32[2,128,128]{2,1,0:T(8,128)S(1)}, f32[2,128,128]{2,1,0:T(8,128)}, u32[]{:S(2)}) copy-start(f32[2,128,128]{2,1,0:T(8,128)} %constant.22.clone.turns) | copy-start | bytes 393220
  14.4 28.9 %copy-start.5 = (bf16[128,512]{1,0:T(8,128)(2,1)S(1)}, bf16[128,512]{1,0:T(8,128)(2,1)}, u32[]{:S(2)}) copy-start(bf16[128,512]{1,0:T(8,128)(2,1)} %constant.21.clone.base) | copy-start | bytes 393220
  14.4 28.9 %copy-start.6 = (bf16[256,256]{1,0:T(8,128)(2,1)S(1)}, bf16[256,256]{1,0:T(8,128)(2,1)}, u32[]{:S(2)}) copy-start(bf16[256,256]{1,0:T(8,128)(2,1)} %constant.20.clone.first_table) | copy-start | bytes 393220
  18.9 55.8 %collective-permute-start = (bf16[2,512,512]{2,1,0:T(8,128)(2,1)}, bf16[2,512,512]{2,1,0:T(8,128)(2,1)S(1)}, u32[]{:S(2)}, u32[]{:S(2)}) collective-permute-start(bf16[2,512,512]{2,1,0:T(8,128)(2,1)} %get-tuple-element.22), channel_id=1, source_target_pairs={{0,32},{32,64},{64,96},{96,0},{128,160},{160,192},{192,224},{224,1... | collective-permute-start | bytes 3145736 | tf_op jit(solution)/shard_map/ppermute | solution.py:335
  20.4 54.3 %collective-permute-start.1 = (bf16[2,512,512]{2,1,0:T(8,128)(2,1)}, bf16[2,512,512]{2,1,0:T(8,128)(2,1)S(1)}, u32[]{:S(2)}, u32[]{:S(2)}) collective-permute-start(bf16[2,512,512]{2,1,0:T(8,128)(2,1)} %get-tuple-element.23), channel_id=1, source_target_pairs={{0,64},{32,96},{64,0},{96,32},{128,192},{160,224},{192,128},{224,1... | collective-permute-start | bytes 3145736 | tf_op jit(solution)/shard_map/ppermute | solution.py:335
  23.2 51.6 %collective-permute-start.2 = (bf16[2,512,512]{2,1,0:T(8,128)(2,1)}, bf16[2,512,512]{2,1,0:T(8,128)(2,1)}, u32[]{:S(2)}, u32[]{:S(2)}) collective-permute-start(bf16[2,512,512]{2,1,0:T(8,128)(2,1)} %get-tuple-element.24), channel_id=1, source_target_pairs={{0,96},{32,0},{64,32},{96,64},{128,224},{160,128},{192,160},{224,1... | collective-permute-start | bytes 3145736 | tf_op jit(solution)/shard_map/ppermute | solution.py:335
  43.3 31.0 %copy-start = (bf16[512,512]{1,0:T(8,128)(2,1)S(1)}, bf16[512,512]{1,0:T(8,128)(2,1)}, u32[]{:S(2)}) copy-start(bf16[512,512]{1,0:T(8,128)(2,1)} %value_ref.1) | copy-start | bytes 1572868
  43.3 31.0 %copy-start.1 = (bf16[512,512]{1,0:T(8,128)(2,1)S(1)}, bf16[512,512]{1,0:T(8,128)(2,1)}, u32[]{:S(2)}) copy-start(bf16[512,512]{1,0:T(8,128)(2,1)} %gate_ref.1) | copy-start | bytes 1572868
  43.3 31.0 %copy-start.2 = (bf16[512,512]{1,0:T(8,128)(2,1)S(1)}, bf16[512,512]{1,0:T(8,128)(2,1)}, u32[]{:S(2)}) copy-start(bf16[512,512]{1,0:T(8,128)(2,1)} %gate_out_ref.1) | copy-start | bytes 1572868
  43.4 31.0 %copy-start.3 = (f32[512]{0:T(512)S(1)}, f32[512]{0:T(512)}, u32[]{:S(2)}) copy-start(f32[512]{0:T(512)} %param.13) | copy-start | bytes 6148
  74.7 10.5 %collective-permute-start.5 = (bf16[256,512]{1,0:T(8,128)(2,1)S(1)}, bf16[256,512]{1,0:T(8,128)(2,1)S(1)}, u32[]{:S(2)}, u32[]{:S(2)}) collective-permute-start(bf16[256,512]{1,0:T(8,128)(2,1)S(1)} %get-tuple-element.25.refs_0_), channel_id=1, source_target_pairs={{0,32},{32,64},{64,96},{96,0},{128,160},{160,192},{192,224},{224,1... | collective-permute-start | bytes 786440 | tf_op jit(solution)/shard_map/ppermute | solution.py:322
  76.3 9.3 %collective-permute-start.3 = (bf16[256,512]{1,0:T(8,128)(2,1)S(1)}, bf16[256,512]{1,0:T(8,128)(2,1)S(1)}, u32[]{:S(2)}, u32[]{:S(2)}) collective-permute-start(bf16[256,512]{1,0:T(8,128)(2,1)S(1)} %get-tuple-element.25.refs_0_), channel_id=1, source_target_pairs={{0,96},{32,0},{64,32},{96,64},{128,224},{160,128},{192,160},{224,1... | collective-permute-start | bytes 786440 | tf_op jit(solution)/shard_map/ppermute | solution.py:322
  78.1 12.5 %collective-permute-start.9 = (bf16[256,512]{1,0:T(8,128)(2,1)S(1)}, bf16[256,512]{1,0:T(8,128)(2,1)S(1)}, u32[]{:S(2)}, u32[]{:S(2)}) collective-permute-start(bf16[256,512]{1,0:T(8,128)(2,1)S(1)} %get-tuple-element.30.refs_0_), channel_id=1, source_target_pairs={{0,32},{32,64},{64,96},{96,0},{128,160},{160,192},{192,224},{224,1... | collective-permute-start | bytes 786440 | tf_op jit(solution)/shard_map/ppermute | solution.py:322
  78.3 12.9 %collective-permute-start.7 = (bf16[256,512]{1,0:T(8,128)(2,1)S(1)}, bf16[256,512]{1,0:T(8,128)(2,1)S(1)}, u32[]{:S(2)}, u32[]{:S(2)}) collective-permute-start(bf16[256,512]{1,0:T(8,128)(2,1)S(1)} %get-tuple-element.30.refs_0_), channel_id=1, source_target_pairs={{0,96},{32,0},{64,32},{96,64},{128,224},{160,128},{192,160},{224,1... | collective-permute-start | bytes 786440 | tf_op jit(solution)/shard_map/ppermute | solution.py:322
  85.3 8.7 %collective-permute-start.6 = (bf16[128,512]{1,0:T(8,128)(2,1)S(1)}, bf16[128,512]{1,0:T(8,128)(2,1)S(1)}, u32[]{:S(2)}, u32[]{:S(2)}) collective-permute-start(bf16[128,512]{1,0:T(8,128)(2,1)S(1)} %slice.17), channel_id=1, source_target_pairs={{0,32},{32,64},{64,96},{96,0},{128,160},{160,192},{192,224},{224,1... | collective-permute-start | bytes 393224 | tf_op jit(solution)/shard_map/ppermute | solution.py:322
  85.7 8.3 %collective-permute-start.4 = (bf16[128,512]{1,0:T(8,128)(2,1)S(1)}, bf16[128,512]{1,0:T(8,128)(2,1)S(1)}, u32[]{:S(2)}, u32[]{:S(2)}) collective-permute-start(bf16[128,512]{1,0:T(8,128)(2,1)S(1)} %slice.16), channel_id=1, source_target_pairs={{0,96},{32,0},{64,32},{96,64},{128,224},{160,128},{192,160},{224,1... | collective-permute-start | bytes 393224 | tf_op jit(solution)/shard_map/ppermute | solution.py:322
  90.6 6.3 %collective-permute-start.10 = (bf16[128,512]{1,0:T(8,128)(2,1)S(1)}, bf16[128,512]{1,0:T(8,128)(2,1)S(1)}, u32[]{:S(2)}, u32[]{:S(2)}) collective-permute-start(bf16[128,512]{1,0:T(8,128)(2,1)S(1)} %slice.19), channel_id=1, source_target_pairs={{0,32},{32,64},{64,96},{96,0},{128,160},{160,192},{192,224},{224,1... | collective-permute-start | bytes 393224 | tf_op jit(solution)/shard_map/ppermute | solution.py:322
  91.3 5.5 %collective-permute-start.8 = (bf16[128,512]{1,0:T(8,128)(2,1)S(1)}, bf16[128,512]{1,0:T(8,128)(2,1)S(1)}, u32[]{:S(2)}, u32[]{:S(2)}) collective-permute-start(bf16[128,512]{1,0:T(8,128)(2,1)S(1)} %slice.18), channel_id=1, source_target_pairs={{0,96},{32,0},{64,32},{96,64},{128,224},{160,128},{192,160},{224,1... | collective-permute-start | bytes 393224 | tf_op jit(solution)/shard_map/ppermute | solution.py:322
  94.7 7.6 %collective-permute-start.11 = (bf16[256,512]{1,0:T(8,128)(2,1)S(1)}, bf16[256,512]{1,0:T(8,128)(2,1)S(1)}, u32[]{:S(2)}, u32[]{:S(2)}) collective-permute-start(bf16[256,512]{1,0:T(8,128)(2,1)S(1)} %project.4), channel_id=1, source_target_pairs={{0,128},{32,160},{64,192},{96,224},{128,0},{160,32},{192,64},{224,... | collective-permute-start | bytes 786440 | tf_op jit(solution)/shard_map/ppermute | solution.py:347
  97.5 7.6 %collective-permute-start.12 = (bf16[256,512]{1,0:T(8,128)(2,1)S(1)}, bf16[256,512]{1,0:T(8,128)(2,1)S(1)}, u32[]{:S(2)}, u32[]{:S(2)}) collective-permute-start(bf16[256,512]{1,0:T(8,128)(2,1)S(1)} %project.5), channel_id=1, source_target_pairs={{0,128},{32,160},{64,192},{96,224},{128,0},{160,32},{192,64},{224,... | collective-permute-start | bytes 786440 | tf_op jit(solution)/shard_map/ppermute | solution.py:347

commit v7 on v6

--- a/solution.py
+++ b/solution.py
@@ -56,16 +56,20 @@
             axis=1,
         )
         scale = jnp.bfloat16(1.0 / EDGE)
+        last[part * EDGE : (part + 1) * EDGE, :] = end * scale
         for place in ((0, 1), (2,))[part]:
             rows = slice(2 * place * EDGE, 2 * (place + 1) * EDGE)
             second[rows, :] = ahead
             third[rows, :] = back * scale
-            last[:, rows] = end * scale
+
+
+def halves(array):
+    high = array.astype(jnp.bfloat16)
+    return high, (array - high.astype(jnp.float32)).astype(jnp.bfloat16)
 
 
 def thirds(array, axis):
-    high = array.astype(jnp.bfloat16)
-    low = (array - high.astype(jnp.float32)).astype(jnp.bfloat16)
+    high, low = halves(array)
     return jnp.concatenate([high, low, high], axis=axis)
 
 
@@ -161,7 +165,9 @@
             cols.append(
                 jnp.concatenate([real * cos - imag * sin, imag * cos + real * sin], axis=0)
             )
-        conv = dot(last[...], thirds(jnp.concatenate(cols, axis=1), 0))
+        high, low = halves(jnp.concatenate(cols, axis=1))
+        both = dot(last[...], high)
+        conv = both[:EDGE] + both[EDGE:] + dot(last[:EDGE, :], low)
         for k in range(BATCH):
             back[pl.ds(first + k, EDGE, stride=chans), :] = conv[:, k * EDGE : (k + 1) * EDGE]
 
@@ -242,7 +248,7 @@
             pltpu.VMEM((rows, EDGE), jnp.float32),
             pltpu.VMEM((6 * EDGE, 2 * EDGE), jnp.bfloat16),
             pltpu.VMEM((6 * EDGE, 2 * EDGE), jnp.bfloat16),
-            pltpu.VMEM((EDGE, 6 * EDGE), jnp.bfloat16),
+            pltpu.VMEM((2 * EDGE, 2 * EDGE), jnp.bfloat16),
         ],
         compiler_params=pltpu.CompilerParams(vmem_limit_bytes=MEDIUM),
         cost_estimate=pl.CostEstimate(

time: 107 us -> 107 us (level)
  no operation moved by 1% of the time
where the time goes in v7:
time: 107 us; the launch traced here: 106 us
  starting transfers between devices  33.5 us (31%)
  waiting for transfers between devices  27.6 us (26%)
  blocking collectives  22.5 us (21%)
  Pallas kernels  21.1 us (20%)
    all_to_all x1, blocking collectives, per_device(): lax.all_to_all(conv, 'ctx', split_axis=0, concat_axis=0, tiled=True)  22.5 us
    all_to_all x1, waiting for transfers between devices, per_device(): lax.all_to_all(packed, 'ctx', split_axis=0, concat_axis=0, tiled=True)  18.7 us
    ppermute x8, starting transfers between devices, send(): return lax.ppermute(rows, 'chan', along_x(shift))  13.3 us
    all_to_all x1, starting transfers between devices, per_device(): lax.all_to_all(packed, 'ctx', split_axis=0, concat_axis=0, tiled=True)  11.7 us
    pallas_call x1, Pallas kernels, convolve(): pl.pallas_call(functools.partial(conv_kernel, chans), in_specs=[whole] *...  8.48 us
    ppermute x3, starting transfers between devices, per_device(): lax.ppermute(piece, 'chan', along_x(i + 1))  5.73 us
    ppermute x8, waiting for transfers between devices, send(): return lax.ppermute(rows, 'chan', along_x(shift))  5.4 us
    pallas_call x1, Pallas kernels, deal(): pl.pallas_call(deal_kernel, in_specs=[pl.BlockSpec(memory_space=pltpu.SME...  4.45 us
  transfers between devices with their start and end apart: 14, of which 6 were waited for; matrix products, arithmetic and copies ran while one was open for 0% of the time, Pallas kernels for 17%

profile of v7, /device:TPU:16, one launch (start us, length us, event | category | flops | bytes accessed | tf_op | source)
XLA Modules:
  0.0 106.1 jit_solution(18317365176055215854)
XLA Ops:
  0.0 2.7 %pack.1 = bf16[32,4,2,16,128]{4,3,2,1,0:T(8,128)(2,1)} custom-call(bf16[512,512]{1,0:T(8,128)(2,1)} %value_ref.1, bf16[512,512]{1,0:T(8,128)(2,1)} %gate_ref.1, bf16[512,512]{1,0:T(8,128)(2,1)} %filt_hbm.1), custom_call_target="tpu_custom_call" | custom-call | tf_op jit(solution)/shard_map/pack/pallas_call | solution.py:211
  2.7 11.7 %all-to-all-start = ((bf16[32,4,2,16,128]{4,3,2,1,0:T(8,128)(2,1)}), bf16[32,4,2,16,128]{4,3,2,1,0:T(8,128)(2,1)}, u32[]{:S(2)}, u32[]{:S(2)}) async-start(bf16[32,4,2,16,128]{4,3,2,1,0:T(8,128)(2,1)} %pack.1), calls=%async_computation | async-start | bytes 2097152 | tf_op jit(solution)/shard_map/all_to_all | solution.py:342
  14.3 0.1 pad_add_fusion.place
  14.4 0.0 copy-start.4
  14.4 0.0 copy-start.5
  14.4 0.0 copy-start.6
  14.4 4.5 %deal.1 = (bf16[2,512,512]{2,1,0:T(8,128)(2,1)}, bf16[2,512,512]{2,1,0:T(8,128)(2,1)}, bf16[2,512,512]{2,1,0:T(8,128)(2,1)}, bf16[2,512,512]{2,1,0:T(8,128)(2,1)S(1)}) custom-call(s32[2]{0:T(128)S(1)} %pad_add_fusion.place, bf16[512,4096]{1,0:T(8,128)(2,1)} %w_hbm.1), custom_call_target="tpu_custom_call" | custom-call | tf_op jit(solution)/shard_map/deal/pallas_call | solution.py:226
  18.9 1.6 %collective-permute-start = (bf16[2,512,512]{2,1,0:T(8,128)(2,1)}, bf16[2,512,512]{2,1,0:T(8,128)(2,1)S(1)}, u32[]{:S(2)}, u32[]{:S(2)}) collective-permute-start(bf16[2,512,512]{2,1,0:T(8,128)(2,1)} %get-tuple-element.22), channel_id=1, source_target_pairs={{0,32},{32,64},{64,96},{96,0},{128,160},{160,192},{192,224},{224,1... | collective-permute-start | bytes 3145736 | tf_op jit(solution)/shard_map/ppermute | solution.py:341
  20.4 2.7 %collective-permute-start.1 = (bf16[2,512,512]{2,1,0:T(8,128)(2,1)}, bf16[2,512,512]{2,1,0:T(8,128)(2,1)S(1)}, u32[]{:S(2)}, u32[]{:S(2)}) collective-permute-start(bf16[2,512,512]{2,1,0:T(8,128)(2,1)} %get-tuple-element.23), channel_id=1, source_target_pairs={{0,64},{32,96},{64,0},{96,32},{128,192},{160,224},{192,128},{224,1... | collective-permute-start | bytes 3145736 | tf_op jit(solution)/shard_map/ppermute | solution.py:341
  23.2 1.4 %collective-permute-start.2 = (bf16[2,512,512]{2,1,0:T(8,128)(2,1)}, bf16[2,512,512]{2,1,0:T(8,128)(2,1)}, u32[]{:S(2)}, u32[]{:S(2)}) collective-permute-start(bf16[2,512,512]{2,1,0:T(8,128)(2,1)} %get-tuple-element.24), channel_id=1, source_target_pairs={{0,96},{32,0},{64,32},{96,64},{128,224},{160,128},{192,160},{224,1... | collective-permute-start | bytes 3145736 | tf_op jit(solution)/shard_map/ppermute | solution.py:341
  24.6 18.7 %all-to-all-done = bf16[32,4,2,16,128]{4,3,2,1,0:T(8,128)(2,1)} async-done(((bf16[32,4,2,16,128]{4,3,2,1,0:T(8,128)(2,1)}), bf16[32,4,2,16,128]{4,3,2,1,0:T(8,128)(2,1)}, u32[]{:S(2)}, u32[]{:S(2)}) %all-to-all-start) | async-done | bytes 1048608 | tf_op jit(solution)/shard_map/all_to_all | solution.py:342
  43.3 0.0 copy-done.4
  43.3 0.0 copy-done.5
  43.3 0.0 copy-done.6
  43.3 0.0 copy-start
  43.3 0.0 copy-start.1
  43.3 0.0 copy-start.2
  43.4 0.0 copy-start.3
  43.4 8.5 %convolve.1 = bf16[2048,128]{1,0:T(8,128)(2,1)S(1)} custom-call(bf16[4096,128]{1,0:T(8,128)(2,1)} %bitcast.in_ref, bf16[256,256]{1,0:T(8,128)(2,1)S(1)} %copy-done.6, bf16[128,512]{1,0:T(8,128)(2,1)S(1)} %copy-done.5, f32[2,128,128]{2,1,0:T(8,128)S(1)} %copy-done.4), custom_call_target="tpu_custom_call" | custom-call | flops 6000000000 | bytes 2000000 | tf_op jit(solution)/shard_map/convolve/pallas_call | solution.py:241
  51.9 22.5 %all_to_all.10.conv_ref = bf16[32,4,16,128]{3,2,1,0:T(8,128)(2,1)S(1)} all-to-all(bf16[32,4,16,128]{3,2,1,0:T(8,128)(2,1)S(1)} %bitcast.5), channel_id=1, replica_groups=mesh['chan'=8,'ctx'=32] {'ctx'}, dimensions={0} | all-to-all | bytes 1048576 | tf_op jit(solution)/shard_map/all_to_all | solution.py:345
  74.4 0.0 copy-done
  74.4 0.0 copy-done.1
  74.4 0.0 copy-done.2
  74.4 0.0 copy-done.3
  74.4 0.4 mix.1
  74.8 0.0 collective-permute-done.refs_1_
  74.8 0.0 collective-permute-done.1.refs_2_
  74.8 0.0 collective-permute-done.2.refs_3_
  74.8 1.6 %collective-permute-start.5 = (bf16[256,512]{1,0:T(8,128)(2,1)S(1)}, bf16[256,512]{1,0:T(8,128)(2,1)S(1)}, u32[]{:S(2)}, u32[]{:S(2)}) collective-permute-start(bf16[256,512]{1,0:T(8,128)(2,1)S(1)} %get-tuple-element.25.refs_0_), channel_id=1, source_target_pairs={{0,32},{32,64},{64,96},{96,0},{128,160},{160,192},{192,224},{224,1... | collective-permute-start | bytes 786440 | tf_op jit(solution)/shard_map/ppermute | solution.py:328
  76.4 1.7 %collective-permute-start.3 = (bf16[256,512]{1,0:T(8,128)(2,1)S(1)}, bf16[256,512]{1,0:T(8,128)(2,1)S(1)}, u32[]{:S(2)}, u32[]{:S(2)}) collective-permute-start(bf16[256,512]{1,0:T(8,128)(2,1)S(1)} %get-tuple-element.25.refs_0_), channel_id=1, source_target_pairs={{0,96},{32,0},{64,32},{96,64},{128,224},{160,128},{192,160},{224,1... | collective-permute-start | bytes 786440 | tf_op jit(solution)/shard_map/ppermute | solution.py:328
  78.1 0.3 collective-permute-start.9
  78.4 3.0 %collective-permute-start.7 = (bf16[256,512]{1,0:T(8,128)(2,1)S(1)}, bf16[256,512]{1,0:T(8,128)(2,1)S(1)}, u32[]{:S(2)}, u32[]{:S(2)}) collective-permute-start(bf16[256,512]{1,0:T(8,128)(2,1)S(1)} %get-tuple-element.30.refs_0_), channel_id=1, source_target_pairs={{0,96},{32,0},{64,32},{96,64},{128,224},{160,128},{192,160},{224,1... | collective-permute-start | bytes 786440 | tf_op jit(solution)/shard_map/ppermute | solution.py:328
  81.4 4.0 %collective-permute-done.5.refs_4_ = bf16[256,512]{1,0:T(8,128)(2,1)S(1)} collective-permute-done((bf16[256,512]{1,0:T(8,128)(2,1)S(1)}, bf16[256,512]{1,0:T(8,128)(2,1)S(1)}, u32[]{:S(2)}, u32[]{:S(2)}) %collective-permute-start.5) | collective-permute-done | bytes 262176 | tf_op jit(solution)/shard_map/ppermute | solution.py:328
  85.4 0.4 collective-permute-start.6
  85.7 0.0 collective-permute-done.3.refs_1_
  85.7 3.0 %collective-permute-start.4 = (bf16[128,512]{1,0:T(8,128)(2,1)S(1)}, bf16[128,512]{1,0:T(8,128)(2,1)S(1)}, u32[]{:S(2)}, u32[]{:S(2)}) collective-permute-start(bf16[128,512]{1,0:T(8,128)(2,1)S(1)} %slice.16), channel_id=1, source_target_pairs={{0,96},{32,0},{64,32},{96,64},{128,224},{160,128},{192,160},{224,1... | collective-permute-start | bytes 393224 | tf_op jit(solution)/shard_map/ppermute | solution.py:328
  88.8 1.2 %stage.2.refs_5_ = bf16[4,512,512]{2,1,0:T(8,128)(2,1)S(1)} custom-call(bf16[2,512,512]{2,1,0:T(8,128)(2,1)S(1)} %get-tuple-element.31.refs_0_, bf16[2,512,512]{2,1,0:T(8,128)(2,1)S(1)} %collective-permute-done.refs_1_, bf16[2,512,512]{2,1,0:T(8,128)(2,1)S(1)} %collective-permute-done.1.refs_2_, bf16[2,512,512]{2,1,0:T(8,128)(2,1)} %collective-permute-done.2.refs_3_), custom_call_target="tpu_custom_call" | custom-call | bytes 8000000 | tf_op jit(solution)/shard_map/stage/pallas_call | solution.py:288
  90.0 0.6 collective-permute-done.9.refs_4_
  90.6 0.7 collective-permute-start.10
  91.3 0.0 collective-permute-done.7.refs_1_
  91.3 2.7 %collective-permute-start.8 = (bf16[128,512]{1,0:T(8,128)(2,1)S(1)}, bf16[128,512]{1,0:T(8,128)(2,1)S(1)}, u32[]{:S(2)}, u32[]{:S(2)}) collective-permute-start(bf16[128,512]{1,0:T(8,128)(2,1)S(1)} %slice.18), channel_id=1, source_target_pairs={{0,96},{32,0},{64,32},{96,64},{128,224},{160,128},{192,160},{224,1... | collective-permute-start | bytes 393224 | tf_op jit(solution)/shard_map/ppermute | solution.py:328
  94.0 0.0 collective-permute-done.6.refs_3_
  94.0 0.0 collective-permute-done.4.refs_2_
  94.0 0.7 project.4
  94.7 1.4 %collective-permute-start.11 = (bf16[256,512]{1,0:T(8,128)(2,1)S(1)}, bf16[256,512]{1,0:T(8,128)(2,1)S(1)}, u32[]{:S(2)}, u32[]{:S(2)}) collective-permute-start(bf16[256,512]{1,0:T(8,128)(2,1)S(1)} %project.4), channel_id=1, source_target_pairs={{0,128},{32,160},{64,192},{96,224},{128,0},{160,32},{192,64},{224,... | collective-permute-start | bytes 786440 | tf_op jit(solution)/shard_map/ppermute | solution.py:353
  96.1 0.8 collective-permute-done.10.refs_3_
  96.9 0.0 collective-permute-done.8.refs_2_
  96.9 0.7 project.5
  97.6 1.4 %collective-permute-start.12 = (bf16[256,512]{1,0:T(8,128)(2,1)S(1)}, bf16[256,512]{1,0:T(8,128)(2,1)S(1)}, u32[]{:S(2)}, u32[]{:S(2)}) collective-permute-start(bf16[256,512]{1,0:T(8,128)(2,1)S(1)} %project.5), channel_id=1, source_target_pairs={{0,128},{32,160},{64,192},{96,224},{128,0},{160,32},{192,64},{224,... | collective-permute-start | bytes 786440 | tf_op jit(solution)/shard_map/ppermute | solution.py:353
  99.0 1.2 %stage.3.refs_5_ = bf16[4,512,512]{2,1,0:T(8,128)(2,1)S(1)} custom-call(bf16[2,512,512]{2,1,0:T(8,128)(2,1)S(1)} %get-tuple-element.31.refs_0_, bf16[2,512,512]{2,1,0:T(8,128)(2,1)S(1)} %collective-permute-done.refs_1_, bf16[2,512,512]{2,1,0:T(8,128)(2,1)S(1)} %collective-permute-done.1.refs_2_, bf16[2,512,512]{2,1,0:T(8,128)(2,1)} %collective-permute-done.2.refs_3_), custom_call_target="tpu_custom_call" | custom-call | bytes 8000000 | tf_op jit(solution)/shard_map/stage/pallas_call | solution.py:288
  100.1 0.7 project.7
  100.8 0.7 project.6
  101.6 0.8 collective-permute-done.11
  102.3 0.1 add_convert_fusion.1
  102.4 2.7 %collective-permute-done.12 = bf16[256,512]{1,0:T(8,128)(2,1)S(1)} collective-permute-done((bf16[256,512]{1,0:T(8,128)(2,1)S(1)}, bf16[256,512]{1,0:T(8,128)(2,1)S(1)}, u32[]{:S(2)}, u32[]{:S(2)}) %collective-permute-start.12) | collective-permute-done | bytes 262176 | tf_op jit(solution)/shard_map/ppermute | solution.py:353
  105.2 0.1 add_convert_fusion
  105.2 0.8 pad_maximum_fusion
  (4 shorter events, 0.0 us)
Async XLA Ops:
  2.7 40.6 %all-to-all-start = ((bf16[32,4,2,16,128]{4,3,2,1,0:T(8,128)(2,1)}), bf16[32,4,2,16,128]{4,3,2,1,0:T(8,128)(2,1)}, u32[]{:S(2)}, u32[]{:S(2)}) async-start(bf16[32,4,2,16,128]{4,3,2,1,0:T(8,128)(2,1)} %pack.1), calls=%async_computation | async-start | bytes 2097152 | tf_op jit(solution)/shard_map/all_to_all | solution.py:342
  14.4 28.9 %copy-start.4 = (f32[2,128,128]{2,1,0:T(8,128)S(1)}, f32[2,128,128]{2,1,0:T(8,128)}, u32[]{:S(2)}) copy-start(f32[2,128,128]{2,1,0:T(8,128)} %constant.22.clone.turns) | copy-start | bytes 393220
  14.4 28.9 %copy-start.5 = (bf16[128,512]{1,0:T(8,128)(2,1)S(1)}, bf16[128,512]{1,0:T(8,128)(2,1)}, u32[]{:S(2)}) copy-start(bf16[128,512]{1,0:T(8,128)(2,1)} %constant.21.clone.base) | copy-start | bytes 393220
  14.4 28.9 %copy-start.6 = (bf16[256,256]{1,0:T(8,128)(2,1)S(1)}, bf16[256,256]{1,0:T(8,128)(2,1)}, u32[]{:S(2)}) copy-start(bf16[256,256]{1,0:T(8,128)(2,1)} %constant.20.clone.first_table) | copy-start | bytes 393220
  18.9 55.9 %collective-permute-start = (bf16[2,512,512]{2,1,0:T(8,128)(2,1)}, bf16[2,512,512]{2,1,0:T(8,128)(2,1)S(1)}, u32[]{:S(2)}, u32[]{:S(2)}) collective-permute-start(bf16[2,512,512]{2,1,0:T(8,128)(2,1)} %get-tuple-element.22), channel_id=1, source_target_pairs={{0,32},{32,64},{64,96},{96,0},{128,160},{160,192},{192,224},{224,1... | collective-permute-start | bytes 3145736 | tf_op jit(solution)/shard_map/ppermute | solution.py:341
  20.4 54.3 %collective-permute-start.1 = (bf16[2,512,512]{2,1,0:T(8,128)(2,1)}, bf16[2,512,512]{2,1,0:T(8,128)(2,1)S(1)}, u32[]{:S(2)}, u32[]{:S(2)}) collective-permute-start(bf16[2,512,512]{2,1,0:T(8,128)(2,1)} %get-tuple-element.23), channel_id=1, source_target_pairs={{0,64},{32,96},{64,0},{96,32},{128,192},{160,224},{192,128},{224,1... | collective-permute-start | bytes 3145736 | tf_op jit(solution)/shard_map/ppermute | solution.py:341
  23.2 51.6 %collective-permute-start.2 = (bf16[2,512,512]{2,1,0:T(8,128)(2,1)}, bf16[2,512,512]{2,1,0:T(8,128)(2,1)}, u32[]{:S(2)}, u32[]{:S(2)}) collective-permute-start(bf16[2,512,512]{2,1,0:T(8,128)(2,1)} %get-tuple-element.24), channel_id=1, source_target_pairs={{0,96},{32,0},{64,32},{96,64},{128,224},{160,128},{192,160},{224,1... | collective-permute-start | bytes 3145736 | tf_op jit(solution)/shard_map/ppermute | solution.py:341
  43.3 31.0 %copy-start = (bf16[512,512]{1,0:T(8,128)(2,1)S(1)}, bf16[512,512]{1,0:T(8,128)(2,1)}, u32[]{:S(2)}) copy-start(bf16[512,512]{1,0:T(8,128)(2,1)} %value_ref.1) | copy-start | bytes 1572868
  43.3 31.0 %copy-start.1 = (bf16[512,512]{1,0:T(8,128)(2,1)S(1)}, bf16[512,512]{1,0:T(8,128)(2,1)}, u32[]{:S(2)}) copy-start(bf16[512,512]{1,0:T(8,128)(2,1)} %gate_ref.1) | copy-start | bytes 1572868
  43.3 31.0 %copy-start.2 = (bf16[512,512]{1,0:T(8,128)(2,1)S(1)}, bf16[512,512]{1,0:T(8,128)(2,1)}, u32[]{:S(2)}) copy-start(bf16[512,512]{1,0:T(8,128)(2,1)} %gate_out_ref.1) | copy-start | bytes 1572868
  43.4 31.0 %copy-start.3 = (f32[512]{0:T(512)S(1)}, f32[512]{0:T(512)}, u32[]{:S(2)}) copy-start(f32[512]{0:T(512)} %param.13) | copy-start | bytes 6148
  74.8 10.5 %collective-permute-start.5 = (bf16[256,512]{1,0:T(8,128)(2,1)S(1)}, bf16[256,512]{1,0:T(8,128)(2,1)S(1)}, u32[]{:S(2)}, u32[]{:S(2)}) collective-permute-start(bf16[256,512]{1,0:T(8,128)(2,1)S(1)} %get-tuple-element.25.refs_0_), channel_id=1, source_target_pairs={{0,32},{32,64},{64,96},{96,0},{128,160},{160,192},{192,224},{224,1... | collective-permute-start | bytes 786440 | tf_op jit(solution)/shard_map/ppermute | solution.py:328
  76.4 9.3 %collective-permute-start.3 = (bf16[256,512]{1,0:T(8,128)(2,1)S(1)}, bf16[256,512]{1,0:T(8,128)(2,1)S(1)}, u32[]{:S(2)}, u32[]{:S(2)}) collective-permute-start(bf16[256,512]{1,0:T(8,128)(2,1)S(1)} %get-tuple-element.25.refs_0_), channel_id=1, source_target_pairs={{0,96},{32,0},{64,32},{96,64},{128,224},{160,128},{192,160},{224,1... | collective-permute-start | bytes 786440 | tf_op jit(solution)/shard_map/ppermute | solution.py:328
  78.1 12.5 %collective-permute-start.9 = (bf16[256,512]{1,0:T(8,128)(2,1)S(1)}, bf16[256,512]{1,0:T(8,128)(2,1)S(1)}, u32[]{:S(2)}, u32[]{:S(2)}) collective-permute-start(bf16[256,512]{1,0:T(8,128)(2,1)S(1)} %get-tuple-element.30.refs_0_), channel_id=1, source_target_pairs={{0,32},{32,64},{64,96},{96,0},{128,160},{160,192},{192,224},{224,1... | collective-permute-start | bytes 786440 | tf_op jit(solution)/shard_map/ppermute | solution.py:328
  78.4 12.9 %collective-permute-start.7 = (bf16[256,512]{1,0:T(8,128)(2,1)S(1)}, bf16[256,512]{1,0:T(8,128)(2,1)S(1)}, u32[]{:S(2)}, u32[]{:S(2)}) collective-permute-start(bf16[256,512]{1,0:T(8,128)(2,1)S(1)} %get-tuple-element.30.refs_0_), channel_id=1, source_target_pairs={{0,96},{32,0},{64,32},{96,64},{128,224},{160,128},{192,160},{224,1... | collective-permute-start | bytes 786440 | tf_op jit(solution)/shard_map/ppermute | solution.py:328
  85.4 8.7 %collective-permute-start.6 = (bf16[128,512]{1,0:T(8,128)(2,1)S(1)}, bf16[128,512]{1,0:T(8,128)(2,1)S(1)}, u32[]{:S(2)}, u32[]{:S(2)}) collective-permute-start(bf16[128,512]{1,0:T(8,128)(2,1)S(1)} %slice.17), channel_id=1, source_target_pairs={{0,32},{32,64},{64,96},{96,0},{128,160},{160,192},{192,224},{224,1... | collective-permute-start | bytes 393224 | tf_op jit(solution)/shard_map/ppermute | solution.py:328
  85.7 8.3 %collective-permute-start.4 = (bf16[128,512]{1,0:T(8,128)(2,1)S(1)}, bf16[128,512]{1,0:T(8,128)(2,1)S(1)}, u32[]{:S(2)}, u32[]{:S(2)}) collective-permute-start(bf16[128,512]{1,0:T(8,128)(2,1)S(1)} %slice.16), channel_id=1, source_target_pairs={{0,96},{32,0},{64,32},{96,64},{128,224},{160,128},{192,160},{224,1... | collective-permute-start | bytes 393224 | tf_op jit(solution)/shard_map/ppermute | solution.py:328
  90.6 6.3 %collective-permute-start.10 = (bf16[128,512]{1,0:T(8,128)(2,1)S(1)}, bf16[128,512]{1,0:T(8,128)(2,1)S(1)}, u32[]{:S(2)}, u32[]{:S(2)}) collective-permute-start(bf16[128,512]{1,0:T(8,128)(2,1)S(1)} %slice.19), channel_id=1, source_target_pairs={{0,32},{32,64},{64,96},{96,0},{128,160},{160,192},{192,224},{224,1... | collective-permute-start | bytes 393224 | tf_op jit(solution)/shard_map/ppermute | solution.py:328
  91.3 5.5 %collective-permute-start.8 = (bf16[128,512]{1,0:T(8,128)(2,1)S(1)}, bf16[128,512]{1,0:T(8,128)(2,1)S(1)}, u32[]{:S(2)}, u32[]{:S(2)}) collective-permute-start(bf16[128,512]{1,0:T(8,128)(2,1)S(1)} %slice.18), channel_id=1, source_target_pairs={{0,96},{32,0},{64,32},{96,64},{128,224},{160,128},{192,160},{224,1... | collective-permute-start | bytes 393224 | tf_op jit(solution)/shard_map/ppermute | solution.py:328
  94.7 7.6 %collective-permute-start.11 = (bf16[256,512]{1,0:T(8,128)(2,1)S(1)}, bf16[256,512]{1,0:T(8,128)(2,1)S(1)}, u32[]{:S(2)}, u32[]{:S(2)}) collective-permute-start(bf16[256,512]{1,0:T(8,128)(2,1)S(1)} %project.4), channel_id=1, source_target_pairs={{0,128},{32,160},{64,192},{96,224},{128,0},{160,32},{192,64},{224,... | collective-permute-start | bytes 786440 | tf_op jit(solution)/shard_map/ppermute | solution.py:353
  97.6 7.6 %collective-permute-start.12 = (bf16[256,512]{1,0:T(8,128)(2,1)S(1)}, bf16[256,512]{1,0:T(8,128)(2,1)S(1)}, u32[]{:S(2)}, u32[]{:S(2)}) collective-permute-start(bf16[256,512]{1,0:T(8,128)(2,1)S(1)} %project.5), channel_id=1, source_target_pairs={{0,128},{32,160},{64,192},{96,224},{128,0},{160,32},{192,64},{224,... | collective-permute-start | bytes 786440 | tf_op jit(solution)/shard_map/ppermute | solution.py:353
